TPU v7x, 32 devices: a whole 2x2x4 slice. The times are simulated.
32 devices in a mesh: row: 4 (over y, x), col: 8 (over z, core).
Axes of the slice: x: 2, y: 2, z: 4, core: 2. Of those that a mesh axis runs over, the one named last changes fastest.
Arguments:
- window: float32 [12288, 12288], P('row', 'col'), may hold values from -6 to 6
- reflectors: float32 [2, 12288, 256], P(None, 'row', 'col'), may hold values from -0.0546875 to 0.0546875
- factors: float32 [2, 256, 256], replicated, may hold values from -0.375 to 0.375
Outputs:
- updated: float32 [12288, 12288], P('row', 'col')
All inputs are finite; a program needn't handle non-finite values.
Results may differ from a plain program's by a relative error of at most 0.0001.
Values sent between devices are 32-bit elements; how exact they have to be, the bound alone decides.
No kernel may reach another device: no remote copies, remote signals or barrier semaphores. Data moves between devices by JAX's collectives and lax.ppermute only.
A program may use at most 128 MiB of HBM per device.

v0:
```python
import jax
import jax.numpy as jnp
from jax import lax
from jax.sharding import PartitionSpec as P

highest = lax.Precision.HIGHEST


def product(factor_one, factor_two):
    return jnp.dot(factor_one, factor_two, precision=highest, preferred_element_type=jnp.float32)


def body(window, reflectors, factors):
    row_index = lax.axis_index("row")
    col_index = lax.axis_index("col")
    row_count = lax.axis_size("row")
    col_count = lax.axis_size("col")
    rows_loc = window.shape[0]
    cols_loc = window.shape[1]
    updated = window
    for panel in range(reflectors.shape[0]):
        sliver = reflectors[panel]
        factor = factors[panel]
        everything = lax.all_gather(sliver[None], ("row", "col"), axis=0, tiled=True)
        piece_cols = sliver.shape[1]
        vectors = everything.reshape(row_count, col_count, rows_loc, piece_cols)
        vectors = vectors.transpose(0, 2, 1, 3).reshape(
            row_count * rows_loc, col_count * piece_cols
        )
        local_vectors = lax.dynamic_slice_in_dim(vectors, row_index * rows_loc, rows_loc, 0)
        column_vectors = lax.dynamic_slice_in_dim(vectors, col_index * cols_loc, cols_loc, 0)
        partial_value = product(local_vectors.T, updated)
        early_image = product(updated, column_vectors)
        projected = lax.psum(partial_value, "row")
        updated = updated - product(local_vectors, product(factor.T, projected))
        crossed = product(projected, column_vectors)
        early_sum, crossed_sum = lax.psum((early_image, crossed), "col")
        image_sum = early_sum - product(local_vectors, product(factor.T, crossed_sum))
        updated = updated - product(product(image_sum, factor), column_vectors.T)
    return updated


def solution(mesh):
    placed = (P("row", "col"), P(None, "row", "col"), P())
    return jax.shard_map(
        body, mesh=mesh, in_specs=placed, out_specs=P("row", "col"), check_vma=False
    )
```

profile of v0, /device:TPU:8, one launch (start us, length us, event | category | flops | bytes accessed | tf_op | source)
XLA Modules:
  0.0 658.5 jit_solution(3726170050543968820)
XLA Ops:
  6.5 0.0 all-gather.3.cloned.1.call-start
  6.5 2.0 fusion.49
  8.6 0.0 all-gather.3.cloned.1.call-update
  8.6 0.0 all-reduce.7.cloned.1.call-start
  8.7 98.4 %all-gather.3.cloned.1.call-done = f32[32,3072,32]{1,2,0:T(8,128)} async-done(((f32[1,3072,32]{1,2,0:T(8,128)}), f32[32,3072,32]{1,2,0:T(8,128)}) %all-gather.3.cloned.1.call-update) | async-done | bytes 12582928 | tf_op jit(solution)/shard_map/all_gather | solution.py:24
  107.0 16.5 %copy.6 = f32[4,8,3072,32]{2,0,3,1:T(4,128)} copy(f32[4,8,3072,32]{2,3,1,0:T(8,128)} %bitcast.63) | data formatting | bytes 25165824 | tf_op jit(solution)/shard_map/reshape | solution.py:26
  123.6 20.4 %copy.10 = f32[32,8,4,3072]{3,1,2,0:T(8,128)} copy(f32[32,8,4,3072]{3,2,1,0:T(4,128)} %bitcast.60) | data formatting | bytes 25165824
  144.0 21.0 %fusion.8 = f32[256,1536]{1,0:T(8,128)} fusion(f32[3072,1536]{1,0:T(8,128)} %param.3, f32[12288,256]{0,1:T(8,128)} %bitcast.48, s32[]{:T(128)S(6)} %select_n.8), kind=kOutput, calls=%fused_computation.13 | convolution fusion | flops 14495514624 | bytes 23592964 | tf_op jit(solution)/shard_map/dot_general | solution.py:10
  165.0 0.0 all-reduce.7.cloned.1.call-update
  165.1 0.0 all-gather.5.cloned.1.call-start
  165.1 0.7 all-gather.5.cloned.1.call-update
  165.8 0.0 all-reduce.13.cloned.1.call-start
  165.8 20.7 %convolution_bitcast_fusion = f32[3072,256]{0,1:T(8,128)} fusion(f32[3072,1536]{1,0:T(8,128)} %param.3, f32[12288,256]{0,1:T(8,128)} %bitcast.49, s32[]{:T(128)S(6)} %select_n.9), kind=kOutput, calls=%fused_computation.4 | convolution fusion | flops 14495514624 | bytes 23592964 | tf_op jit(solution)/shard_map/dot_general | solution.py:10
  186.5 38.4 %all-reduce.7.cloned.1.call-done = f32[256,1536]{1,0:T(8,128)} async-done(((f32[256,1536]{1,0:T(8,128)}), f32[256,1536]{1,0:T(8,128)}) %all-reduce.7.cloned.1.call-update) | async-done | bytes 1572880 | tf_op jit(solution)/shard_map/psum | solution.py:34
  224.9 4.0 fusion.16
  229.0 0.0 all-reduce.13.cloned.1.call-update
  229.0 0.0 all-reduce.9.cloned.1.call-start
  229.1 94.8 %all-gather.5.cloned.1.call-done = f32[32,3072,32]{1,2,0:T(8,128)} async-done(((f32[1,3072,32]{1,2,0:T(8,128)}), f32[32,3072,32]{1,2,0:T(8,128)}) %all-gather.5.cloned.1.call-update) | async-done | bytes 12582928 | tf_op jit(solution)/shard_map/all_gather | solution.py:24
  323.9 16.6 %copy.8 = f32[4,8,3072,32]{2,0,3,1:T(4,128)} copy(f32[4,8,3072,32]{2,3,1,0:T(8,128)} %bitcast.62) | data formatting | bytes 25165824 | tf_op jit(solution)/shard_map/reshape | solution.py:26
  340.5 0.0 copy-start
  340.5 0.0 copy-start.2
  340.5 20.8 %copy.11 = f32[32,8,4,3072]{3,1,2,0:T(8,128)} copy(f32[32,8,4,3072]{3,2,1,0:T(4,128)} %bitcast.61) | data formatting | bytes 25165824
  361.3 0.0 copy-done
  361.3 0.0 copy-done.2
  361.3 2.9 fusion.29
  364.2 34.3 %fusion.6 = f32[3072,1536]{1,0:T(8,128)} fusion(f32[1536,256]{1,0:T(8,128)S(1)} %fusion.29, f32[12288,256]{0,1:T(8,128)} %bitcast.51, s32[]{:T(128)S(6)} %select_n.8), kind=kOutput, calls=%fused_computation.11 | convolution fusion | flops 14495514624 | bytes 23592964 | tf_op jit(solution)/shard_map/dot_general | solution.py:10
  398.5 8.8 %all-reduce.13.cloned.1.call-done = (f32[3072,256]{0,1:T(8,128)}, f32[256,256]{1,0:T(8,128)}) async-done(((f32[3072,256]{0,1:T(8,128)}, f32[256,256]{1,0:T(8,128)}), (f32[3072,256]{0,1:T(8,128)}, f32[256,256]{1,0:T(8,128)})) %all-reduce.13.cloned.1.call-update) | async-done | bytes 3407888 | tf_op jit(solution)/shard_map/psum | solution.py:37
  407.3 1.5 fusion.27
  408.8 6.1 convolution_subtract_fusion.1
  415.0 5.4 fusion.25
  420.3 25.3 %subtract_subtract_fusion.1 = f32[3072,1536]{1,0:T(8,128)} fusion(f32[3072,1536]{1,0:T(8,128)} %param.3, f32[3072,1536]{1,0:T(8,128)} %fusion.6, f32[3072,256]{1,0:T(8,128)S(1)} %fusion.25, f32[12288,256]{0,1:T(8,128)} %bitcast.53, s32[]{:T(128)S(6)} %select_n.9), kind=kOutput, calls=%fused_computation.1 | convolution fusion | flops 14504951808 | bytes 61341700 | tf_op jit(solution)/shard_map/dot_general | solution.py:10
  445.6 20.6 %fusion.3 = f32[256,1536]{1,0:T(8,128)} fusion(f32[3072,1536]{1,0:T(8,128)} %subtract_subtract_fusion.1, f32[12288,256]{0,1:T(8,128)} %bitcast.54, s32[]{:T(128)S(6)} %select_n.8), kind=kOutput, calls=%fused_computation.8 | convolution fusion | flops 14495514624 | bytes 23592964 | tf_op jit(solution)/shard_map/dot_general | solution.py:10
  466.2 0.0 all-reduce.9.cloned.1.call-update
  466.3 0.0 all-reduce.11.cloned.1.call-start
  466.3 19.7 %fusion.13 = f32[3072,256]{1,0:T(8,128)} fusion(f32[3072,1536]{1,0:T(8,128)} %subtract_subtract_fusion.1, f32[12288,256]{0,1:T(8,128)} %bitcast.55, s32[]{:T(128)S(6)} %select_n.9), kind=kOutput, calls=%fused_computation.18 | convolution fusion | flops 14495514624 | bytes 23592964 | tf_op jit(solution)/shard_map/dot_general | solution.py:10
  486.0 41.3 %all-reduce.9.cloned.1.call-done = f32[256,1536]{1,0:T(8,128)} async-done(((f32[256,1536]{1,0:T(8,128)}), f32[256,1536]{1,0:T(8,128)}) %all-reduce.9.cloned.1.call-update) | async-done | bytes 1572880 | tf_op jit(solution)/shard_map/psum | solution.py:34
  527.3 0.0 copy-start.1
  527.3 4.1 fusion.11
  531.5 0.0 all-reduce.11.cloned.1.call-update
  531.5 0.0 copy-done.1
  531.5 2.6 fusion.23
  534.1 34.3 %fusion.1 = f32[3072,1536]{1,0:T(8,128)} fusion(f32[1536,256]{1,0:T(8,128)S(1)} %fusion.23, f32[12288,256]{0,1:T(8,128)} %bitcast.57, s32[]{:T(128)S(6)} %select_n.8), kind=kOutput, calls=%fused_computation.6 | convolution fusion | flops 14495514624 | bytes 23592964 | tf_op jit(solution)/shard_map/dot_general | solution.py:10
  568.4 45.3 %all-reduce.11.cloned.1.call-done = (f32[3072,256]{1,0:T(8,128)}, f32[256,256]{1,0:T(8,128)}) async-done(((f32[3072,256]{1,0:T(8,128)}, f32[256,256]{1,0:T(8,128)}), (f32[3072,256]{1,0:T(8,128)}, f32[256,256]{1,0:T(8,128)})) %all-reduce.11.cloned.1.call-update) | async-done | bytes 3407888 | tf_op jit(solution)/shard_map/psum | solution.py:37
  613.7 1.5 fusion.21
  615.3 8.3 %convolution_subtract_fusion = f32[3072,256]{1,0:T(8,128)S(1)} fusion(f32[3072,256]{1,0:T(8,128)} %get-tuple-element.5, f32[256,256]{1,0:T(8,128)S(1)} %fusion.21, f32[12288,256]{0,1:T(8,128)} %bitcast.58, s32[]{:T(128)S(6)} %select_n.8), kind=kOutput, calls=%fused_computation.2 | convolution fusion | flops 2416705536 | bytes 9699332 | tf_op jit(solution)/shard_map/dot_general | solution.py:10
  623.5 2.6 fusion.19
  626.2 25.3 %subtract_subtract_fusion = f32[3072,1536]{1,0:T(8,128)} fusion(f32[3072,1536]{1,0:T(8,128)} %subtract_subtract_fusion.1, f32[3072,1536]{1,0:T(8,128)} %fusion.1, f32[3072,256]{1,0:T(8,128)S(1)} %fusion.19, f32[12288,256]{0,1:T(8,128)} %bitcast.59, s32[]{:T(128)S(6)} %select_n.9), kind=kOutput, calls=%fused_computation | convolution fusion | flops 14504951808 | bytes 61341700 | tf_op jit(solution)/shard_map/dot_general | solution.py:10
Async XLA Ops:
  6.5 100.5 %all-gather.3.cloned.1.call-start = ((), (), s32[]{:S(2)}) async-start(), calls=%async_computation | async-start | bytes 12976128 | tf_op jit(solution)/shard_map/all_gather | solution.py:24
  8.6 216.3 %all-reduce.7.cloned.1.call-start = ((), (), s32[]{:S(2)}) async-start(), calls=%async_computation.1 | async-start | bytes 3145728 | tf_op jit(solution)/shard_map/psum | solution.py:34
  165.1 158.8 %all-gather.5.cloned.1.call-start = ((), (), s32[]{:S(2)}) async-start(), calls=%async_computation.2 | async-start | bytes 12976128 | tf_op jit(solution)/shard_map/all_gather | solution.py:24
  165.8 241.5 %all-reduce.13.cloned.1.call-start = ((), (), s32[]{:S(2)}) async-start(), calls=%async_computation.5 | async-start | bytes 6815744 | tf_op jit(solution)/shard_map/psum | solution.py:37
  229.0 298.3 %all-reduce.9.cloned.1.call-start = ((), (), s32[]{:S(2)}) async-start(), calls=%async_computation.3 | async-start | bytes 3145728 | tf_op jit(solution)/shard_map/psum | solution.py:34
  340.5 20.8 %copy-start = (f32[256,1536]{1,0:T(8,128)S(1)}, f32[256,1536]{1,0:T(8,128)}, u32[]{:S(2)}) copy-start(f32[256,1536]{1,0:T(8,128)} %all-reduce.7.cloned.1.call-done) | copy-start | bytes 4718596
  340.5 20.8 %copy-start.2 = (f32[2,256,256]{2,1,0:T(8,128)S(1)}, f32[2,256,256]{2,1,0:T(8,128)}, u32[]{:S(2)}) copy-start(f32[2,256,256]{2,1,0:T(8,128)} %param.5) | copy-start | bytes 1572868
  466.3 147.5 %all-reduce.11.cloned.1.call-start = ((), (), s32[]{:S(2)}) async-start(), calls=%async_computation.4 | async-start | bytes 6815744 | tf_op jit(solution)/shard_map/psum | solution.py:37
  527.3 4.2 copy-start.1
Sparse Core Ops, SparseCore 0:
  10.4 96.6 all-gather.2
  165.2 59.7 all-reduce.6
  228.4 95.4 all-gather.4
  326.3 80.8 all-reduce.12
  466.4 60.9 all-reduce.8
  531.6 82.0 all-reduce.10
where the time goes:
time: 663 us; the launch traced here: 659 us
  waiting for transfers between devices  328 us (49%)
  matrix products  240 us (36%)
  local copies, waits for them, and re-layouts  76.4 us (12%)
  between operations  13.8 us (2%)
    dot_general x18, matrix products, product(): jnp.dot(factor_one, factor_two, precision=highest, preferred_element_type...  240 us
    all_gather x2, waiting for transfers between devices, body(): lax.all_gather(sliver[None], ('row', 'col'), axis=0, tiled=True)  193 us
    psum x2, waiting for transfers between devices, body(): projected = lax.psum(partial_value, 'row')  79.8 us
    psum x2, waiting for transfers between devices, body(): early_sum, crossed_sum = lax.psum((early_image, crossed), 'col')  54.1 us
    unnamed x8, local copies, waits for them, and re-layouts  41.2 us
    reshape x2, local copies, waits for them, and re-layouts, body(): vectors = everything.reshape(row_count, col_count, rows_loc, piece_cols)  33.1 us
  transfers between devices with their start and end apart: 6, of which 6 were waited for; matrix products, arithmetic and copies ran while one was open for 24% of the time, Pallas kernels for 0%

commit v1 on v0

v1 whole, which is shorter than its diff:
```python
import functools

import jax
import jax.numpy as jnp
from jax import lax
from jax.experimental import pallas as pl
from jax.experimental.pallas import tpu as pltpu
from jax.sharding import PartitionSpec as P

f32 = jnp.float32
bf16 = jnp.bfloat16
VMEM_BYTES = 50 * 1024 * 1024


def halves(value):
    high = value.astype(bf16)
    return high, (value - high.astype(f32)).astype(bf16)


def dot(one, two, one_dim=1, two_dim=0):
    return lax.dot_general(
        one, two, (((one_dim,), (two_dim,)), ((), ())), preferred_element_type=f32
    )


def small(one, two, one_dim=1, two_dim=0):
    return lax.dot_general(
        one,
        two,
        (((one_dim,), (two_dim,)), ((), ())),
        precision=lax.Precision.HIGH,
        preferred_element_type=f32,
    )


def call(kernel, grid, in_specs, out_specs, out_shape, scratch, flops, nbytes):
    return pl.pallas_call(
        kernel,
        grid=grid,
        in_specs=in_specs,
        out_specs=out_specs,
        out_shape=out_shape,
        scratch_shapes=scratch,
        compiler_params=pltpu.CompilerParams(vmem_limit_bytes=VMEM_BYTES),
        cost_estimate=pl.CostEstimate(flops=flops, bytes_accessed=nbytes, transcendentals=0),
    )


def project_kernel(vectors_ref, window_ref, out_ref, both_ref):
    width = vectors_ref.shape[0]

    @pl.when(pl.program_id(0) == 0)
    def _():
        high, low = halves(vectors_ref[...])
        both_ref[:width] = high
        both_ref[width:] = low

    high, low = halves(window_ref[...])
    first = dot(both_ref[...], high)
    out_ref[...] = first[:width] + first[width:] + dot(both_ref[:width], low)


def project(vectors, window, block=256):
    width, rows = vectors.shape
    cols = window.shape[1]
    return call(
        project_kernel,
        (cols // block,),
        [
            pl.BlockSpec((width, rows), lambda i: (0, 0)),
            pl.BlockSpec((rows, block), lambda i: (0, i)),
        ],
        pl.BlockSpec((width, block), lambda i: (0, i)),
        jax.ShapeDtypeStruct((width, cols), f32),
        [pltpu.VMEM((2 * width, rows), bf16)],
        6 * width * rows * cols,
        4 * (rows * cols + width * (rows + cols)),
    )(vectors, window)


def image_kernel(window_ref, vectors_ref, out_ref, both_ref):
    width = vectors_ref.shape[0]

    @pl.when(pl.program_id(0) == 0)
    def _():
        high, low = halves(vectors_ref[...])
        both_ref[:width] = high
        both_ref[width:] = low

    high, low = halves(window_ref[...])
    first = dot(high, both_ref[...], 1, 1)
    out_ref[...] = first[:, :width] + first[:, width:] + dot(low, both_ref[:width], 1, 1)


def image(window, vectors, block=512):
    rows, cols = window.shape
    width = vectors.shape[0]
    block = min(block, rows)
    return call(
        image_kernel,
        (rows // block,),
        [
            pl.BlockSpec((block, cols), lambda i: (i, 0)),
            pl.BlockSpec((width, cols), lambda i: (0, 0)),
        ],
        pl.BlockSpec((block, width), lambda i: (i, 0)),
        jax.ShapeDtypeStruct((rows, width), f32),
        [pltpu.VMEM((2 * width, cols), bf16)],
        6 * width * rows * cols,
        4 * (rows * cols + width * (rows + cols)),
    )(window, vectors)


def subtract_kernel(flip, window_ref, left_ref, right_ref, out_ref, high_ref, low_ref):
    @pl.when(pl.program_id(0) == 0)
    def _():
        high_ref[...], low_ref[...] = halves(right_ref[...])

    left = left_ref[...].T if flip else left_ref[...]
    high, low = halves(left)
    out_ref[...] = window_ref[...] - (
        dot(high, high_ref[...]) + (dot(high, low_ref[...]) + dot(low, high_ref[...]))
    )


def subtract(window, left, right, flip=False, block=512):
    rows, cols = window.shape
    width = right.shape[0]
    block = min(block, rows)
    if flip:
        left_spec = pl.BlockSpec((width, block), lambda i: (0, i))
    else:
        left_spec = pl.BlockSpec((block, width), lambda i: (i, 0))
    return call(
        functools.partial(subtract_kernel, flip),
        (rows // block,),
        [
            pl.BlockSpec((block, cols), lambda i: (i, 0)),
            left_spec,
            pl.BlockSpec((width, cols), lambda i: (0, 0)),
        ],
        pl.BlockSpec((block, cols), lambda i: (i, 0)),
        jax.ShapeDtypeStruct((rows, cols), f32),
        [pltpu.VMEM((width, cols), bf16)] * 2,
        6 * width * rows * cols,
        4 * (2 * rows * cols + width * (rows + cols)),
    )(window, left, right)


def spread(value, row_count, col_count):
    bits = [1 << bit for bit in range(row_count.bit_length() - 1)]
    row_index = lax.axis_index("row")
    col_index = lax.axis_index("col")
    distance = row_index ^ (col_index * row_count // col_count)
    results = []
    middle = value.shape[0] // 2
    for part, order in ((value[:middle], bits), (value[middle:], bits[::-1])):
        have = [0]
        for bit in order:
            pairs = []
            for col in range(col_count):
                source = col * row_count // col_count
                for offset in have:
                    pairs.append(
                        (
                            (source ^ offset) * col_count + col,
                            (source ^ offset ^ bit) * col_count + col,
                        )
                    )
            arrived = lax.ppermute(part, ("row", "col"), pairs)
            takes = functools.reduce(jnp.logical_or, [distance == offset ^ bit for offset in have])
            part = jnp.where(takes, arrived, part)
            have += [offset ^ bit for offset in have]
        results.append(part)
    return jnp.concatenate(results, 0)


def body(window, reflectors, factors):
    row_count = lax.axis_size("row")
    col_count = lax.axis_size("col")
    row_index = lax.axis_index("row")
    col_index = lax.axis_index("col")
    rows, cols = window.shape
    panels = reflectors.shape[0]
    slivers = jnp.swapaxes(reflectors, 1, 2)
    offset = (col_index * cols) % rows

    row_vectors, col_vectors, projected, images = [], [], [], []
    for panel in range(panels):
        vectors = lax.all_gather(slivers[panel], "col", axis=0, tiled=True)
        row_vectors.append(vectors)
        mine = lax.dynamic_slice_in_dim(vectors, offset, cols, 1)
        col_vectors.append(spread(mine, row_count, col_count))
    for panel in range(panels):
        projected.append(project(row_vectors[panel], window))
        images.append(image(window, col_vectors[panel]))
    row_all = jnp.concatenate(row_vectors, 0)
    col_all = jnp.concatenate(col_vectors, 0)
    projected = jnp.concatenate(projected, 0)
    crossed = small(projected, col_all, 1, 1)
    share = rows // col_count
    part = lax.dynamic_slice_in_dim(row_all, col_index * share, share, 1)
    inner = small(part, part, 1, 1)
    crossed, inner = lax.psum((crossed, inner), ("row", "col"))
    projected = lax.psum(projected, "row")
    images = [lax.psum(value, "col") for value in images]

    width = row_vectors[0].shape[0]
    joined = factors[0]
    for panel in range(1, panels):
        done = panel * width
        factor = factors[panel]
        between = -small(joined, small(inner[:done, done : done + width], factor))
        joined = jnp.block([[joined, between], [jnp.zeros((width, done), f32), factor]])
    right = small(joined, col_all)
    left = small(joined, projected - small(crossed, right), 0, 0)
    updated = subtract(window, row_all, left, flip=True)
    for panel in range(panels):
        updated = subtract(updated, images[panel], right[panel * width : (panel + 1) * width])
    return updated


def solution(mesh):
    placed = (P("row", "col"), P(None, "row", "col"), P())
    return jax.shard_map(
        body, mesh=mesh, in_specs=placed, out_specs=P("row", "col"), check_vma=False
    )
```

time: 663 us -> 570 us (0.86)
  matrix products: 240 us -> 20.8 us
  Pallas kernels: 0 us -> 112 us
  local copies, waits for them, and re-layouts: 76.4 us -> 14.2 us
  waiting for transfers between devices: 328 us -> 385 us
  starting transfers between devices: 0.21 us -> 11.9 us
  other arithmetic: 0 us -> 10.6 us
    dot_general x18 -> x7, matrix products: 240 us -> 20.8 us  [small(): lax.dot_general(one, two, (((one_dim,), (two_dim,)), ((), ())), precision...]
    psum x4 -> x3, waiting for transfers between devices: 134 us -> 285 us  [the longest x1 108 us: body(): images = [lax.psum(value, 'col') for value in images]]
    all_gather x2, waiting for transfers between devices: 193 us -> 57.9 us  [body(): vectors = lax.all_gather(slivers[panel], 'col', axis=0, tiled=True)]
    pallas_call x0 -> x7, Pallas kernels: none -> 112 us  [the longest x3 58.2 us: subtract(): call(functools.partial(subtract_kernel, flip), (rows // block,), [pl.Bloc...]
    ppermute x0 -> x8, waiting for transfers between devices: none -> 41.3 us  [spread(): arrived = lax.ppermute(part, ('row', 'col'), pairs)]
    unnamed x8 -> x34, local copies, waits for them, and re-layouts: 41.2 us -> 6.49 us
    reshape x2 -> x0, local copies, waits for them, and re-layouts: 33.1 us -> none  [body(): vectors = everything.reshape(row_count, col_count, rows_loc, piece_cols)]
    ppermute x0 -> x8, starting transfers between devices: none -> 11.7 us  [spread(): arrived = lax.ppermute(part, ('row', 'col'), pairs)]
  transfers between devices with their start and end apart: 6 -> 13, of which waited for: 6 -> 9; matrix products, arithmetic and copies ran while one was open for 24% -> 6% of each run, Pallas kernels for 0% -> 13%
where the time goes in v1:
time: 570 us; the launch traced here: 567 us
  waiting for transfers between devices  385 us (68%)
  Pallas kernels  112 us (20%)
  matrix products  20.8 us (4%)
  local copies, waits for them, and re-layouts  14.2 us (2%)
  between operations  13.5 us (2%)
  starting transfers between devices  11.9 us (2%)
  other arithmetic  10.6 us (2%)
    psum x1, waiting for transfers between devices, body(): images = [lax.psum(value, 'col') for value in images]  108 us
    psum x1, waiting for transfers between devices, body(): crossed, inner = lax.psum((crossed, inner), ('row', 'col'))  95.6 us
    psum x1, waiting for transfers between devices, body(): projected = lax.psum(projected, 'row')  81.1 us
    pallas_call x3, Pallas kernels, subtract(): call(functools.partial(subtract_kernel, flip), (rows // block,), [pl.Bloc...  58.2 us
    all_gather x2, waiting for transfers between devices, body(): vectors = lax.all_gather(slivers[panel], 'col', axis=0, tiled=True)  57.9 us
    ppermute x8, waiting for transfers between devices, spread(): arrived = lax.ppermute(part, ('row', 'col'), pairs)  41.3 us
    pallas_call x2, Pallas kernels, project(): call(project_kernel, (cols // block,), [pl.BlockSpec((width, rows), lambd...  27 us
    pallas_call x2, Pallas kernels, image(): call(image_kernel, (rows // block,), [pl.BlockSpec((block, cols), lambda...  26.5 us
  transfers between devices with their start and end apart: 13, of which 9 were waited for; matrix products, arithmetic and copies ran while one was open for 6% of the time, Pallas kernels for 13%

profile of v1, /device:TPU:8, one launch (start us, length us, event | category | flops | bytes accessed | tf_op | source)
XLA Modules:
  0.0 567.3 jit_solution(13760126471632791776)
XLA Ops:
  6.5 2.0 fusion.27
  8.6 0.0 all-gather.7.cloned.1.call-update
  8.6 0.0 all-gather.5.cloned.1.call-start
  8.7 0.7 all-gather.5.cloned.1.call-update
  9.4 0.0 all-reduce.9.cloned.1.call-start
  9.5 38.0 %all-gather.7.cloned.1.call-done = f32[1,256,3072]{2,1,0:T(8,128)} async-done(((f32[1,32,3072]{2,1,0:T(8,128)}), f32[1,256,3072]{2,1,0:T(8,128)}) %all-gather.7.cloned.1.call-update) | async-done | bytes 3145744 | tf_op jit(solution)/shard_map/all_gather | solution.py:190
  47.5 3.0 dynamic-slice_bitcast_fusion.1
  50.5 1.3 collective-permute-start.4
  51.8 1.5 collective-permute-start.6
  53.4 13.1 %shard_map.38 = f32[256,1536]{1,0:T(8,128)S(1)} custom-call(f32[256,3072]{1,0:T(8,128)} %bitcast.25, f32[3072,1536]{1,0:T(8,128)} %window_ref.9), custom_call_target="tpu_custom_call" | custom-call | flops 7247757312 | bytes 23592960 | tf_op jit(solution)/shard_map/pallas_call | solution.py:66
  66.4 19.9 %all-gather.5.cloned.1.call-done = f32[1,256,3072]{2,1,0:T(8,128)} async-done(((f32[1,32,3072]{2,1,0:T(8,128)}), f32[1,256,3072]{2,1,0:T(8,128)}) %all-gather.5.cloned.1.call-update) | async-done | bytes 3145744 | tf_op jit(solution)/shard_map/all_gather | solution.py:190
  86.3 13.9 %shard_map.37 = f32[256,1536]{1,0:T(8,128)S(1)} custom-call(f32[256,3072]{1,0:T(8,128)} %bitcast.28, f32[3072,1536]{1,0:T(8,128)} %window_ref.9), custom_call_target="tpu_custom_call" | custom-call | flops 7247757312 | bytes 23592960 | tf_op jit(solution)/shard_map/pallas_call | solution.py:66
  100.3 0.5 dynamic-slice_bitcast_fusion.3
  100.7 1.4 collective-permute-start
  102.2 0.7 collective-permute-start.2
  102.9 2.0 fusion.4
  104.9 0.0 collective-permute-done.4
  104.9 1.2 broadcast_select_fusion.4
  106.1 2.8 collective-permute-start.5
  109.0 1.2 broadcast_select_fusion
  110.2 1.3 collective-permute-start.7
  111.5 11.6 %collective-permute-done = f32[128,1536]{1,0:T(8,128)S(1)} collective-permute-done((f32[128,1536]{1,0:T(8,128)S(1)}, f32[128,1536]{1,0:T(8,128)S(1)}, u32[]{:S(2)}, u32[]{:S(2)}) %collective-permute-start) | collective-permute-done | bytes 786464 | tf_op jit(solution)/shard_map/ppermute | solution.py:170
  123.1 0.1 broadcast_select_fusion.5
  123.3 1.3 collective-permute-start.1
  124.6 0.1 broadcast_select_fusion.1
  124.7 1.3 collective-permute-start.3
  126.0 0.8 collective-permute-done.5
  126.8 0.1 broadcast_select_fusion.6
  126.9 16.1 %collective-permute-done.1 = f32[128,1536]{1,0:T(8,128)S(1)} collective-permute-done((f32[128,1536]{1,0:T(8,128)S(1)}, f32[128,1536]{1,0:T(8,128)S(1)}, u32[]{:S(2)}, u32[]{:S(2)}) %collective-permute-start.1) | collective-permute-done | bytes 786464 | tf_op jit(solution)/shard_map/ppermute | solution.py:170
  143.0 0.1 broadcast_select_fusion.7
  143.1 0.1 broadcast_select_fusion.2
  143.3 12.9 %collective-permute-done.3 = f32[128,1536]{1,0:T(8,128)S(1)} collective-permute-done((f32[128,1536]{1,0:T(8,128)S(1)}, f32[128,1536]{1,0:T(8,128)S(1)}, u32[]{:S(2)}, u32[]{:S(2)}) %collective-permute-start.3) | collective-permute-done | bytes 786464 | tf_op jit(solution)/shard_map/ppermute | solution.py:170
  156.2 0.1 broadcast_select_fusion.3
  156.3 0.9 copy-done.11
  157.2 3.8 fusion.1
  161.0 0.0 all-reduce.9.cloned.1.call-update
  161.0 0.0 all-reduce.7.cloned.1.call-start
  161.0 1.9 pad_maximum_fusion.1
  162.9 0.0 all-reduce.7.cloned.1.call-update
  162.9 0.0 all-reduce.11.cloned.1.call-start
  163.0 1.9 fusion.28
  164.9 1.8 copy.6
  166.7 0.8 copy.7
  167.5 5.4 pad_maximum_fusion.left_ref
  173.0 0.1 pad_maximum_fusion.5.vectors_ref
  173.1 1.0 copy-done.5
  174.1 0.2 copy-done.10
  174.3 0.1 pad_maximum_fusion.6.vectors_ref
  174.4 13.3 %shard_map.42 = f32[3072,256]{1,0:T(8,128)} custom-call(f32[3072,1536]{1,0:T(8,128)} %window_ref.9, f32[256,1536]{1,0:T(8,128)S(1)} %pad_maximum_fusion.6.vectors_ref), custom_call_target="tpu_custom_call" | custom-call | flops 7247757312 | bytes 23592960 | tf_op jit(solution)/shard_map/pallas_call | solution.py:99
  187.8 13.1 %shard_map.40 = f32[3072,256]{1,0:T(8,128)} custom-call(f32[3072,1536]{1,0:T(8,128)} %window_ref.9, f32[256,1536]{1,0:T(8,128)S(1)} %pad_maximum_fusion.5.vectors_ref), custom_call_target="tpu_custom_call" | custom-call | flops 7247757312 | bytes 23592960 | tf_op jit(solution)/shard_map/pallas_call | solution.py:99
  200.9 0.0 all-reduce.11.cloned.1.call-update
  201.0 95.6 %all-reduce.9.cloned.1.call-done = (f32[512,512]{1,0:T(8,128)}, f32[512,512]{1,0:T(8,128)}) async-done(((f32[512,512]{1,0:T(8,128)}, f32[512,512]{1,0:T(8,128)}), (f32[512,512]{1,0:T(8,128)}, f32[512,512]{1,0:T(8,128)})) %all-reduce.9.cloned.1.call-update) | async-done | bytes 2097168 | tf_op jit(solution)/shard_map/psum | solution.py:204
  296.5 1.3 fusion.11
  297.8 1.3 fusion.2
  299.2 3.8 fusion
  303.0 1.7 copy-done.3
  304.7 0.2 fusion.26
  304.9 81.1 %all-reduce.7.cloned.1.call-done = f32[512,1536]{1,0:T(8,128)} async-done(((f32[512,1536]{1,0:T(8,128)}), f32[512,1536]{1,0:T(8,128)}) %all-reduce.7.cloned.1.call-update) | async-done | bytes 3145744 | tf_op jit(solution)/shard_map/psum | solution.py:205
  386.0 5.9 %convolution_subtract_fusion = f32[512,1536]{1,0:T(8,128)S(1)} fusion(f32[512,1536]{1,0:T(8,128)} %all-reduce.7.cloned.1.call-done, f32[512,512]{1,0:T(8,128)} %get-tuple-element.5, f32[512,1536]{1,0:T(8,128)} %copy-done.3), kind=kOutput, calls=%fused_computation.3 | convolution fusion | flops 2416705536 | bytes 10485760 | tf_op jit(solution)/shard_map/dot_general | solution.py:27
  391.9 2.7 fusion.6.right_ref
  394.6 22.2 %shard_map.39.window_ref = f32[3072,1536]{1,0:T(8,128)} custom-call(f32[3072,1536]{1,0:T(8,128)} %window_ref.9, f32[512,3072]{1,0:T(8,128)} %pad_maximum_fusion.left_ref, f32[512,1536]{1,0:T(8,128)S(1)} %fusion.6.right_ref), custom_call_target="tpu_custom_call" | custom-call | flops 14495514624 | bytes 47185920 | tf_op jit(solution)/shard_map/pallas_call | solution.py:134
  416.8 107.9 %all-reduce.11.cloned.1.call-done = (f32[3072,256]{1,0:T(8,128)}, f32[3072,256]{1,0:T(8,128)}) async-done(((f32[3072,256]{1,0:T(8,128)}, f32[3072,256]{1,0:T(8,128)}), (f32[3072,256]{1,0:T(8,128)}, f32[3072,256]{1,0:T(8,128)})) %all-reduce.11.cloned.1.call-update) | async-done | bytes 6291472 | tf_op jit(solution)/shard_map/psum | solution.py:206
  524.7 18.0 %shard_map.41.window_ref = f32[3072,1536]{1,0:T(8,128)} custom-call(f32[3072,1536]{1,0:T(8,128)} %shard_map.39.window_ref, f32[3072,256]{1,0:T(8,128)} %get-tuple-element.7.left_ref, f32[256,1536]{1,0:T(8,128)S(1)} %get-tuple-element.10.right_ref), custom_call_target="tpu_custom_call" | custom-call | flops 7247757312 | bytes 42467328 | tf_op jit(solution)/shard_map/pallas_call | solution.py:134
  542.7 18.0 %shard_map.43 = f32[3072,1536]{1,0:T(8,128)} custom-call(f32[3072,1536]{1,0:T(8,128)} %shard_map.41.window_ref, f32[3072,256]{1,0:T(8,128)} %get-tuple-element.8.left_ref, f32[256,1536]{1,0:T(8,128)S(1)} %get-tuple-element.9.right_ref), custom_call_target="tpu_custom_call" | custom-call | flops 7247757312 | bytes 42467328 | tf_op jit(solution)/shard_map/pallas_call | solution.py:134
  (32 shorter events, 0.1 us)
Async XLA Ops:
  6.5 41.0 %all-gather.7.cloned.1.call-start = ((), (), s32[]{:S(2)}) async-start(), calls=%async_computation.2 | async-start | bytes 3538944 | tf_op jit(solution)/shard_map/all_gather | solution.py:190
  8.6 77.7 %all-gather.5.cloned.1.call-start = ((), (), s32[]{:S(2)}) async-start(), calls=%async_computation.1 | async-start | bytes 3538944 | tf_op jit(solution)/shard_map/all_gather | solution.py:190
  9.4 287.2 %all-reduce.9.cloned.1.call-start = ((), (), s32[]{:S(2)}) async-start(), calls=%async_computation.3 | async-start | bytes 4194304 | tf_op jit(solution)/shard_map/psum | solution.py:204
  50.5 54.4 %collective-permute-start.4 = (f32[128,1536]{1,0:T(8,128)}, f32[128,1536]{1,0:T(8,128)}, u32[]{:S(2)}, u32[]{:S(2)}) collective-permute-start(f32[128,1536]{1,0:T(8,128)} %get-tuple-element.13), channel_id=1, source_target_pairs={{0,8},{1,9},{10,2},{11,3},{20,28},{21,29},{30,22},{31,23}} | collective-permute-start | bytes 2359304 | tf_op jit(solution)/shard_map/ppermute | solution.py:170
  51.8 57.2 %collective-permute-start.6 = (f32[128,1536]{1,0:T(8,128)}, f32[128,1536]{1,0:T(8,128)}, u32[]{:S(2)}, u32[]{:S(2)}) collective-permute-start(f32[128,1536]{1,0:T(8,128)} %get-tuple-element.14), channel_id=1, source_target_pairs={{0,16},{1,17},{10,26},{11,27},{20,4},{21,5},{30,14},{31,15}} | collective-permute-start | bytes 2359304 | tf_op jit(solution)/shard_map/ppermute | solution.py:170
  86.3 13.9 %copy-start.2 = (f32[1,256,3072]{2,1,0:T(8,128)S(1)}, f32[1,256,3072]{2,1,0:T(8,128)}, u32[]{:S(2)}) copy-start(f32[1,256,3072]{2,1,0:T(8,128)} %all-gather.5.cloned.1.call-done) | copy-start | bytes 9437188
  100.3 2.6 copy-start
  100.7 22.4 %collective-permute-start = (f32[128,1536]{1,0:T(8,128)S(1)}, f32[128,1536]{1,0:T(8,128)S(1)}, u32[]{:S(2)}, u32[]{:S(2)}) collective-permute-start(f32[128,1536]{1,0:T(8,128)S(1)} %get-tuple-element.11), channel_id=1, source_target_pairs={{0,8},{1,9},{10,2},{11,3},{20,28},{21,29},{30,22},{31,23}} | collective-permute-start | bytes 2359304 | tf_op jit(solution)/shard_map/ppermute | solution.py:170
  102.2 22.4 %collective-permute-start.2 = (f32[128,1536]{1,0:T(8,128)S(1)}, f32[128,1536]{1,0:T(8,128)S(1)}, u32[]{:S(2)}, u32[]{:S(2)}) collective-permute-start(f32[128,1536]{1,0:T(8,128)S(1)} %get-tuple-element.12), channel_id=1, source_target_pairs={{0,16},{1,17},{10,26},{11,27},{20,4},{21,5},{30,14},{31,15}} | collective-permute-start | bytes 2359304 | tf_op jit(solution)/shard_map/ppermute | solution.py:170
  106.1 20.7 %collective-permute-start.5 = (f32[128,1536]{1,0:T(8,128)S(1)}, f32[128,1536]{1,0:T(8,128)S(1)}, u32[]{:S(2)}, u32[]{:S(2)}) collective-permute-start(f32[128,1536]{1,0:T(8,128)S(1)} %broadcast_select_fusion.4), channel_id=1, source_target_pairs={{0,16},{8,24},{1,17},{9,25},{10,26},{2,18},{11,27},{3,19},{20,4},{... | collective-permute-start | bytes 2359304 | tf_op jit(solution)/shard_map/ppermute | solution.py:170
  110.2 32.9 %collective-permute-start.7 = (f32[128,1536]{1,0:T(8,128)S(1)}, f32[128,1536]{1,0:T(8,128)S(1)}, u32[]{:S(2)}, u32[]{:S(2)}) collective-permute-start(f32[128,1536]{1,0:T(8,128)S(1)} %broadcast_select_fusion), channel_id=1, source_target_pairs={{0,8},{16,24},{1,9},{17,25},{10,2},{26,18},{11,3},{27,19},{20,28},... | collective-permute-start | bytes 2359304 | tf_op jit(solution)/shard_map/ppermute | solution.py:170
  123.3 19.7 %collective-permute-start.1 = (f32[128,1536]{1,0:T(8,128)S(1)}, f32[128,1536]{1,0:T(8,128)S(1)}, u32[]{:S(2)}, u32[]{:S(2)}) collective-permute-start(f32[128,1536]{1,0:T(8,128)S(1)} %broadcast_select_fusion.5), channel_id=1, source_target_pairs={{0,16},{8,24},{1,17},{9,25},{10,26},{2,18},{11,27},{3,19},{20,4},{... | collective-permute-start | bytes 2359304 | tf_op jit(solution)/shard_map/ppermute | solution.py:170
  124.7 31.4 %collective-permute-start.3 = (f32[128,1536]{1,0:T(8,128)S(1)}, f32[128,1536]{1,0:T(8,128)S(1)}, u32[]{:S(2)}, u32[]{:S(2)}) collective-permute-start(f32[128,1536]{1,0:T(8,128)S(1)} %broadcast_select_fusion.1), channel_id=1, source_target_pairs={{0,8},{16,24},{1,9},{17,25},{10,2},{26,18},{11,3},{27,19},{20,28},... | collective-permute-start | bytes 2359304 | tf_op jit(solution)/shard_map/ppermute | solution.py:170
  126.9 29.4 %copy-start.4 = (f32[128,1536]{1,0:T(8,128)}, f32[128,1536]{1,0:T(8,128)S(1)}, u32[]{:S(2)}) copy-start(f32[128,1536]{1,0:T(8,128)S(1)} %broadcast_select_fusion.6) | copy-start | bytes 2359300
  143.1 13.1 %copy-start.6 = (f32[128,1536]{1,0:T(8,128)}, f32[128,1536]{1,0:T(8,128)S(1)}, u32[]{:S(2)}) copy-start(f32[128,1536]{1,0:T(8,128)S(1)} %broadcast_select_fusion.7) | copy-start | bytes 2359300
  143.3 13.0 %copy-start.9 = (f32[128,1536]{1,0:T(8,128)}, f32[128,1536]{1,0:T(8,128)S(1)}, u32[]{:S(2)}) copy-start(f32[128,1536]{1,0:T(8,128)S(1)} %broadcast_select_fusion.2) | copy-start | bytes 2359300
  156.3 0.9 copy-start.11
  161.0 225.0 %all-reduce.7.cloned.1.call-start = ((), (), s32[]{:S(2)}) async-start(), calls=%async_computation | async-start | bytes 6291456 | tf_op jit(solution)/shard_map/psum | solution.py:205
  162.9 4.6 copy-start.1
  162.9 361.8 %all-reduce.11.cloned.1.call-start = ((), (), s32[]{:S(2)}) async-start(), calls=%async_computation.4 | async-start | bytes 12582912 | tf_op jit(solution)/shard_map/psum | solution.py:206
  167.5 5.4 copy-start.7
  167.5 5.4 copy-start.12
  172.9 1.1 copy-start.5
  172.9 1.4 copy-start.10
  200.9 98.3 %copy-start.8 = (f32[128,1536]{1,0:T(8,128)S(1)}, f32[128,1536]{1,0:T(8,128)}, u32[]{:S(2)}) copy-start(f32[128,1536]{1,0:T(8,128)} %copy-done.6) | copy-start | bytes 2359300
  200.9 98.3 %copy-start.13 = (f32[128,1536]{1,0:T(8,128)S(1)}, f32[128,1536]{1,0:T(8,128)}, u32[]{:S(2)}) copy-start(f32[128,1536]{1,0:T(8,128)} %copy-done.11) | copy-start | bytes 2359300
  303.0 1.7 copy-start.3
  386.0 5.9 %copy-start.14 = (f32[1,256,256]{1,2,0:T(8,128)S(1)}, f32[1,256,256]{1,2,0:T(8,128)}, u32[]{:S(2)}) copy-start(f32[1,256,256]{1,2,0:T(8,128)} %copy.6) | copy-start | bytes 786436
  386.0 5.9 %copy-start.15 = (f32[1,256,256]{1,2,0:T(8,128)S(1)}, f32[1,256,256]{1,2,0:T(8,128)}, u32[]{:S(2)}) copy-start(f32[1,256,256]{1,2,0:T(8,128)} %copy.7) | copy-start | bytes 786436
Sparse Core Ops, SparseCore 0:
  9.0 38.4 all-gather.6
  49.1 37.1 all-gather.4
  161.1 135.3 all-reduce.8
  299.8 86.1 all-reduce.6
  388.2 136.4 all-reduce.10

commit v2 on v1

v2 whole, which is shorter than its diff:
```python
import functools

import jax
import jax.numpy as jnp
from jax import lax
from jax.experimental import pallas as pl
from jax.experimental.pallas import tpu as pltpu
from jax.sharding import PartitionSpec as P

f32 = jnp.float32
bf16 = jnp.bfloat16
VMEM_BYTES = 50 * 1024 * 1024


def halves(value):
    high = value.astype(bf16)
    return high, (value - high.astype(f32)).astype(bf16)


def dot(one, two, one_dim=1, two_dim=0):
    return lax.dot_general(
        one, two, (((one_dim,), (two_dim,)), ((), ())), preferred_element_type=f32
    )


def small(one, two, one_dim=1, two_dim=0):
    return lax.dot_general(
        one,
        two,
        (((one_dim,), (two_dim,)), ((), ())),
        precision=lax.Precision.HIGH,
        preferred_element_type=f32,
    )


def call(kernel, grid, in_specs, out_specs, out_shape, scratch=(), aliases=None):
    return pl.pallas_call(
        kernel,
        grid=grid,
        in_specs=in_specs,
        out_specs=out_specs,
        out_shape=out_shape,
        scratch_shapes=scratch,
        input_output_aliases=aliases or {},
        compiler_params=pltpu.CompilerParams(vmem_limit_bytes=VMEM_BYTES),
        cost_estimate=pl.CostEstimate(flops=1, bytes_accessed=1, transcendentals=0),
    )


def project_kernel(vectors_ref, window_ref, out_ref, both_ref):
    width = vectors_ref.shape[0]

    @pl.when(pl.program_id(0) == 0)
    def _():
        high, low = halves(vectors_ref[...])
        both_ref[:width] = high
        both_ref[width:] = low

    high, low = halves(window_ref[...])
    first = dot(both_ref[...], high)
    out_ref[...] = first[:width] + first[width:] + dot(both_ref[:width], low)


def project(vectors, window, block=256):
    width, rows = vectors.shape
    cols = window.shape[1]
    return call(
        project_kernel,
        (cols // block,),
        [
            pl.BlockSpec((width, rows), lambda i: (0, 0)),
            pl.BlockSpec((rows, block), lambda i: (0, i)),
        ],
        pl.BlockSpec((width, block), lambda i: (0, i)),
        jax.ShapeDtypeStruct((width, cols), f32),
        [pltpu.VMEM((2 * width, rows), bf16)],
    )(vectors, window)


def image_kernel(window_ref, vectors_ref, out_ref, both_ref):
    width = vectors_ref.shape[0]

    @pl.when(pl.program_id(0) == 0)
    def _():
        high, low = halves(vectors_ref[...])
        both_ref[:width] = high
        both_ref[width:] = low

    high, low = halves(window_ref[...])
    first = dot(high, both_ref[...], 1, 1)
    out_ref[...] = first[:, :width] + first[:, width:] + dot(low, both_ref[:width], 1, 1)


def image(window, vectors, block=512):
    rows, cols = window.shape
    width = vectors.shape[0]
    block = min(block, rows)
    return call(
        image_kernel,
        (rows // block,),
        [
            pl.BlockSpec((block, cols), lambda i: (i, 0)),
            pl.BlockSpec((width, cols), lambda i: (0, 0)),
        ],
        pl.BlockSpec((block, width), lambda i: (i, 0)),
        jax.ShapeDtypeStruct((rows, width), f32),
        [pltpu.VMEM((2 * width, cols), bf16)],
    )(window, vectors)


def three_products(high, low, high_ref, low_ref):
    return dot(high, high_ref[...]) + (dot(high, low_ref[...]) + dot(low, high_ref[...]))


def update_kernel(window_ref, near_ref, far_ref, high_ref, low_ref, out_ref):
    vectors = jnp.concatenate([near_ref[...].T, far_ref[...].T], 1)
    out_ref[...] = window_ref[...] - three_products(*halves(vectors), high_ref, low_ref)


def update(window, near, far, high, low, block=512):
    rows, cols = window.shape
    part, width = near.shape[0], high.shape[0]
    block = min(block, rows)
    return call(
        update_kernel,
        (rows // block,),
        [
            pl.BlockSpec((block, cols), lambda i: (i, 0)),
            pl.BlockSpec((part, block), lambda i: (0, i)),
            pl.BlockSpec((part, block), lambda i: (0, i)),
            pl.BlockSpec((width, cols), lambda i: (0, 0)),
            pl.BlockSpec((width, cols), lambda i: (0, 0)),
        ],
        pl.BlockSpec((block, cols), lambda i: (i, 0)),
        jax.ShapeDtypeStruct((rows, cols), f32),
    )(window, near, far, high, low)


def finish_kernel(
    window_ref, near_ref, far_ref, middle_high, middle_low, high_ref, low_ref, *refs
):
    vectors = jnp.concatenate([near_ref[...].T, far_ref[...].T], 1)
    *image_refs, out_ref = refs
    images = jnp.concatenate([one[...] for one in image_refs], 1)
    left = images - three_products(*halves(vectors), middle_high, middle_low)
    out_ref[...] = window_ref[...] - three_products(*halves(left), high_ref, low_ref)


def finish(window, near, far, images, middle, right, block=512):
    rows, cols = window.shape
    part, width = near.shape[0], right[0].shape[0]
    block = min(block, rows)
    return call(
        finish_kernel,
        (rows // block,),
        [
            pl.BlockSpec((block, cols), lambda i: (i, 0)),
            pl.BlockSpec((part, block), lambda i: (0, i)),
            pl.BlockSpec((part, block), lambda i: (0, i)),
            pl.BlockSpec((width, width), lambda i: (0, 0)),
            pl.BlockSpec((width, width), lambda i: (0, 0)),
            pl.BlockSpec((width, cols), lambda i: (0, 0)),
            pl.BlockSpec((width, cols), lambda i: (0, 0)),
        ]
        + [pl.BlockSpec((block, one.shape[1]), lambda i: (i, 0)) for one in images],
        pl.BlockSpec((block, cols), lambda i: (i, 0)),
        jax.ShapeDtypeStruct((rows, cols), f32),
        aliases={0: 0},
    )(window, near, far, *middle, *right, *images)


def swap_cores(value):
    count = lax.axis_size("col")
    return lax.ppermute(value, "col", [(col, col ^ 1) for col in range(count)])


def swap_chips(value, distance):
    count = lax.axis_size("col")
    return lax.ppermute(value, "col", [(col, col ^ (2 * distance)) for col in range(count)])


def swap_rows(value, distance):
    count = lax.axis_size("row")
    return lax.ppermute(value, "row", [(row, row ^ distance) for row in range(count)])


def at(value, index, dim):
    return lax.dynamic_index_in_dim(value, index, dim, keepdims=False)


def put(whole, value, index, dim):
    return lax.dynamic_update_slice_in_dim(whole, jnp.expand_dims(value, dim), index, dim)


def together(*values):
    return lax.optimization_barrier(values)


def region(run, *operands):
    results = jax.eval_shape(run, *operands)

    def nothing(*_):
        return jax.tree.map(lambda one: jnp.zeros(one.shape, one.dtype), results)

    return lax.cond(lax.axis_index("col") >= 0, run, nothing, *operands)


def ordered(condition, one, two, dim):
    return jnp.concatenate([jnp.where(condition, one, two), jnp.where(condition, two, one)], dim)


def by_chip(choose):
    chip = lax.axis_index("col") // 2
    value = choose(0)
    for one in range(1, lax.axis_size("col") // 2):
        value = jnp.where(chip == one, choose(one), value)
    return value


def send_along(value, chips, step, count=None):
    count = chips if count is None else count
    ends = range(count) if step < 0 else range(chips - count, chips)
    return lax.ppermute(
        value,
        "col",
        [
            (2 * (chip - step) + core, 2 * chip + core)
            for chip in ends
            for core in range(2)
            if 0 <= chip - step < chips
        ],
    )


def both_cores(mine, other):
    core = lax.axis_index("col") % 2
    pairs = []
    for place in range(mine.shape[1]):
        one, two = mine[:, place], other[:, place]
        pairs += [jnp.where(core == 0, one, two), jnp.where(core == 0, two, one)]
    return jnp.concatenate(pairs, 1).reshape(-1, mine.shape[-1])


def gather_vectors(slivers, row_count, chips, window):
    col_index, row = lax.axis_index("col"), lax.axis_index("row")
    core, chip = col_index % 2, col_index // 2
    panels, piece, rows = slivers.shape
    cols = rows // 2
    share = 2 * piece // row_count
    distances = range(1, row_count)
    half = chips // 2

    mine = lax.dynamic_slice_in_dim(slivers, core * cols, cols, 2)
    other = swap_cores(lax.dynamic_slice_in_dim(slivers, (1 - core) * cols, cols, 2))
    shares = ordered(core == 0, mine, other, 1).reshape(panels, row_count, share, cols)
    arrived = [swap_rows(at(shares, row ^ distance, 1), distance) for distance in distances]
    held = {0: slivers}
    for step in range(1, half):
        after, before, *arrived = together(
            send_along(held[step - 1], chips, -1), send_along(held[1 - step], chips, 1), *arrived
        )
        held[step], held[-step] = after, before
    by_row = jnp.zeros((panels, row_count, share, cols), f32)
    by_row = put(by_row, at(shares, row, 1), row, 1)
    for distance, value in zip(distances, arrived):
        by_row = put(by_row, value, row ^ distance, 1)

    near = jnp.stack(
        [by_chip(lambda one: held[one // half * half + place - one]) for place in range(half)], 1
    )

    def along_line(panel):
        return [swap_chips(at(by_row[panel], chip ^ distance, 0), distance) for distance in distances]

    def line_shares(panel, arrived):
        shares = jnp.zeros((row_count, share, cols), f32)
        shares = put(shares, at(by_row[panel], chip, 0), chip, 0)
        for distance, value in zip(distances, arrived):
            shares = put(shares, value, chip ^ distance, 0)
        return shares

    def all_rows(shares, arrived):
        whole = jnp.zeros((row_count, row_count, share, cols), f32)
        whole = put(whole, shares, row, 1)
        for distance, value in zip(distances, arrived):
            whole = put(whole, value, row ^ distance, 1)
        return whole.reshape(2 * chips * piece, cols)

    other, arrived = together(swap_cores(near), along_line(0))
    near = both_cores(near, other)
    shares = [line_shares(0, arrived)]
    last = (held[half - 1], held[1 - half])
    *last, near, shares[0] = together(*last, near, shares[0])

    columns, images = [], []
    for panel in range(panels):
        arrived = [swap_rows(shares[panel], distance) for distance in distances]
        following = along_line(panel + 1) if panel + 1 < panels else []
        if panel == 0:
            projected, arrived, following = together(project(near, window), arrived, following)
        else:
            jumps = range(1, half)
            after = [send_along(last[0], chips, -jump, chips - half - jump + 1) for jump in jumps]
            before = [send_along(last[1], chips, jump, chips - half - jump + 1) for jump in jumps]
            images.append(image(window, columns[-1]))
            images[-1], arrived, following, after, before = together(
                images[-1], arrived, following, after, before
            )
            for jump, one, two in zip(jumps, after, before):
                held[half - 1 + jump], held[1 - half - jump] = one, two
        columns.append(all_rows(shares[panel], arrived))
        if following:
            shares.append(line_shares(panel + 1, following))
    ends = lax.ppermute(
        jnp.where(chip < half, last[1], last[0]),
        "col",
        [
            (2 * one + which, 2 * two + which)
            for one, two in ((half, 0), (half - 1, chips - 1))
            for which in range(2)
        ],
    )
    return near, held, ends, columns, projected, images


def scatter_step(value, bit):
    half = value.shape[0] // 2
    upper = (lax.axis_index("row") // bit) % 2
    sent = lax.dynamic_slice_in_dim(value, (1 - upper) * half, half, 0)
    kept = lax.dynamic_slice_in_dim(value, upper * half, half, 0)
    return swap_rows(sent, bit), kept


def gather_step(value, bit):
    upper = (lax.axis_index("row") // bit) % 2
    return ordered(upper == 0, value, swap_rows(value, bit), 1)


def line_step(value, hop, chips):
    middle = chips // 2
    place = lax.axis_index("col") // 2
    if hop < middle:
        pairs = [(hop, hop + 1), (chips - 1 - hop, chips - 2 - hop)]
    else:
        hop = chips - 2 - hop
        pairs = [(hop + 1, hop), (chips - 2 - hop, chips - 1 - hop)]
    arrived = lax.ppermute(
        value, "col", [(2 * one + core, 2 * two + core) for one, two in pairs for core in range(2)]
    )

    def combine(value, arrived):
        if pairs[0][0] < pairs[0][1]:
            return value + arrived
        return jnp.where((place == pairs[0][1]) | (place == pairs[1][1]), arrived, value)

    return arrived, combine


def split(value):
    high = lax.reduce_precision(value, 8, 7)
    return high.astype(bf16), (value - high).astype(bf16)


def region(run, *operands):
    results = jax.eval_shape(run, *operands)

    def nothing(*_):
        return jax.tree.map(lambda one: jnp.zeros(one.shape, one.dtype), results)

    return lax.cond(lax.axis_index("col") >= 0, run, nothing, *operands)


def together(*values):
    return lax.optimization_barrier(values)


def body(window, reflectors, factors):
    row_count = lax.axis_size("row")
    chips = lax.axis_size("col") // 2
    row, chip = lax.axis_index("row"), lax.axis_index("col") // 2
    lower = chip < chips // 2
    rows, cols = window.shape
    panels = reflectors.shape[0]
    bits = [1 << bit for bit in range(row_count.bit_length() - 1)]
    orders = [bits[::-1] if panel % 2 else bits for panel in range(panels)]
    slivers = jnp.swapaxes(reflectors, 1, 2)
    near, held, ends, columns, near_projected, images = gather_vectors(
        slivers, row_count, chips, window
    )
    summed = [lax.psum(one, "col") for one in images]
    near_parts = [
        near_projected[near.shape[0] // panels * panel : near.shape[0] // panels * (panel + 1)]
        for panel in range(panels)
    ]
    steps = [scatter_step(one, order[0]) for one, order in zip(near_parts, orders)]
    last_columns, *images = together(columns[-1], *images)
    last_image, ends, *arrived = together(
        image(window, last_columns), ends, *[one for one, _ in steps]
    )
    near_parts = [one + kept for one, (_, kept) in zip(arrived, steps)]
    summed.append(lax.psum(last_image, "col"))
    half = chips // 2
    held[chips - 1], held[1 - chips] = ends, ends
    far = jnp.stack(
        [
            by_chip(lambda one: held[(1 - one // half) * half + place - one])
            for place in range(half)
        ],
        1,
    )
    columns = jnp.concatenate(columns, 0)
    total = columns.shape[0]
    width = total // panels
    part = width // 2

    def projections(window, near, far, columns, factors, *near_parts):
        near_parts = list(near_parts)
        far = both_cores(far, swap_cores(far))
        far_projected = project(far, window)
        for step in range(1, len(bits)):
            steps = [scatter_step(one, order[step]) for one, order in zip(near_parts, orders)]
            arrived = [one for one, _ in steps]
            if step == 1:
                far_projected, *arrived = together(far_projected, *arrived)
            near_parts = [one + kept for one, (_, kept) in zip(arrived, steps)]
        far_projected, near, far = together(far_projected, near, far)
        far_parts = [far_projected[part * panel : part * (panel + 1)] for panel in range(panels)]
        same, mixed, opposite = small(near, near, 1, 1), small(near, far, 1, 1), small(far, far, 1, 1)

        def of(value, one, two):
            return value[part * one : part * (one + 1), part * two : part * (two + 1)]

        inner = [
            ordered(
                lower,
                ordered(lower, of(same, one, two), of(mixed, one, two), 1),
                ordered(lower, of(mixed, two, one).T, of(opposite, one, two), 1),
                0,
            )
            for one in range(panels)
            for two in range(one + 1, panels)
        ]
        for step in range(len(bits)):
            steps = [scatter_step(one, order[step]) for one, order in zip(far_parts, orders)]
            arrived = [one for one, _ in steps]
            if step + 1 == len(bits):
                arrived, inner = together(arrived, inner)
            far_parts = [one + kept for one, (_, kept) in zip(arrived, steps)]

        mine = [ordered(lower, one, two, 0) for one, two in zip(near_parts, far_parts)]
        crossed = small(jnp.concatenate(mine, 0), columns, 1, 1)
        parts = [jnp.stack([one, two]) for one, two in zip(near_parts, far_parts)]
        others = [swap_rows(one, bits[0]) for one in inner]
        other, parts, others = together(
            swap_cores(crossed),
            [gather_step(one, order[-1]) for one, order in zip(parts, orders)],
            others,
        )
        crossed = crossed + other
        inner = [one + two for one, two in zip(inner, others)]
        arrived, combine = line_step(crossed, 0, chips)
        for step in range(len(bits) - 1)[::-1]:
            parts = [gather_step(one, order[step]) for one, order in zip(parts, orders)]
        for bit in bits[1:]:
            inner = [one + swap_rows(one, bit) for one in inner]
        arrived, parts, inner = together(arrived, parts, inner)
        crossed = combine(crossed, arrived)
        projected = jnp.concatenate(parts, 0).reshape(total, cols)

        joined = factors[0]
        for panel in range(1, panels):
            done = panel * width
            products = jnp.concatenate(
                [
                    inner[one * (panels - 1) - one * (one - 1) // 2 + panel - one - 1]
                    for one in range(panel)
                ],
                0,
            )
            between = -small(joined, small(products, factors[panel]))
            joined = jnp.block([[joined, between], [jnp.zeros((width, done), f32), factors[panel]]])
        def chosen(value, panel, other, dim):
            start = panel * width
            one = lax.slice_in_dim(value, start, start + part, axis=dim)
            two = lax.slice_in_dim(value, start + part, start + width, axis=dim)
            return jnp.where(lower == (other == 0), one, two)

        local = jnp.concatenate(
            [chosen(joined, panel, other, 1) for other in range(2) for panel in range(panels)], 1
        )
        both = jnp.concatenate(
            [chosen(local, panel, other, 0) for panel in range(panels) for other in range(2)], 0
        )
        left = split(small(both, projected, 0, 0))
        if chips > 2:
            arrived, combine = line_step(crossed, 1, chips)
            arrived, *left = together(arrived, *left)
            crossed = combine(crossed, arrived)

        def last_step(crossed, window, near, far, *left):
            arrived, combine = line_step(crossed, chips - 2, chips)
            updated, arrived = together(update(window, near, far, *left), arrived)
            return combine(crossed, arrived), updated

        for hop in range(2, chips - 2):
            arrived, combine = line_step(crossed, hop, chips)
            crossed = combine(crossed, arrived)
        if chips > 2:
            crossed, updated = region(last_step, crossed, window, near, far, *left)
        else:
            updated = update(window, near, far, *left)
        everyone = [swap_rows(crossed, distance) for distance in range(1, row_count)]
        right, everyone = together(split(small(joined, columns)), everyone)
        everyone = [crossed] + everyone
        crossed = jnp.zeros((panels, 2, part, total), f32)
        for distance, value in enumerate(everyone):
            source = row ^ distance
            value = value.reshape(panels, 2, -1, total)
            for panel, order in enumerate(orders):
                place, size = 0, part
                for bit in order:
                    size = size // 2
                    place = place + (source // bit) % 2 * size
                crossed = lax.dynamic_update_slice(
                    crossed, value[panel : panel + 1], (panel, 0, place, 0)
                )
        between = split(small(local, crossed.reshape(total, total), 0, 0))
        return updated, far, between, right

    updated, far, between, right = region(
        projections, window, near, far, columns, factors, *near_parts
    )
    return finish(updated, near, far, summed, between, right)


def solution(mesh):
    placed = (P("row", "col"), P(None, "row", "col"), P())
    return jax.shard_map(
        body, mesh=mesh, in_specs=placed, out_specs=P("row", "col"), check_vma=False
    )
```

time: 570 us -> 326 us (0.57)
  waiting for transfers between devices: 385 us -> 76 us
  starting transfers between devices: 11.9 us -> 57.9 us
  other arithmetic: 10.6 us -> 32.1 us
  Pallas kernels: 112 us -> 98.5 us
  local copies, waits for them, and re-layouts: 14.2 us -> 22.7 us
    psum x3 -> x1, waiting for transfers between devices: 285 us -> 0.01 us  [body(): summed = [lax.psum(one, 'col') for one in images]]
    all_gather x2 -> x0, waiting for transfers between devices: 57.9 us -> none  [body(): vectors = lax.all_gather(slivers[panel], 'col', axis=0, tiled=True)]
    ppermute x8 -> x44, starting transfers between devices: 11.7 us -> 57.9 us  [the longest x26 29.2 us: swap_rows(): lax.ppermute(value, 'row', [(row, row ^ distance) for row in range(count)])]
    ppermute x8 -> x44, waiting for transfers between devices: 41.3 us -> 76 us  [the longest x26 52.2 us: swap_rows(): lax.ppermute(value, 'row', [(row, row ^ distance) for row in range(count)])]
    select_n x8 -> x17, other arithmetic: 3.11 us -> 15 us  [the longest x2 4.39 us: by_chip(): value = jnp.where(chip == one, choose(one), value)]
    pallas_call x3 -> x2, Pallas kernels: 58.2 us -> 47.1 us  [the longest x1 26.4 us: finish(): call(finish_kernel, (rows // block,), [pl.BlockSpec((block, cols), lambda...]
    cond x0 -> x49, local copies, waits for them, and re-layouts: none -> 7.7 us
    add x0 -> x9, other arithmetic: none -> 7.31 us  [the longest x2 2.34 us: body(): near_parts = [one + kept for one, (_, kept) in zip(arrived, steps)]]
  transfers between devices with their start and end apart: 13 -> 45, of which waited for: 9 -> 17; matrix products, arithmetic and copies ran while one was open for 6% -> 21% of each run, Pallas kernels for 13% -> 22%
where the time goes in v2:
time: 326 us; the launch traced here: 324 us
  Pallas kernels  98.5 us (30%)
  waiting for transfers between devices  76 us (23%)
  starting transfers between devices  57.9 us (18%)
  other arithmetic  32.1 us (10%)
  local copies, waits for them, and re-layouts  22.7 us (7%)
  matrix products  22.4 us (7%)
  between operations  13.9 us (4%)
    ppermute x26, waiting for transfers between devices, swap_rows(): lax.ppermute(value, 'row', [(row, row ^ distance) for row in range(count)])  52.2 us
    ppermute x26, starting transfers between devices, swap_rows(): lax.ppermute(value, 'row', [(row, row ^ distance) for row in range(count)])  29.2 us
    pallas_call x1, Pallas kernels, finish(): call(finish_kernel, (rows // block,), [pl.BlockSpec((block, cols), lambda...  26.4 us
    pallas_call x2, Pallas kernels, image(): call(image_kernel, (rows // block,), [pl.BlockSpec((block, cols), lambda...  26.2 us
    pallas_call x2, Pallas kernels, project(): call(project_kernel, (cols // block,), [pl.BlockSpec((width, rows), lambd...  25.2 us
    dot_general x9, matrix products, small(): lax.dot_general(one, two, (((one_dim,), (two_dim,)), ((), ())), precision...  22.4 us
    pallas_call x1, Pallas kernels, update(): call(update_kernel, (rows // block,), [pl.BlockSpec((block, cols), lambda...  20.8 us
    ppermute x4, starting transfers between devices, send_along(): lax.ppermute(value, 'col', [(2 * (chip - step) + core, 2 * chip + core) f...  12.7 us
  transfers between devices with their start and end apart: 45, of which 17 were waited for; matrix products, arithmetic and copies ran while one was open for 21% of the time, Pallas kernels for 22%

profile of v2, /device:TPU:8, one launch (start us, length us, event | category | flops | bytes accessed | tf_op | source)
XLA Modules:
  0.0 324.2 jit_solution(8483632254086941851)
XLA Ops:
  7.6 3.5 %collective-permute-start.22 = (f32[2,32,3072]{2,1,0:T(8,128)}, f32[2,32,3072]{2,1,0:T(8,128)}, u32[]{:S(2)}, u32[]{:S(2)}) collective-permute-start(f32[2,32,3072]{2,1,0:T(8,128)} %bitcast.152), channel_id=1, source_target_pairs={{0,2},{1,3},{2,4},{3,5},{4,6},{5,7},{8,10},{9,11},{10,12},{11,13},... | collective-permute-start | bytes 2359304 | tf_op jit(solution)/shard_map/ppermute | solution.py:223
  11.1 3.2 %collective-permute-start.21 = (f32[2,32,3072]{2,1,0:T(8,128)}, f32[2,32,3072]{2,1,0:T(8,128)}, u32[]{:S(2)}, u32[]{:S(2)}) collective-permute-start(f32[2,32,3072]{2,1,0:T(8,128)} %bitcast.153), channel_id=1, source_target_pairs={{2,0},{3,1},{4,2},{5,3},{6,4},{7,5},{10,8},{11,9},{12,10},{13,11},... | collective-permute-start | bytes 2359304 | tf_op jit(solution)/shard_map/ppermute | solution.py:223
  15.7 2.5 collective-permute-start.25
  19.3 5.2 %collective-permute-done.25 = f32[2,16,1536]{2,1,0:T(8,128)S(1)} collective-permute-done((f32[2,16,1536]{2,1,0:T(8,128)S(1)}, f32[2,16,1536]{2,1,0:T(8,128)S(1)}, u32[]{:S(2)}, u32[]{:S(2)}) %collective-permute-start.25) | collective-permute-done | bytes 196640 | tf_op jit(solution)/shard_map/ppermute | solution.py:184
  24.5 3.1 collective-permute-done.24
  27.7 2.0 collective-permute-done.22
  29.8 3.2 collective-permute-done.21
  33.0 1.6 fusion.40
  35.0 1.6 collective-permute-start.29
  36.6 2.1 collective-permute-start.28
  38.9 1.4 collective-permute-start.35
  40.3 4.5 %collective-permute-done.29 = f32[16,1536]{1,0:T(8,128)S(1)} collective-permute-done((f32[16,1536]{1,0:T(8,128)S(1)}, f32[16,1536]{1,0:T(8,128)S(1)}, u32[]{:S(2)}, u32[]{:S(2)}) %collective-permute-start.29) | collective-permute-done | bytes 98336 | tf_op jit(solution)/shard_map/ppermute | solution.py:179
  44.8 4.8 %collective-permute-done.28 = f32[16,1536]{1,0:T(8,128)S(1)} collective-permute-done((f32[16,1536]{1,0:T(8,128)S(1)}, f32[16,1536]{1,0:T(8,128)S(1)}, u32[]{:S(2)}, u32[]{:S(2)}) %collective-permute-start.28) | collective-permute-done | bytes 98336 | tf_op jit(solution)/shard_map/ppermute | solution.py:179
  49.6 3.0 collective-permute-start.33
  53.3 2.5 collective-permute-start.32
  56.4 2.1 broadcast_select_fusion.15
  59.2 12.0 %shard_map.38 = f32[256,1536]{1,0:T(8,128)S(1)} custom-call(f32[256,3072]{1,0:T(8,128)S(1)} %bitcast.145, f32[3072,1536]{1,0:T(8,128)} %window_ref.5), custom_call_target="tpu_custom_call" | custom-call | flops 1 | bytes 1 | tf_op jit(solution)/shard_map/pallas_call | solution.py:67
  71.3 1.9 collective-permute-start.39
  73.2 4.0 %collective-permute-start.40 = (f32[2,32,3072]{2,1,0:T(8,128)}, f32[2,32,3072]{2,1,0:T(8,128)S(1)}, u32[]{:S(2)}, u32[]{:S(2)}) collective-permute-start(f32[2,32,3072]{2,1,0:T(8,128)} %collective-permute-done.22), channel_id=1, source_target_pairs={{2,4},{3,5},{4,6},{5,7},{10,12},{11,13},{12,14},{13,15},{18,20},{1... | collective-permute-start | bytes 2359304 | tf_op jit(solution)/shard_map/ppermute | solution.py:223
  77.3 2.5 collective-permute-start.38
  82.1 13.1 %shard_map.39 = f32[3072,256]{1,0:T(8,128)} custom-call(f32[3072,1536]{1,0:T(8,128)} %window_ref.5, f32[256,1536]{1,0:T(8,128)S(1)} %bitcast.143), custom_call_target="tpu_custom_call" | custom-call | flops 1 | bytes 1 | tf_op jit(solution)/shard_map/pallas_call | solution.py:98
  96.2 2.2 collective-permute-start.41
  98.4 1.5 collective-permute-start.42
  99.9 1.5 collective-permute-start.43
  101.6 13.1 %shard_map.40 = f32[3072,256]{1,0:T(8,128)} custom-call(f32[3072,1536]{1,0:T(8,128)} %window_ref.5, f32[256,1536]{1,0:T(8,128)S(1)} %bitcast.141), custom_call_target="tpu_custom_call" | custom-call | flops 1 | bytes 1 | tf_op jit(solution)/shard_map/pallas_call | solution.py:98
  114.7 1.8 pad_maximum_fusion.14
  116.6 2.8 select_select_fusion.3
  119.5 2.9 pad_maximum_fusion.16
  122.3 166.8 %conditional.2 = (f32[3072,1536]{1,0:T(8,128)}, f32[256,3072]{1,0:T(8,128)}, bf16[512,512]{1,0:T(8,128)(2,1)}, bf16[512,512]{1,0:T(8,128)(2,1)}, bf16[512,1536]{1,0:T(8,128)(2,1)}, /*index=5*/bf16[512,1536]{1,0:T(8,128)(2,1)}) conditional(s32[]{:T(128)} %convert_element_type.24, () %tuple.40, (pred[]{:T(512)}, f32[2,2,32,3072]{3,2,0,1:T(8,128)}, ...), branch_computations={%region_0.1_spmd, %region_1.4_spmd} | conditional | flops 8275492864 | bytes 207491728 | solution.py:370
  129.1 2.1 fusion.27
  131.2 2.0 pad_maximum_fusion
  133.2 13.1 %branch_1_fun.3 = f32[256,1536]{1,0:T(8,128)S(1)} custom-call(f32[256,3072]{1,0:T(8,128)} %bitcast.4.vectors_ref, f32[3072,1536]{1,0:T(8,128)} %get-tuple-element.87.window_ref), custom_call_target="tpu_custom_call" | custom-call | flops 1 | bytes 1 | tf_op jit(solution)/shard_map/cond/branch_1_fun/pallas_call | solution.py:67
  147.4 1.3 collective-permute-start.4
  148.7 3.5 %fusion.48 = f32[256,256]{1,0:T(8,128)S(1)} fusion(f32[256,3072]{1,0:T(8,128)S(1)} %get-tuple-element.99, f32[256,3072]{1,0:T(8,128)} %bitcast.4.vectors_ref), kind=kOutput, calls=%fused_computation.167 | convolution fusion | flops 1207959552 | bytes 6553600 | tf_op jit(solution)/shard_map/cond/branch_1_fun/dot_general | solution.py:27
  152.2 3.4 %fusion.33 = (f32[128,128]{0,1:T(8,128)}, f32[128,128]{0,1:T(8,128)}) fusion(f32[256,256]{1,0:T(8,128)S(1)} %fusion.48, pred[]{:T(512)} %get-tuple-element.101, f32[256,3072]{1,0:T(8,128)} %bitcast.4.vectors_ref), kind=kOutput, calls=%fused_computation.88 | convolution fusion | flops 302022656 | bytes 3342337 | tf_op jit(solution)/shard_map/cond/branch_1_fun/dot_general | solution.py:27
  157.0 1.6 copy.15
  159.7 1.6 broadcast_select_fusion.14
  163.5 7.3 %collective-permute-done.6 = f32[64,1536]{1,0:T(8,128)S(1)} collective-permute-done((f32[64,1536]{1,0:T(8,128)}, f32[64,1536]{1,0:T(8,128)S(1)}, u32[]{:S(2)}, u32[]{:S(2)}) %collective-permute-start.6) | collective-permute-done | bytes 393248 | tf_op jit(solution)/shard_map/cond/branch_1_fun/ppermute | solution.py:184
  172.9 3.7 %collective-permute-done.7 = f32[32,1536]{1,0:T(8,128)S(1)} collective-permute-done((f32[32,1536]{1,0:T(8,128)S(1)}, f32[32,1536]{1,0:T(8,128)S(1)}, u32[]{:S(2)}, u32[]{:S(2)}) %collective-permute-start.7) | collective-permute-done | bytes 196640 | tf_op jit(solution)/shard_map/cond/branch_1_fun/ppermute | solution.py:184
  176.6 1.3 broadcast_select_fusion.10
  179.3 1.8 fusion.18
  182.1 1.3 collective-permute-start.10
  183.3 2.5 collective-permute-done.9
  185.9 12.4 %collective-permute-done.10 = f32[2,32,1536]{2,1,0:T(8,128)S(1)} collective-permute-done((f32[2,32,1536]{2,1,0:T(8,128)S(1)}, f32[2,32,1536]{2,1,0:T(8,128)S(1)}, u32[]{:S(2)}, u32[]{:S(2)}) %collective-permute-start.10) | collective-permute-done | bytes 393248 | tf_op jit(solution)/shard_map/cond/branch_1_fun/ppermute | solution.py:184
  202.6 2.0 copy.14
  207.0 1.5 collective-permute-start.12
  208.5 1.4 collective-permute-start.14
  211.0 8.9 %collective-permute-done.13 = f32[2,64,1536]{2,1,0:T(8,128)} collective-permute-done((f32[2,64,1536]{2,1,0:T(8,128)}, f32[2,64,1536]{2,1,0:T(8,128)}, u32[]{:S(2)}, u32[]{:S(2)}) %collective-permute-start.13) | collective-permute-done | bytes 786464 | tf_op jit(solution)/shard_map/cond/branch_1_fun/ppermute | solution.py:184
  219.9 1.5 broadcast_select_fusion.4
  221.5 5.7 %collective-permute-done.14 = f32[2,64,1536]{2,1,0:T(8,128)S(1)} collective-permute-done((f32[2,64,1536]{2,1,0:T(8,128)S(1)}, f32[2,64,1536]{2,1,0:T(8,128)S(1)}, u32[]{:S(2)}, u32[]{:S(2)}) %collective-permute-start.14) | collective-permute-done | bytes 786464 | tf_op jit(solution)/shard_map/cond/branch_1_fun/ppermute | solution.py:184
  229.2 1.9 collective-permute-start.16
  232.8 2.8 fusion
  235.7 9.2 %collective-permute-done.16 = f32[128,512]{1,0:T(8,128)S(1)} collective-permute-done((f32[128,512]{1,0:T(8,128)S(1)}, f32[128,512]{1,0:T(8,128)S(1)}, u32[]{:S(2)}, u32[]{:S(2)}) %collective-permute-start.16) | collective-permute-done | bytes 262176 | tf_op jit(solution)/shard_map/cond/branch_1_fun/ppermute | solution.py:347
  244.9 28.7 %conditional = (f32[128,512]{1,0:T(8,128)}, f32[3072,1536]{1,0:T(8,128)}, f32[64,512]{1,0:T(8,128)}, f32[64,512]{1,0:T(8,128)}, f32[1,2,32,512]{3,2,1,0:T(8,128)S(1)}, /*index=5*/f32[1,2,32,512]{3,2,1,0:T(8,128)S(1)}) conditional(s32[]{:T(128)} %convert_element_type.16, () %tuple.21, (f32[3072,1536]{1,0:T(8,128)}, f32[256,3072]{1,0:T(8,128)S(1)}, ...), branch_computations={%region_2.2_spmd, %region_3.3_spmd} | conditional | flops 131093 | bytes 19660872 | solution.py:370
  245.6 2.0 collective-permute-start
  247.6 20.8 %branch_1_fun.2 = f32[3072,1536]{1,0:T(8,128)} custom-call(f32[3072,1536]{1,0:T(8,128)} %get-tuple-element.78.window_ref, f32[256,3072]{1,0:T(8,128)S(1)} %get-tuple-element.79.near_ref, f32[256,3072]{1,0:T(8,128)} %get-tuple-element.80.far_ref, bf16[512,1536]{1,0:T(8,128)(2,1)S(1)} %get-tuple-element.81.high_ref, ...), custom_call_target="tpu_custom_call" | custom-call | flops 1 | bytes 1 | tf_op jit(solution)/shard_map/cond/branch_1_fun/cond/branch_1_fun/pallas_call | solution.py:124
  268.4 1.7 broadcast_select_fusion
  270.1 1.7 fusion.41
  273.6 2.0 collective-permute-start.19
  277.1 6.6 %fusion.1 = (bf16[512,1536]{1,0:T(8,128)(2,1)}, bf16[512,1536]{1,0:T(8,128)(2,1)}) fusion(f32[512,1536]{1,0:T(8,128)} %get-tuple-element.107, f32[256,256]{0,1:T(8,128)} %copy-done.14, f32[256,256]{0,1:T(8,128)S(1)} %fusion.8, f32[256,256]{0,1:T(8,128)} %copy-done.13), kind=kOutput, calls=%fused_computation.6 | convolution fusion | flops 2420113408 | bytes 7077888 | tf_op jit(solution)/shard_map/cond/branch_1_fun/dot_general | solution.py:27
  283.8 1.9 collective-permute-done.18
  287.0 2.1 fusion.9
  289.1 1.9 copy-done
  291.0 26.4 %shard_map.41 = f32[3072,1536]{1,0:T(8,128)} custom-call(f32[3072,1536]{1,0:T(8,128)} %get-tuple-element.198.window_ref, f32[256,3072]{1,0:T(8,128)S(1)} %bitcast.147, f32[256,3072]{1,0:T(8,128)} %get-tuple-element.199.far_ref, bf16[512,512]{1,0:T(8,128)(2,1)} %get-tuple-element.200.middle_high, ...), custom_call_target="tpu_custom_call", output_to_operand_aliasing={{}: (0, {})} | custom-call | flops 1 | bytes 1 | tf_op jit(solution)/shard_map/pallas_call | solution.py:153
  (210 shorter events, 43.0 us)
Async XLA Ops:
  6.5 282.5 %all-reduce.4.cloned.1.call-start = ((), (), s32[]{:S(2)}) async-start(), calls=%async_computation | async-start | bytes 12582912 | tf_op jit(solution)/shard_map/psum | solution.py:390
  7.6 6.9 %collective-permute-start.20 = (f32[2,32,1536]{2,1,0:T(8,128)S(1)}, f32[2,32,1536]{2,1,0:T(8,128)S(1)}, u32[]{:S(2)}, u32[]{:S(2)}) collective-permute-start(f32[2,32,1536]{2,1,0:T(8,128)S(1)} %dynamic-slice_bitcast_fusion), channel_id=1, source_target_pairs={{0,1},{1,0},{2,3},{3,2},{4,5},{5,4},{6,7},{7,6},{8,9},{9,8},{10,11... | collective-permute-start | bytes 1179656 | tf_op jit(solution)/shard_map/ppermute | solution.py:174
  7.6 22.1 %collective-permute-start.22 = (f32[2,32,3072]{2,1,0:T(8,128)}, f32[2,32,3072]{2,1,0:T(8,128)}, u32[]{:S(2)}, u32[]{:S(2)}) collective-permute-start(f32[2,32,3072]{2,1,0:T(8,128)} %bitcast.152), channel_id=1, source_target_pairs={{0,2},{1,3},{2,4},{3,5},{4,6},{5,7},{8,10},{9,11},{10,12},{11,13},... | collective-permute-start | bytes 2359304 | tf_op jit(solution)/shard_map/ppermute | solution.py:223
  11.1 21.9 %collective-permute-start.21 = (f32[2,32,3072]{2,1,0:T(8,128)}, f32[2,32,3072]{2,1,0:T(8,128)}, u32[]{:S(2)}, u32[]{:S(2)}) collective-permute-start(f32[2,32,3072]{2,1,0:T(8,128)} %bitcast.153), channel_id=1, source_target_pairs={{2,0},{3,1},{4,2},{5,3},{6,4},{7,5},{10,8},{11,9},{12,10},{13,11},... | collective-permute-start | bytes 2359304 | tf_op jit(solution)/shard_map/ppermute | solution.py:223
  15.6 17.4 %copy-start.5 = (f32[2,3072,32]{1,2,0:T(8,128)S(1)}, f32[2,3072,32]{1,2,0:T(8,128)}, u32[]{:S(2)}) copy-start(f32[2,3072,32]{1,2,0:T(8,128)} %param.8) | copy-start | bytes 2359300
  15.7 8.8 %collective-permute-start.25 = (f32[2,16,1536]{2,1,0:T(8,128)S(1)}, f32[2,16,1536]{2,1,0:T(8,128)S(1)}, u32[]{:S(2)}, u32[]{:S(2)}) collective-permute-start(f32[2,16,1536]{2,1,0:T(8,128)S(1)} %get-tuple-element.294), channel_id=1, source_target_pairs={{0,24},{8,16},{16,8},{24,0},{1,25},{9,17},{17,9},{25,1},{2,26},{10... | collective-permute-start | bytes 589832 | tf_op jit(solution)/shard_map/ppermute | solution.py:184
  18.2 9.4 %collective-permute-start.24 = (f32[2,16,1536]{2,1,0:T(8,128)S(1)}, f32[2,16,1536]{2,1,0:T(8,128)S(1)}, u32[]{:S(2)}, u32[]{:S(2)}) collective-permute-start(f32[2,16,1536]{2,1,0:T(8,128)S(1)} %get-tuple-element.295), channel_id=1, source_target_pairs={{0,16},{8,24},{16,0},{24,8},{1,17},{9,25},{17,1},{25,9},{2,18},{10... | collective-permute-start | bytes 589832 | tf_op jit(solution)/shard_map/ppermute | solution.py:184
  18.8 9.0 %collective-permute-start.23 = (f32[2,16,1536]{2,1,0:T(8,128)S(1)}, f32[2,16,1536]{2,1,0:T(8,128)S(1)}, u32[]{:S(2)}, u32[]{:S(2)}) collective-permute-start(f32[2,16,1536]{2,1,0:T(8,128)S(1)} %get-tuple-element.296), channel_id=1, source_target_pairs={{0,8},{8,0},{16,24},{24,16},{1,9},{9,1},{17,25},{25,17},{2,10},{10... | collective-permute-start | bytes 589832 | tf_op jit(solution)/shard_map/ppermute | solution.py:184
  34.7 17.9 %collective-permute-start.26 = (f32[2,2,32,3072]{3,2,0,1:T(8,128)S(1)}, f32[2,2,32,3072]{3,2,0,1:T(8,128)S(1)}, u32[]{:S(2)}, u32[]{:S(2)}) collective-permute-start(f32[2,2,32,3072]{3,2,0,1:T(8,128)S(1)} %pad_maximum_fusion.15), channel_id=1, source_target_pairs={{0,1},{1,0},{2,3},{3,2},{4,5},{5,4},{6,7},{7,6},{8,9},{9,8},{10,11... | collective-permute-start | bytes 4718600 | tf_op jit(solution)/shard_map/ppermute | solution.py:174
  35.0 9.9 %collective-permute-start.29 = (f32[16,1536]{1,0:T(8,128)S(1)}, f32[16,1536]{1,0:T(8,128)S(1)}, u32[]{:S(2)}, u32[]{:S(2)}) collective-permute-start(f32[16,1536]{1,0:T(8,128)S(1)} %get-tuple-element.302), channel_id=1, source_target_pairs={{0,6},{1,7},{2,4},{3,5},{4,2},{5,3},{6,0},{7,1},{8,14},{9,15},{10,... | collective-permute-start | bytes 294920 | tf_op jit(solution)/shard_map/ppermute | solution.py:179
  36.6 13.0 %collective-permute-start.28 = (f32[16,1536]{1,0:T(8,128)S(1)}, f32[16,1536]{1,0:T(8,128)S(1)}, u32[]{:S(2)}, u32[]{:S(2)}) collective-permute-start(f32[16,1536]{1,0:T(8,128)S(1)} %get-tuple-element.303), channel_id=1, source_target_pairs={{0,4},{1,5},{2,6},{3,7},{4,0},{5,1},{6,2},{7,3},{8,12},{9,13},{10,... | collective-permute-start | bytes 294920 | tf_op jit(solution)/shard_map/ppermute | solution.py:179
  38.7 13.9 %collective-permute-start.27 = (f32[16,1536]{1,0:T(8,128)S(1)}, f32[16,1536]{1,0:T(8,128)S(1)}, u32[]{:S(2)}, u32[]{:S(2)}) collective-permute-start(f32[16,1536]{1,0:T(8,128)S(1)} %get-tuple-element.304), channel_id=1, source_target_pairs={{0,2},{1,3},{2,0},{3,1},{4,6},{5,7},{6,4},{7,5},{8,10},{9,11},{10,... | collective-permute-start | bytes 294920 | tf_op jit(solution)/shard_map/ppermute | solution.py:179
  38.9 19.6 %collective-permute-start.35 = (f32[16,1536]{1,0:T(8,128)S(1)}, f32[16,1536]{1,0:T(8,128)S(1)}, u32[]{:S(2)}, u32[]{:S(2)}) collective-permute-start(f32[16,1536]{1,0:T(8,128)S(1)} %get-tuple-element.299), channel_id=1, source_target_pairs={{0,6},{1,7},{2,4},{3,5},{4,2},{5,3},{6,0},{7,1},{8,14},{9,15},{10,... | collective-permute-start | bytes 294920 | tf_op jit(solution)/shard_map/ppermute | solution.py:179
  44.8 26.4 %collective-permute-start.34 = (f32[16,1536]{1,0:T(8,128)S(1)}, f32[16,1536]{1,0:T(8,128)S(1)}, u32[]{:S(2)}, u32[]{:S(2)}) collective-permute-start(f32[16,1536]{1,0:T(8,128)S(1)} %get-tuple-element.300), channel_id=1, source_target_pairs={{0,4},{1,5},{2,6},{3,7},{4,0},{5,1},{6,2},{7,3},{8,12},{9,13},{10,... | collective-permute-start | bytes 294920 | tf_op jit(solution)/shard_map/ppermute | solution.py:179
  49.6 23.6 %collective-permute-start.33 = (f32[16,1536]{1,0:T(8,128)S(1)}, f32[16,1536]{1,0:T(8,128)S(1)}, u32[]{:S(2)}, u32[]{:S(2)}) collective-permute-start(f32[16,1536]{1,0:T(8,128)S(1)} %get-tuple-element.301), channel_id=1, source_target_pairs={{0,2},{1,3},{2,0},{3,1},{4,6},{5,7},{6,4},{7,5},{8,10},{9,11},{10,... | collective-permute-start | bytes 294920 | tf_op jit(solution)/shard_map/ppermute | solution.py:179
  53.3 5.9 %copy-start.1 = (f32[2,128,3072]{2,1,0:T(8,128)}, f32[2,128,3072]{2,1,0:T(8,128)S(1)}, u32[]{:S(2)}) copy-start(f32[2,128,3072]{2,1,0:T(8,128)S(1)} %pad_maximum_fusion.13) | copy-start | bytes 9437188
  53.3 23.9 %collective-permute-start.32 = (f32[4,16,1536]{2,1,0:T(8,128)S(1)}, f32[4,16,1536]{2,1,0:T(8,128)S(1)}, u32[]{:S(2)}, u32[]{:S(2)}) collective-permute-start(f32[4,16,1536]{2,1,0:T(8,128)S(1)} %bitcast_dynamic-update-slice_fusion.14), channel_id=1, source_target_pairs={{0,24},{8,16},{16,8},{24,0},{1,25},{9,17},{17,9},{25,1},{2,26},{10... | collective-permute-start | bytes 1179656 | tf_op jit(solution)/shard_map/ppermute | solution.py:184
  55.8 21.4 %collective-permute-start.31 = (f32[4,16,1536]{2,1,0:T(8,128)S(1)}, f32[4,16,1536]{2,1,0:T(8,128)S(1)}, u32[]{:S(2)}, u32[]{:S(2)}) collective-permute-start(f32[4,16,1536]{2,1,0:T(8,128)S(1)} %bitcast_dynamic-update-slice_fusion.14), channel_id=1, source_target_pairs={{0,16},{8,24},{16,0},{24,8},{1,17},{9,25},{17,1},{25,9},{2,18},{10... | collective-permute-start | bytes 1179656 | tf_op jit(solution)/shard_map/ppermute | solution.py:184
  58.5 18.8 %collective-permute-start.30 = (f32[4,16,1536]{2,1,0:T(8,128)S(1)}, f32[4,16,1536]{2,1,0:T(8,128)S(1)}, u32[]{:S(2)}, u32[]{:S(2)}) collective-permute-start(f32[4,16,1536]{2,1,0:T(8,128)S(1)} %bitcast_dynamic-update-slice_fusion.14), channel_id=1, source_target_pairs={{0,8},{8,0},{16,24},{24,16},{1,9},{9,1},{17,25},{25,17},{2,10},{10... | collective-permute-start | bytes 1179656 | tf_op jit(solution)/shard_map/ppermute | solution.py:184
  71.3 24.9 %collective-permute-start.39 = (f32[2,32,3072]{2,1,0:T(8,128)}, f32[2,32,3072]{2,1,0:T(8,128)S(1)}, u32[]{:S(2)}, u32[]{:S(2)}) collective-permute-start(f32[2,32,3072]{2,1,0:T(8,128)} %collective-permute-done.21), channel_id=1, source_target_pairs={{2,0},{3,1},{4,2},{5,3},{10,8},{11,9},{12,10},{13,11},{18,16},{19,... | collective-permute-start | bytes 2359304 | tf_op jit(solution)/shard_map/ppermute | solution.py:223
  73.2 25.2 %collective-permute-start.40 = (f32[2,32,3072]{2,1,0:T(8,128)}, f32[2,32,3072]{2,1,0:T(8,128)S(1)}, u32[]{:S(2)}, u32[]{:S(2)}) collective-permute-start(f32[2,32,3072]{2,1,0:T(8,128)} %collective-permute-done.22), channel_id=1, source_target_pairs={{2,4},{3,5},{4,6},{5,7},{10,12},{11,13},{12,14},{13,15},{18,20},{1... | collective-permute-start | bytes 2359304 | tf_op jit(solution)/shard_map/ppermute | solution.py:223
  77.3 22.6 %collective-permute-start.38 = (f32[4,16,1536]{2,1,0:T(8,128)S(1)}, f32[4,16,1536]{2,1,0:T(8,128)S(1)}, u32[]{:S(2)}, u32[]{:S(2)}) collective-permute-start(f32[4,16,1536]{2,1,0:T(8,128)S(1)} %bitcast_dynamic-update-slice_fusion.11), channel_id=1, source_target_pairs={{0,24},{8,16},{16,8},{24,0},{1,25},{9,17},{17,9},{25,1},{2,26},{10... | collective-permute-start | bytes 1179656 | tf_op jit(solution)/shard_map/ppermute | solution.py:184
  79.9 21.6 %collective-permute-start.37 = (f32[4,16,1536]{2,1,0:T(8,128)S(1)}, f32[4,16,1536]{2,1,0:T(8,128)S(1)}, u32[]{:S(2)}, u32[]{:S(2)}) collective-permute-start(f32[4,16,1536]{2,1,0:T(8,128)S(1)} %bitcast_dynamic-update-slice_fusion.11), channel_id=1, source_target_pairs={{0,16},{8,24},{16,0},{24,8},{1,17},{9,25},{17,1},{25,9},{2,18},{10... | collective-permute-start | bytes 1179656 | tf_op jit(solution)/shard_map/ppermute | solution.py:184
  80.4 21.1 %collective-permute-start.36 = (f32[4,16,1536]{2,1,0:T(8,128)S(1)}, f32[4,16,1536]{2,1,0:T(8,128)S(1)}, u32[]{:S(2)}, u32[]{:S(2)}) collective-permute-start(f32[4,16,1536]{2,1,0:T(8,128)S(1)} %bitcast_dynamic-update-slice_fusion.11), channel_id=1, source_target_pairs={{0,8},{8,0},{16,24},{24,16},{1,9},{9,1},{17,25},{25,17},{2,10},{10... | collective-permute-start | bytes 1179656 | tf_op jit(solution)/shard_map/ppermute | solution.py:184
  81.0 14.1 %copy-start.7 = (f32[128,1536]{1,0:T(8,128)}, f32[128,1536]{1,0:T(8,128)S(1)}, u32[]{:S(2)}) copy-start(f32[128,1536]{1,0:T(8,128)S(1)} %get-tuple-element.286) | copy-start | bytes 2359300
  96.2 5.4 %copy-start.25 = (f32[2,32,3072]{2,1,0:T(8,128)}, f32[2,32,3072]{2,1,0:T(8,128)S(1)}, u32[]{:S(2)}) copy-start(f32[2,32,3072]{2,1,0:T(8,128)S(1)} %collective-permute-done.39) | copy-start | bytes 2359300
  96.2 18.5 %collective-permute-start.41 = (f32[2,32,3072]{2,1,0:T(8,128)}, f32[2,32,3072]{2,1,0:T(8,128)}, u32[]{:S(2)}, u32[]{:S(2)}) collective-permute-start(f32[2,32,3072]{2,1,0:T(8,128)} %broadcast_select_fusion.15), channel_id=1, source_target_pairs={{4,0},{5,1},{2,6},{3,7},{12,8},{13,9},{10,14},{11,15},{20,16},{21,... | collective-permute-start | bytes 2359304 | tf_op jit(solution)/shard_map/ppermute | solution.py:314
  98.4 3.2 copy-start.27
  98.4 16.3 %collective-permute-start.42 = (f32[64,1536]{1,0:T(8,128)}, f32[64,1536]{1,0:T(8,128)S(1)}, u32[]{:S(2)}, u32[]{:S(2)}) collective-permute-start(f32[64,1536]{1,0:T(8,128)} %constant_dynamic-slice_fusion.6), channel_id=1, source_target_pairs={{0,8},{8,0},{16,24},{24,16},{1,9},{9,1},{17,25},{25,17},{2,10},{10... | collective-permute-start | bytes 1179656 | tf_op jit(solution)/shard_map/ppermute | solution.py:184
  99.9 14.8 %collective-permute-start.43 = (f32[64,1536]{1,0:T(8,128)}, f32[64,1536]{1,0:T(8,128)}, u32[]{:S(2)}, u32[]{:S(2)}) collective-permute-start(f32[64,1536]{1,0:T(8,128)} %constant_dynamic-slice_fusion.7), channel_id=1, source_target_pairs={{0,16},{8,24},{16,0},{24,8},{1,17},{9,25},{17,1},{25,9},{2,18},{10... | collective-permute-start | bytes 1179656 | tf_op jit(solution)/shard_map/ppermute | solution.py:184
  114.7 1.9 copy-start.28
  119.5 2.9 copy-start.2
  122.3 6.8 %collective-permute-start.1 = (f32[2,2,32,3072]{3,2,0,1:T(8,128)}, f32[2,2,32,3072]{3,2,0,1:T(8,128)}, u32[]{:S(2)}, u32[]{:S(2)}) collective-permute-start(f32[2,2,32,3072]{3,2,0,1:T(8,128)} %get-tuple-element.89), channel_id=1, source_target_pairs={{0,1},{1,0},{2,3},{3,2},{4,5},{5,4},{6,7},{7,6},{8,9},{9,8},{10,11... | collective-permute-start | bytes 4718600 | tf_op jit(solution)/shard_map/cond/branch_1_fun/ppermute | solution.py:174
  124.9 21.5 %collective-permute-start.3 = (f32[32,1536]{1,0:T(8,128)}, f32[32,1536]{1,0:T(8,128)}, u32[]{:S(2)}, u32[]{:S(2)}) collective-permute-start(f32[32,1536]{1,0:T(8,128)} %constant_dynamic-slice_fusion.4), channel_id=1, source_target_pairs={{0,8},{8,0},{16,24},{24,16},{1,9},{9,1},{17,25},{25,17},{2,10},{10... | collective-permute-start | bytes 589832 | tf_op jit(solution)/shard_map/cond/branch_1_fun/ppermute | solution.py:184
  128.4 18.0 %collective-permute-start.2 = (f32[32,1536]{1,0:T(8,128)}, f32[32,1536]{1,0:T(8,128)}, u32[]{:S(2)}, u32[]{:S(2)}) collective-permute-start(f32[32,1536]{1,0:T(8,128)} %constant_dynamic-slice_fusion.5), channel_id=1, source_target_pairs={{0,16},{8,24},{16,0},{24,8},{1,17},{9,25},{17,1},{25,9},{2,18},{10... | collective-permute-start | bytes 589832 | tf_op jit(solution)/shard_map/cond/branch_1_fun/ppermute | solution.py:184
  146.5 5.7 %copy-start.10 = (f32[128,1536]{1,0:T(8,128)}, f32[128,1536]{1,0:T(8,128)S(1)}, u32[]{:S(2)}) copy-start(f32[128,1536]{1,0:T(8,128)S(1)} %get-tuple-element.245) | copy-start | bytes 2359300 | tf_op jit(solution)/shard_map/cond
  146.5 9.0 %copy-start.8 = (f32[128,1536]{1,0:T(8,128)}, f32[128,1536]{1,0:T(8,128)S(1)}, u32[]{:S(2)}) copy-start(f32[128,1536]{1,0:T(8,128)S(1)} %get-tuple-element.244) | copy-start | bytes 2359300 | tf_op jit(solution)/shard_map/cond
  147.4 14.0 %collective-permute-start.4 = (f32[64,1536]{1,0:T(8,128)}, f32[64,1536]{1,0:T(8,128)}, u32[]{:S(2)}, u32[]{:S(2)}) collective-permute-start(f32[64,1536]{1,0:T(8,128)} %constant_dynamic-slice_fusion.3), channel_id=1, source_target_pairs={{0,8},{8,0},{16,24},{24,16},{1,9},{9,1},{17,25},{25,17},{2,10},{10... | collective-permute-start | bytes 1179656 | tf_op jit(solution)/shard_map/cond/branch_1_fun/ppermute | solution.py:184
  158.5 2.9 copy-start.11
  158.5 12.3 %collective-permute-start.6 = (f32[64,1536]{1,0:T(8,128)}, f32[64,1536]{1,0:T(8,128)S(1)}, u32[]{:S(2)}, u32[]{:S(2)}) collective-permute-start(f32[64,1536]{1,0:T(8,128)} %constant_dynamic-slice_fusion.1), channel_id=1, source_target_pairs={{0,16},{8,24},{16,0},{24,8},{1,17},{9,25},{17,1},{25,9},{2,18},{10... | collective-permute-start | bytes 1179656 | tf_op jit(solution)/shard_map/cond/branch_1_fun/ppermute | solution.py:184
  161.4 9.4 %copy-start.9 = (f32[128,1536]{1,0:T(8,128)S(1)}, f32[128,1536]{1,0:T(8,128)}, u32[]{:S(2)}) copy-start(f32[128,1536]{1,0:T(8,128)} %copy-done.8) | copy-start | bytes 2359300 | tf_op jit(solution)/shard_map/cond
  161.4 10.3 %copy-start.31 = (f32[128,128]{0,1:T(8,128)S(1)}, f32[128,128]{0,1:T(8,128)}, u32[]{:S(2)}) copy-start(f32[128,128]{0,1:T(8,128)} %get-tuple-element.264) | copy-start | bytes 196612 | tf_op jit(solution)/shard_map/cond
  161.4 10.3 %copy-start.32 = (f32[128,128]{0,1:T(8,128)S(1)}, f32[128,128]{0,1:T(8,128)}, u32[]{:S(2)}) copy-start(f32[128,128]{0,1:T(8,128)} %get-tuple-element.265) | copy-start | bytes 196612 | tf_op jit(solution)/shard_map/cond
  162.6 14.1 %copy-start.16 = (f32[64,1536]{1,0:T(8,128)S(1)}, f32[64,1536]{1,0:T(8,128)}, u32[]{:S(2)}) copy-start(f32[64,1536]{1,0:T(8,128)} %copy-done.15) | copy-start | bytes 1179652 | tf_op jit(solution)/shard_map/cond
  162.6 10.3 %collective-permute-start.5 = (f32[32,1536]{1,0:T(8,128)S(1)}, f32[32,1536]{1,0:T(8,128)S(1)}, u32[]{:S(2)}, u32[]{:S(2)}) collective-permute-start(f32[32,1536]{1,0:T(8,128)S(1)} %constant_dynamic-slice_fusion.2), channel_id=1, source_target_pairs={{0,16},{8,24},{16,0},{24,8},{1,17},{9,25},{17,1},{25,9},{2,18},{10... | collective-permute-start | bytes 589832 | tf_op jit(solution)/shard_map/cond/branch_1_fun/ppermute | solution.py:184
  170.9 5.7 %collective-permute-start.7 = (f32[32,1536]{1,0:T(8,128)S(1)}, f32[32,1536]{1,0:T(8,128)S(1)}, u32[]{:S(2)}, u32[]{:S(2)}) collective-permute-start(f32[32,1536]{1,0:T(8,128)S(1)} %constant_dynamic-slice_fusion), channel_id=1, source_target_pairs={{0,8},{8,0},{16,24},{24,16},{1,9},{9,1},{17,25},{25,17},{2,10},{10... | collective-permute-start | bytes 589832 | tf_op jit(solution)/shard_map/cond/branch_1_fun/ppermute | solution.py:184
  176.6 2.7 copy-start.3
  178.0 7.8 %collective-permute-start.9 = (f32[2,32,1536]{2,1,0:T(8,128)S(1)}, f32[2,32,1536]{2,1,0:T(8,128)S(1)}, u32[]{:S(2)}, u32[]{:S(2)}) collective-permute-start(f32[2,32,1536]{2,1,0:T(8,128)S(1)} %pad_maximum_fusion.7), channel_id=1, source_target_pairs={{0,16},{8,24},{16,0},{24,8},{1,17},{9,25},{17,1},{25,9},{2,18},{10... | collective-permute-start | bytes 1179656 | tf_op jit(solution)/shard_map/cond/branch_1_fun/ppermute | solution.py:184
  181.1 19.2 %collective-permute-start.8 = (f32[128,512]{1,0:T(8,128)S(1)}, f32[128,512]{1,0:T(8,128)S(1)}, u32[]{:S(2)}, u32[]{:S(2)}) collective-permute-start(f32[128,512]{1,0:T(8,128)S(1)} %fusion.18), channel_id=1, source_target_pairs={{0,1},{1,0},{2,3},{3,2},{4,5},{5,4},{6,7},{7,6},{8,9},{9,8},{10,11... | collective-permute-start | bytes 786440 | tf_op jit(solution)/shard_map/cond/branch_1_fun/ppermute | solution.py:174
  181.2 19.2 %collective-permute-start.11 = (f32[256,256]{0,1:T(8,128)S(1)}, f32[256,256]{0,1:T(8,128)S(1)}, u32[]{:S(2)}, u32[]{:S(2)}) collective-permute-start(f32[256,256]{0,1:T(8,128)S(1)} %pad_maximum_fusion.9), channel_id=1, source_target_pairs={{0,8},{8,0},{16,24},{24,16},{1,9},{9,1},{17,25},{25,17},{2,10},{10... | collective-permute-start | bytes 786440 | tf_op jit(solution)/shard_map/cond/branch_1_fun/ppermute | solution.py:184
  182.1 16.2 %collective-permute-start.10 = (f32[2,32,1536]{2,1,0:T(8,128)S(1)}, f32[2,32,1536]{2,1,0:T(8,128)S(1)}, u32[]{:S(2)}, u32[]{:S(2)}) collective-permute-start(f32[2,32,1536]{2,1,0:T(8,128)S(1)} %pad_maximum_fusion.8), channel_id=1, source_target_pairs={{0,8},{8,0},{16,24},{24,16},{1,9},{9,1},{17,25},{25,17},{2,10},{10... | collective-permute-start | bytes 1179656 | tf_op jit(solution)/shard_map/cond/branch_1_fun/ppermute | solution.py:184
  200.3 19.6 %collective-permute-start.13 = (f32[2,64,1536]{2,1,0:T(8,128)}, f32[2,64,1536]{2,1,0:T(8,128)}, u32[]{:S(2)}, u32[]{:S(2)}) collective-permute-start(f32[2,64,1536]{2,1,0:T(8,128)} %pad_maximum_fusion.5), channel_id=1, source_target_pairs={{0,8},{8,0},{16,24},{24,16},{1,9},{9,1},{17,25},{25,17},{2,10},{10... | collective-permute-start | bytes 2359304 | tf_op jit(solution)/shard_map/cond/branch_1_fun/ppermute | solution.py:184
  201.9 8.0 %collective-permute-start.15 = (f32[256,256]{0,1:T(8,128)}, f32[256,256]{0,1:T(8,128)}, u32[]{:S(2)}, u32[]{:S(2)}) collective-permute-start(f32[256,256]{0,1:T(8,128)} %add.226), channel_id=1, source_target_pairs={{0,16},{8,24},{16,0},{24,8},{1,17},{9,25},{17,1},{25,9},{2,18},{10... | collective-permute-start | bytes 786440 | tf_op jit(solution)/shard_map/cond/branch_1_fun/ppermute | solution.py:184
  204.7 3.9 %copy-start.12 = (f32[2,64,1536]{2,1,0:T(8,128)S(1)}, f32[2,64,1536]{2,1,0:T(8,128)}, u32[]{:S(2)}) copy-start(f32[2,64,1536]{2,1,0:T(8,128)} %pad_maximum_fusion.6) | copy-start | bytes 2359300 | tf_op jit(solution)/shard_map/cond
  205.8 25.4 %copy-start.13 = (f32[256,256]{0,1:T(8,128)}, f32[256,256]{0,1:T(8,128)S(1)}, u32[]{:S(2)}) copy-start(f32[256,256]{0,1:T(8,128)S(1)} %get-tuple-element.262) | copy-start | bytes 786436 | tf_op jit(solution)/shard_map/cond
  205.8 25.4 %copy-start.14 = (f32[256,256]{0,1:T(8,128)}, f32[256,256]{0,1:T(8,128)S(1)}, u32[]{:S(2)}) copy-start(f32[256,256]{0,1:T(8,128)S(1)} %get-tuple-element.263) | copy-start | bytes 786436 | tf_op jit(solution)/shard_map/cond
  207.0 20.5 %collective-permute-start.12 = (f32[128,512]{1,0:T(8,128)S(1)}, f32[128,512]{1,0:T(8,128)S(1)}, u32[]{:S(2)}, u32[]{:S(2)}) collective-permute-start(f32[128,512]{1,0:T(8,128)S(1)} %add.225), channel_id=1, source_target_pairs={{0,2},{1,3},{6,4},{7,5},{8,10},{9,11},{14,12},{15,13},{16,18},{17,... | collective-permute-start | bytes 786440 | tf_op jit(solution)/shard_map/cond/branch_1_fun/ppermute | solution.py:347
  208.5 18.7 %collective-permute-start.14 = (f32[2,64,1536]{2,1,0:T(8,128)S(1)}, f32[2,64,1536]{2,1,0:T(8,128)S(1)}, u32[]{:S(2)}, u32[]{:S(2)}) collective-permute-start(f32[2,64,1536]{2,1,0:T(8,128)S(1)} %copy-done.12), channel_id=1, source_target_pairs={{0,16},{8,24},{16,0},{24,8},{1,17},{9,25},{17,1},{25,9},{2,18},{10... | collective-permute-start | bytes 2359304 | tf_op jit(solution)/shard_map/cond/branch_1_fun/ppermute | solution.py:184
  229.2 15.6 %collective-permute-start.16 = (f32[128,512]{1,0:T(8,128)S(1)}, f32[128,512]{1,0:T(8,128)S(1)}, u32[]{:S(2)}, u32[]{:S(2)}) collective-permute-start(f32[128,512]{1,0:T(8,128)S(1)} %add.228), channel_id=1, source_target_pairs={{2,4},{3,5},{4,2},{5,3},{10,12},{11,13},{12,10},{13,11},{18,20},{1... | collective-permute-start | bytes 786440 | tf_op jit(solution)/shard_map/cond/branch_1_fun/ppermute | solution.py:347
  245.6 22.8 %collective-permute-start = (f32[128,512]{1,0:T(8,128)}, f32[128,512]{1,0:T(8,128)}, u32[]{:S(2)}, u32[]{:S(2)}) collective-permute-start(f32[128,512]{1,0:T(8,128)} %add.201), channel_id=1, source_target_pairs={{2,0},{3,1},{4,6},{5,7},{10,8},{11,9},{12,14},{13,15},{18,16},{19,... | collective-permute-start | bytes 786440 | tf_op jit(solution)/shard_map/cond/branch_1_fun/cond/branch_1_fun/ppermute | solution.py:347
  273.6 10.2 %collective-permute-start.19 = (f32[128,512]{1,0:T(8,128)}, f32[128,512]{1,0:T(8,128)S(1)}, u32[]{:S(2)}, u32[]{:S(2)}) collective-permute-start(f32[128,512]{1,0:T(8,128)} %get-tuple-element.125), channel_id=1, source_target_pairs={{0,24},{8,16},{16,8},{24,0},{1,25},{9,17},{17,9},{25,1},{2,26},{10... | collective-permute-start | bytes 786440 | tf_op jit(solution)/shard_map/cond/branch_1_fun/ppermute | solution.py:184
  275.6 10.1 %collective-permute-start.18 = (f32[128,512]{1,0:T(8,128)}, f32[128,512]{1,0:T(8,128)S(1)}, u32[]{:S(2)}, u32[]{:S(2)}) collective-permute-start(f32[128,512]{1,0:T(8,128)} %get-tuple-element.125), channel_id=1, source_target_pairs={{0,16},{8,24},{16,0},{24,8},{1,17},{9,25},{17,1},{25,9},{2,18},{10... | collective-permute-start | bytes 786440 | tf_op jit(solution)/shard_map/cond/branch_1_fun/ppermute | solution.py:184
  276.4 9.4 %collective-permute-start.17 = (f32[128,512]{1,0:T(8,128)}, f32[128,512]{1,0:T(8,128)S(1)}, u32[]{:S(2)}, u32[]{:S(2)}) collective-permute-start(f32[128,512]{1,0:T(8,128)} %get-tuple-element.125), channel_id=1, source_target_pairs={{0,8},{8,0},{16,24},{24,16},{1,9},{9,1},{17,25},{25,17},{2,10},{10... | collective-permute-start | bytes 786440 | tf_op jit(solution)/shard_map/cond/branch_1_fun/ppermute | solution.py:184
  289.1 1.9 copy-start
  (14 other events, 14.8 us)
Sparse Core Ops, SparseCore 0:
  114.8 142.4 all-reduce.3

commit v3 on v2

--- a/solution.py
+++ b/solution.py
@@ -47,34 +47,44 @@
     )
 
 
-def project_kernel(vectors_ref, window_ref, out_ref, both_ref):
-    width = vectors_ref.shape[0]
+def three_products(one, two, one_dim=1, two_dim=0):
+    (high, low), (other_high, other_low) = one, two
+    return dot(high, other_high, one_dim, two_dim) + (
+        dot(high, other_low, one_dim, two_dim) + dot(low, other_high, one_dim, two_dim)
+    )
+
+
+def project_kernel(pairs, count, *refs):
+    vectors_refs, (window_ref, out_ref) = refs[:count], refs[count : count + 2]
+    products_refs, both_ref = refs[count + 2 : -1], refs[-1]
+    width = out_ref.shape[0]
 
     @pl.when(pl.program_id(0) == 0)
     def _():
-        high, low = halves(vectors_ref[...])
-        both_ref[:width] = high
-        both_ref[width:] = low
+        values = [halves(ref[...]) for ref in vectors_refs]
+        both_ref[:width], both_ref[width:] = values[0]
+        for (one, two), ref in zip(pairs, products_refs):
+            ref[...] = three_products(values[one], values[two], 1, 1)
 
     high, low = halves(window_ref[...])
     first = dot(both_ref[...], high)
     out_ref[...] = first[:width] + first[width:] + dot(both_ref[:width], low)
 
 
-def project(vectors, window, block=256):
-    width, rows = vectors.shape
+def project(vectors, window, pairs, block=256):
+    width, rows = vectors[0].shape
     cols = window.shape[1]
     return call(
-        project_kernel,
+        functools.partial(project_kernel, pairs, len(vectors)),
         (cols // block,),
-        [
-            pl.BlockSpec((width, rows), lambda i: (0, 0)),
-            pl.BlockSpec((rows, block), lambda i: (0, i)),
-        ],
-        pl.BlockSpec((width, block), lambda i: (0, i)),
-        jax.ShapeDtypeStruct((width, cols), f32),
+        [pl.BlockSpec((width, rows), lambda i: (0, 0))] * len(vectors)
+        + [pl.BlockSpec((rows, block), lambda i: (0, i))],
+        [pl.BlockSpec((width, block), lambda i: (0, i))]
+        + [pl.BlockSpec((width, width), lambda i: (0, 0))] * len(pairs),
+        [jax.ShapeDtypeStruct((width, cols), f32)]
+        + [jax.ShapeDtypeStruct((width, width), f32)] * len(pairs),
         [pltpu.VMEM((2 * width, rows), bf16)],
-    )(vectors, window)
+    )(*vectors, window)
 
 
 def image_kernel(window_ref, vectors_ref, out_ref, both_ref):
@@ -108,47 +118,114 @@
     )(window, vectors)
 
 
-def three_products(high, low, high_ref, low_ref):
-    return dot(high, high_ref[...]) + (dot(high, low_ref[...]) + dot(low, high_ref[...]))
-
-
-def update_kernel(window_ref, near_ref, far_ref, high_ref, low_ref, out_ref):
-    vectors = jnp.concatenate([near_ref[...].T, far_ref[...].T], 1)
-    out_ref[...] = window_ref[...] - three_products(*halves(vectors), high_ref, low_ref)
-
-
-def update(window, near, far, high, low, block=512):
+def cross_kernel(near_ref, far_ref, *refs):
+    *image_refs, out_ref = refs
+
+    @pl.when(pl.program_id(0) == 0)
+    def _():
+        out_ref[...] = jnp.zeros_like(out_ref)
+
+    vectors = jnp.concatenate([near_ref[...], far_ref[...]], 0)
+    images = jnp.concatenate([one[...] for one in image_refs], 1)
+    out_ref[...] += three_products(halves(vectors), halves(images))
+
+
+def cross(near, far, images, block=512):
+    part, rows = near.shape
+    block = min(block, rows)
+    width = sum(one.shape[1] for one in images)
+    return call(
+        cross_kernel,
+        (rows // block,),
+        [pl.BlockSpec((part, block), lambda i: (0, i))] * 2
+        + [pl.BlockSpec((block, one.shape[1]), lambda i: (i, 0)) for one in images],
+        pl.BlockSpec((2 * part, width), lambda i: (0, 0)),
+        jax.ShapeDtypeStruct((2 * part, width), f32),
+    )(near, far, *images)
+
+
+def prepare_kernel(panels, lower_ref, projected_ref, columns_ref, factors_ref, *refs):
+    *inner_refs, local_ref, left_ref, high_ref, low_ref = refs
+    lower = lower_ref[0] == 1
+    width = factors_ref.shape[1]
+    part = width // 2
+    joined = factors_ref[0]
+    for panel in range(1, panels):
+        done = panel * width
+        inner = [
+            inner_refs[one * (panels - 1) - one * (one - 1) // 2 + panel - one - 1][...]
+            for one in range(panel)
+        ]
+        inner = jnp.concatenate(inner, 0) if panel > 1 else inner[0]
+        factor = factors_ref[panel]
+        between = three_products(halves(inner), halves(factor))
+        between = -three_products(halves(joined), halves(between))
+        joined = jnp.concatenate(
+            [
+                jnp.concatenate([joined, between], 1),
+                jnp.concatenate([jnp.zeros((width, done), f32), factor], 1),
+            ],
+            0,
+        )
+
+    def chosen(value, panel, other, dim):
+        start = panel * width
+        one = lax.slice_in_dim(value, start, start + part, axis=dim)
+        two = lax.slice_in_dim(value, start + part, start + width, axis=dim)
+        return jnp.where(lower == (other == 0), one, two)
+
+    local = jnp.concatenate(
+        [chosen(joined, panel, other, 1) for other in range(2) for panel in range(panels)], 1
+    )
+    both = jnp.concatenate(
+        [chosen(local, panel, other, 0) for panel in range(panels) for other in range(2)], 0
+    )
+    local_ref[...] = local
+    left_ref[...] = three_products(halves(both), halves(projected_ref[...]), 0, 0)
+    high_ref[...], low_ref[...] = halves(
+        three_products(halves(joined), halves(columns_ref[...]))
+    )
+
+
+def prepare(lower, projected, columns, factors, inner):
+    total, cols = projected.shape
+    return call(
+        functools.partial(prepare_kernel, factors.shape[0]),
+        (),
+        [pl.BlockSpec(memory_space=pltpu.SMEM)]
+        + [pl.BlockSpec(memory_space=pltpu.VMEM)] * (3 + len(inner)),
+        [pl.BlockSpec(memory_space=pltpu.VMEM)] * 4,
+        [
+            jax.ShapeDtypeStruct((total, total), f32),
+            jax.ShapeDtypeStruct((total, cols), f32),
+            jax.ShapeDtypeStruct((total, cols), bf16),
+            jax.ShapeDtypeStruct((total, cols), bf16),
+        ],
+    )(lower.astype(jnp.int32).reshape(1), projected, columns, factors, *inner)
+
+
+def finish_kernel(
+    window_ref, near_ref, far_ref, local_ref, crossed_ref, left_ref, right_high, right_low, *refs
+):
+    *image_refs, out_ref, high_ref, low_ref = refs
+    width = left_ref.shape[0]
+
+    @pl.when(pl.program_id(0) == 0)
+    def _():
+        middle = three_products(halves(local_ref[...]), halves(crossed_ref[...]), 0, 0)
+        left = left_ref[...] - three_products(halves(middle), (right_high[...], right_low[...]))
+        high_ref[:width], low_ref[:width] = halves(left)
+        high_ref[width:], low_ref[width:] = right_high[...], right_low[...]
+
+    both = jnp.concatenate(
+        [near_ref[...].T, far_ref[...].T] + [one[...] for one in image_refs], 1
+    )
+    out_ref[...] = window_ref[...] - three_products(halves(both), (high_ref[...], low_ref[...]))
+
+
+def finish(window, near, far, local, crossed, left, right, images, block=512):
     rows, cols = window.shape
-    part, width = near.shape[0], high.shape[0]
-    block = min(block, rows)
-    return call(
-        update_kernel,
-        (rows // block,),
-        [
-            pl.BlockSpec((block, cols), lambda i: (i, 0)),
-            pl.BlockSpec((part, block), lambda i: (0, i)),
-            pl.BlockSpec((part, block), lambda i: (0, i)),
-            pl.BlockSpec((width, cols), lambda i: (0, 0)),
-            pl.BlockSpec((width, cols), lambda i: (0, 0)),
-        ],
-        pl.BlockSpec((block, cols), lambda i: (i, 0)),
-        jax.ShapeDtypeStruct((rows, cols), f32),
-    )(window, near, far, high, low)
-
-
-def finish_kernel(
-    window_ref, near_ref, far_ref, middle_high, middle_low, high_ref, low_ref, *refs
-):
-    vectors = jnp.concatenate([near_ref[...].T, far_ref[...].T], 1)
-    *image_refs, out_ref = refs
-    images = jnp.concatenate([one[...] for one in image_refs], 1)
-    left = images - three_products(*halves(vectors), middle_high, middle_low)
-    out_ref[...] = window_ref[...] - three_products(*halves(left), high_ref, low_ref)
-
-
-def finish(window, near, far, images, middle, right, block=512):
-    rows, cols = window.shape
-    part, width = near.shape[0], right[0].shape[0]
+    part, width = near.shape[0], local.shape[0]
     block = min(block, rows)
     return call(
         finish_kernel,
@@ -157,16 +234,14 @@
             pl.BlockSpec((block, cols), lambda i: (i, 0)),
             pl.BlockSpec((part, block), lambda i: (0, i)),
             pl.BlockSpec((part, block), lambda i: (0, i)),
-            pl.BlockSpec((width, width), lambda i: (0, 0)),
-            pl.BlockSpec((width, width), lambda i: (0, 0)),
-            pl.BlockSpec((width, cols), lambda i: (0, 0)),
-            pl.BlockSpec((width, cols), lambda i: (0, 0)),
         ]
+        + [pl.BlockSpec((width, width), lambda i: (0, 0))] * 2
+        + [pl.BlockSpec((width, cols), lambda i: (0, 0))] * 3
         + [pl.BlockSpec((block, one.shape[1]), lambda i: (i, 0)) for one in images],
         pl.BlockSpec((block, cols), lambda i: (i, 0)),
         jax.ShapeDtypeStruct((rows, cols), f32),
-        aliases={0: 0},
-    )(window, near, far, *middle, *right, *images)
+        [pltpu.VMEM((2 * width, cols), bf16)] * 2,
+    )(window, near, far, local, crossed, left, *right, *images)
 
 
 def swap_cores(value):
@@ -297,7 +372,7 @@
         arrived = [swap_rows(shares[panel], distance) for distance in distances]
         following = along_line(panel + 1) if panel + 1 < panels else []
         if panel == 0:
-            projected, arrived, following = together(project(near, window), arrived, following)
+            projected, arrived, following = together(project([near], window, [(0, 0)]), arrived, following)
         else:
             jumps = range(1, half)
             after = [send_along(last[0], chips, -jump, chips - half - jump + 1) for jump in jumps]
@@ -356,11 +431,6 @@
     return arrived, combine
 
 
-def split(value):
-    high = lax.reduce_precision(value, 8, 7)
-    return high.astype(bf16), (value - high).astype(bf16)
-
-
 def region(run, *operands):
     results = jax.eval_shape(run, *operands)
 
@@ -384,23 +454,20 @@
     bits = [1 << bit for bit in range(row_count.bit_length() - 1)]
     orders = [bits[::-1] if panel % 2 else bits for panel in range(panels)]
     slivers = jnp.swapaxes(reflectors, 1, 2)
-    near, held, ends, columns, near_projected, images = gather_vectors(
+    near, held, ends, columns, (near_projected, same), images = gather_vectors(
         slivers, row_count, chips, window
     )
-    summed = [lax.psum(one, "col") for one in images]
-    near_parts = [
-        near_projected[near.shape[0] // panels * panel : near.shape[0] // panels * (panel + 1)]
-        for panel in range(panels)
-    ]
+    part = near.shape[0] // panels
+    width = 2 * part
+    total = panels * width
+    near_parts = [near_projected[part * panel : part * (panel + 1)] for panel in range(panels)]
     steps = [scatter_step(one, order[0]) for one, order in zip(near_parts, orders)]
     last_columns, *images = together(columns[-1], *images)
     last_image, ends, *arrived = together(
         image(window, last_columns), ends, *[one for one, _ in steps]
     )
-    near_parts = [one + kept for one, (_, kept) in zip(arrived, steps)]
-    summed.append(lax.psum(last_image, "col"))
+    held[chips - 1], held[1 - chips] = ends, ends
     half = chips // 2
-    held[chips - 1], held[1 - chips] = ends, ends
     far = jnp.stack(
         [
             by_chip(lambda one: held[(1 - one // half) * half + place - one])
@@ -408,24 +475,44 @@
         ],
         1,
     )
+    images.append(last_image)
+    near_parts = [one + kept for one, (_, kept) in zip(arrived, steps)]
+    summed = [lax.psum(one, "col") for one in images]
     columns = jnp.concatenate(columns, 0)
-    total = columns.shape[0]
-    width = total // panels
-    part = width // 2
-
-    def projections(window, near, far, columns, factors, *near_parts):
-        near_parts = list(near_parts)
+
+    def factors_of(window, near, far, same, columns, factors, images, near_parts):
         far = both_cores(far, swap_cores(far))
-        far_projected = project(far, window)
-        for step in range(1, len(bits)):
+        crossed = cross(near, far, images)
+        crossed = ordered(lower, crossed[: total // 2], crossed[total // 2 :], 0)
+        sums = [crossed[: total // 2], crossed[total // 2 :]]
+        steps = [scatter_step(one, order[0]) for one, order in zip(sums, (bits, bits[::-1]))]
+        near_steps = [scatter_step(one, order[1]) for one, order in zip(near_parts, orders)]
+        (far_projected, opposite, crossing, mixed), arrived, near_arrived = together(
+            project([far, near], window, [(0, 0), (0, 1), (1, 0)]),
+            [one for one, _ in steps],
+            [one for one, _ in near_steps],
+        )
+        sums = [one + kept for one, (_, kept) in zip(arrived, steps)]
+        near_parts = [one + kept for one, (_, kept) in zip(near_arrived, near_steps)]
+        for step in range(2, len(bits)):
             steps = [scatter_step(one, order[step]) for one, order in zip(near_parts, orders)]
-            arrived = [one for one, _ in steps]
-            if step == 1:
-                far_projected, *arrived = together(far_projected, *arrived)
-            near_parts = [one + kept for one, (_, kept) in zip(arrived, steps)]
-        far_projected, near, far = together(far_projected, near, far)
+            near_parts = [one + kept for one, kept in steps]
         far_parts = [far_projected[part * panel : part * (panel + 1)] for panel in range(panels)]
-        same, mixed, opposite = small(near, near, 1, 1), small(near, far, 1, 1), small(far, far, 1, 1)
+        for step in range(len(bits)):
+            far_steps = [scatter_step(one, order[step]) for one, order in zip(far_parts, orders)]
+            steps = []
+            if step + 1 < len(bits):
+                steps = [
+                    scatter_step(one, order[step + 1])
+                    for one, order in zip(sums, (bits, bits[::-1]))
+                ]
+            else:
+                crossed = jnp.concatenate(sums, 0)
+                steps = [(swap_cores(crossed), crossed)]
+            arrived, far_arrived = together([one for one, _ in steps], [one for one, _ in far_steps])
+            sums = [one + kept for one, (_, kept) in zip(arrived, steps)]
+            far_parts = [one + kept for one, (_, kept) in zip(far_arrived, far_steps)]
+        (crossed,) = sums
 
         def of(value, one, two):
             return value[part * one : part * (one + 1), part * two : part * (two + 1)]
@@ -434,103 +521,56 @@
             ordered(
                 lower,
                 ordered(lower, of(same, one, two), of(mixed, one, two), 1),
-                ordered(lower, of(mixed, two, one).T, of(opposite, one, two), 1),
+                ordered(lower, of(crossing, one, two), of(opposite, one, two), 1),
                 0,
             )
             for one in range(panels)
             for two in range(one + 1, panels)
         ]
-        for step in range(len(bits)):
-            steps = [scatter_step(one, order[step]) for one, order in zip(far_parts, orders)]
-            arrived = [one for one, _ in steps]
-            if step + 1 == len(bits):
-                arrived, inner = together(arrived, inner)
-            far_parts = [one + kept for one, (_, kept) in zip(arrived, steps)]
-
-        mine = [ordered(lower, one, two, 0) for one, two in zip(near_parts, far_parts)]
-        crossed = small(jnp.concatenate(mine, 0), columns, 1, 1)
         parts = [jnp.stack([one, two]) for one, two in zip(near_parts, far_parts)]
-        others = [swap_rows(one, bits[0]) for one in inner]
-        other, parts, others = together(
-            swap_cores(crossed),
-            [gather_step(one, order[-1]) for one, order in zip(parts, orders)],
-            others,
-        )
-        crossed = crossed + other
-        inner = [one + two for one, two in zip(inner, others)]
-        arrived, combine = line_step(crossed, 0, chips)
-        for step in range(len(bits) - 1)[::-1]:
-            parts = [gather_step(one, order[step]) for one, order in zip(parts, orders)]
-        for bit in bits[1:]:
-            inner = [one + swap_rows(one, bit) for one in inner]
-        arrived, parts, inner = together(arrived, parts, inner)
-        crossed = combine(crossed, arrived)
+        hops = chips - 1
+        for step, bit in enumerate(bits):
+            others = [swap_rows(one, bit) for one in inner]
+            parts = [gather_step(one, order[-1 - step]) for one, order in zip(parts, orders)]
+            if step < hops:
+                arrived, combine = line_step(crossed, step, chips)
+                parts, others, arrived = together(parts, others, arrived)
+                crossed = combine(crossed, arrived)
+            else:
+                parts, others = together(parts, others)
+            inner = [one + two for one, two in zip(inner, others)]
         projected = jnp.concatenate(parts, 0).reshape(total, cols)
 
-        joined = factors[0]
-        for panel in range(1, panels):
-            done = panel * width
-            products = jnp.concatenate(
-                [
-                    inner[one * (panels - 1) - one * (one - 1) // 2 + panel - one - 1]
-                    for one in range(panel)
-                ],
-                0,
-            )
-            between = -small(joined, small(products, factors[panel]))
-            joined = jnp.block([[joined, between], [jnp.zeros((width, done), f32), factors[panel]]])
-        def chosen(value, panel, other, dim):
-            start = panel * width
-            one = lax.slice_in_dim(value, start, start + part, axis=dim)
-            two = lax.slice_in_dim(value, start + part, start + width, axis=dim)
-            return jnp.where(lower == (other == 0), one, two)
-
-        local = jnp.concatenate(
-            [chosen(joined, panel, other, 1) for other in range(2) for panel in range(panels)], 1
-        )
-        both = jnp.concatenate(
-            [chosen(local, panel, other, 0) for panel in range(panels) for other in range(2)], 0
-        )
-        left = split(small(both, projected, 0, 0))
-        if chips > 2:
-            arrived, combine = line_step(crossed, 1, chips)
-            arrived, *left = together(arrived, *left)
-            crossed = combine(crossed, arrived)
-
-        def last_step(crossed, window, near, far, *left):
-            arrived, combine = line_step(crossed, chips - 2, chips)
-            updated, arrived = together(update(window, near, far, *left), arrived)
-            return combine(crossed, arrived), updated
-
-        for hop in range(2, chips - 2):
+        for hop in range(len(bits), hops - 1):
             arrived, combine = line_step(crossed, hop, chips)
             crossed = combine(crossed, arrived)
-        if chips > 2:
-            crossed, updated = region(last_step, crossed, window, near, far, *left)
-        else:
-            updated = update(window, near, far, *left)
-        everyone = [swap_rows(crossed, distance) for distance in range(1, row_count)]
-        right, everyone = together(split(small(joined, columns)), everyone)
-        everyone = [crossed] + everyone
-        crossed = jnp.zeros((panels, 2, part, total), f32)
+        local, left, *right = prepare(lower, projected, columns, factors, inner)
+        if len(bits) < hops:
+            arrived, combine = line_step(crossed, hops - 1, chips)
+            arrived, local, left, right = together(arrived, local, left, right)
+            crossed = combine(crossed, arrived)
+        everyone = [crossed] + [swap_rows(crossed, distance) for distance in range(1, row_count)]
+        crossed = jnp.zeros((2, total // 2, total), f32)
         for distance, value in enumerate(everyone):
             source = row ^ distance
-            value = value.reshape(panels, 2, -1, total)
-            for panel, order in enumerate(orders):
-                place, size = 0, part
+            for other, order in enumerate((bits, bits[::-1])):
+                place, size = 0, total // 2
                 for bit in order:
                     size = size // 2
                     place = place + (source // bit) % 2 * size
                 crossed = lax.dynamic_update_slice(
-                    crossed, value[panel : panel + 1], (panel, 0, place, 0)
+                    crossed, value[other * size : (other + 1) * size][None], (other, place, 0)
                 )
-        between = split(small(local, crossed.reshape(total, total), 0, 0))
-        return updated, far, between, right
-
-    updated, far, between, right = region(
-        projections, window, near, far, columns, factors, *near_parts
-    )
-    return finish(updated, near, far, summed, between, right)
+        crossed = crossed.reshape(2, panels, part, total)
+        crossed = jnp.concatenate(
+            [crossed[other, panel] for panel in range(panels) for other in range(2)], 0
+        )
+        return far, local, crossed, left, right
+
+    far, local, crossed, left, right = region(
+        factors_of, window, near, far, same, columns, factors, images, near_parts
+    )
+    return finish(window, near, far, local, crossed, left, right, summed)
 
 
 def solution(mesh):

time: 326 us -> 312 us (0.957)
  matrix products: 22.4 us -> 0 us
  Pallas kernels: 98.5 us -> 113 us
  waiting for transfers between devices: 76 us -> 68 us
  starting transfers between devices: 57.9 us -> 63.7 us
  local copies, waits for them, and re-layouts: 22.7 us -> 17.3 us
    dot_general x9 -> x0, matrix products: 22.4 us -> none  [small(): lax.dot_general(one, two, (((one_dim,), (two_dim,)), ((), ())), precision...]
    pallas_call x1, Pallas kernels: 26.4 us -> 41 us  [finish(): call(finish_kernel, (rows // block,), [pl.BlockSpec((block, cols), lambda...]
    ppermute x26 -> x30, starting transfers between devices: 29.2 us -> 35 us  [swap_rows(): lax.ppermute(value, 'row', [(row, row ^ distance) for row in range(count)])]
    ppermute x3, waiting for transfers between devices: 9.19 us -> 4.13 us  [line_step(): lax.ppermute(value, 'col', [(2 * one + core, 2 * two + core) for one, two...]
    cond x49 -> x38, local copies, waits for them, and re-layouts: 7.7 us -> 5.13 us
    pallas_call x3 -> x4, Pallas kernels: 45.9 us -> 45.8 us  [the longest x2 30.5 us: project(): call(functools.partial(project_kernel, pairs, len(vectors)), (cols // blo...]
    ppermute x26 -> x30, waiting for transfers between devices: 52.2 us -> 52.1 us  [swap_rows(): lax.ppermute(value, 'row', [(row, row ^ distance) for row in range(count)])]
  transfers between devices with their start and end apart: 45 -> 49, of which waited for: 17 -> 18; matrix products, arithmetic and copies ran while one was open for 21% -> 12% of each run, Pallas kernels for 22% -> 23%
where the time goes in v3:
time: 312 us; the launch traced here: 307 us
  Pallas kernels  113 us (36%)
  waiting for transfers between devices  68 us (22%)
  starting transfers between devices  63.7 us (20%)
  other arithmetic  31 us (10%)
  local copies, waits for them, and re-layouts  17.3 us (6%)
  between operations  14 us (4%)
    ppermute x30, waiting for transfers between devices, swap_rows(): lax.ppermute(value, 'row', [(row, row ^ distance) for row in range(count)])  52.1 us
    pallas_call x1, Pallas kernels, finish(): call(finish_kernel, (rows // block,), [pl.BlockSpec((block, cols), lambda...  41 us
    ppermute x30, starting transfers between devices, swap_rows(): lax.ppermute(value, 'row', [(row, row ^ distance) for row in range(count)])  35 us
    pallas_call x2, Pallas kernels, project(): call(functools.partial(project_kernel, pairs, len(vectors)), (cols // blo...  30.5 us
    pallas_call x2, Pallas kernels, image(): call(image_kernel, (rows // block,), [pl.BlockSpec((block, cols), lambda...  26.2 us
    ppermute x4, starting transfers between devices, send_along(): lax.ppermute(value, 'col', [(2 * (chip - step) + core, 2 * chip + core) f...  11.8 us
    ppermute x6, starting transfers between devices, swap_chips(): lax.ppermute(value, 'col', [(col, col ^ 2 * distance) for col in range(co...  9.53 us
    pallas_call x1, Pallas kernels, prepare(): call(functools.partial(prepare_kernel, factors.shape[0]), (), [pl.BlockSp...  7.94 us
  transfers between devices with their start and end apart: 49, of which 18 were waited for; matrix products, arithmetic and copies ran while one was open for 12% of the time, Pallas kernels for 23%

profile of v3, /device:TPU:8, one launch (start us, length us, event | category | flops | bytes accessed | tf_op | source)
XLA Modules:
  0.0 307.5 jit_solution(8447448286458030566)
XLA Ops:
  7.6 3.5 %collective-permute-start.25 = (f32[2,32,3072]{2,1,0:T(8,128)}, f32[2,32,3072]{2,1,0:T(8,128)S(1)}, u32[]{:S(2)}, u32[]{:S(2)}) collective-permute-start(f32[2,32,3072]{2,1,0:T(8,128)} %bitcast.168), channel_id=1, source_target_pairs={{0,2},{1,3},{2,4},{3,5},{4,6},{5,7},{8,10},{9,11},{10,12},{11,13},... | collective-permute-start | bytes 2359304 | tf_op jit(solution)/shard_map/ppermute | solution.py:298
  11.1 2.4 collective-permute-start.24
  15.6 2.4 collective-permute-start.29
  19.0 5.4 %collective-permute-done.29 = f32[2,16,1536]{2,1,0:T(8,128)S(1)} collective-permute-done((f32[2,16,1536]{2,1,0:T(8,128)}, f32[2,16,1536]{2,1,0:T(8,128)S(1)}, u32[]{:S(2)}, u32[]{:S(2)}) %collective-permute-start.29) | collective-permute-done | bytes 196640 | tf_op jit(solution)/shard_map/ppermute | solution.py:259
  24.5 3.1 %collective-permute-done.28 = f32[2,16,1536]{2,1,0:T(8,128)S(1)} collective-permute-done((f32[2,16,1536]{2,1,0:T(8,128)S(1)}, f32[2,16,1536]{2,1,0:T(8,128)S(1)}, u32[]{:S(2)}, u32[]{:S(2)}) %collective-permute-start.28) | collective-permute-done | bytes 196640 | tf_op jit(solution)/shard_map/ppermute | solution.py:259
  27.7 2.0 collective-permute-done.25
  29.7 3.2 %collective-permute-done.24 = f32[2,32,3072]{2,1,0:T(8,128)S(1)} collective-permute-done((f32[2,32,3072]{2,1,0:T(8,128)}, f32[2,32,3072]{2,1,0:T(8,128)S(1)}, u32[]{:S(2)}, u32[]{:S(2)}) %collective-permute-start.24) | collective-permute-done | bytes 786464 | tf_op jit(solution)/shard_map/ppermute | solution.py:298
  32.9 1.6 fusion.17
  35.9 1.6 collective-permute-start.33
  37.6 1.3 collective-permute-start.32
  39.6 1.6 collective-permute-start.39
  41.3 5.1 %collective-permute-done.33 = f32[16,1536]{1,0:T(8,128)S(1)} collective-permute-done((f32[16,1536]{1,0:T(8,128)S(1)}, f32[16,1536]{1,0:T(8,128)S(1)}, u32[]{:S(2)}, u32[]{:S(2)}) %collective-permute-start.33) | collective-permute-done | bytes 98336 | tf_op jit(solution)/shard_map/ppermute | solution.py:254
  46.4 1.4 collective-permute-done.32
  47.8 4.3 %collective-permute-start.37 = (f32[16,1536]{1,0:T(8,128)S(1)}, f32[16,1536]{1,0:T(8,128)S(1)}, u32[]{:S(2)}, u32[]{:S(2)}) collective-permute-start(f32[16,1536]{1,0:T(8,128)S(1)} %get-tuple-element.259), channel_id=1, source_target_pairs={{0,2},{1,3},{2,0},{3,1},{4,6},{5,7},{6,4},{7,5},{8,10},{9,11},{10,... | collective-permute-start | bytes 294920 | tf_op jit(solution)/shard_map/ppermute | solution.py:254
  52.9 2.5 collective-permute-start.36
  57.7 13.8 %shard_map.38 = (f32[256,1536]{1,0:T(8,128)S(1)}, f32[256,256]{1,0:T(8,128)}) custom-call(f32[256,3072]{1,0:T(8,128)S(1)} %bitcast.161, f32[3072,1536]{1,0:T(8,128)} %window_ref.5), custom_call_target="tpu_custom_call" | custom-call | flops 1 | bytes 1 | tf_op jit(solution)/shard_map/pallas_call | solution.py:77
  71.5 1.9 collective-permute-start.43
  73.4 4.0 %collective-permute-start.44 = (f32[2,32,3072]{2,1,0:T(8,128)S(1)}, f32[2,32,3072]{2,1,0:T(8,128)S(1)}, u32[]{:S(2)}, u32[]{:S(2)}) collective-permute-start(f32[2,32,3072]{2,1,0:T(8,128)S(1)} %copy-done.7), channel_id=1, source_target_pairs={{2,4},{3,5},{4,6},{5,7},{10,12},{11,13},{12,14},{13,15},{18,20},{1... | collective-permute-start | bytes 2359304 | tf_op jit(solution)/shard_map/ppermute | solution.py:298
  77.6 2.5 collective-permute-start.42
  82.3 13.1 %shard_map.39 = f32[3072,256]{1,0:T(8,128)} custom-call(f32[3072,1536]{1,0:T(8,128)} %window_ref.5, f32[256,1536]{1,0:T(8,128)S(1)} %bitcast.158), custom_call_target="tpu_custom_call" | custom-call | flops 1 | bytes 1 | tf_op jit(solution)/shard_map/pallas_call | solution.py:108
  96.4 2.2 collective-permute-start.45
  98.6 1.5 collective-permute-start.46
  100.1 1.5 collective-permute-start.47
  101.7 13.1 %shard_map.40 = f32[3072,256]{1,0:T(8,128)} custom-call(f32[3072,1536]{1,0:T(8,128)} %window_ref.5, f32[256,1536]{1,0:T(8,128)S(1)} %bitcast.156), custom_call_target="tpu_custom_call" | custom-call | flops 1 | bytes 1 | tf_op jit(solution)/shard_map/pallas_call | solution.py:108
  114.9 1.8 pad_maximum_fusion.14
  117.8 2.7 select_select_fusion.3
  120.5 2.9 pad_maximum_fusion.16
  123.4 134.3 %conditional.1 = (f32[256,3072]{1,0:T(8,128)}, f32[512,512]{1,0:T(8,128)}, f32[512,512]{1,0:T(8,128)}, f32[512,1536]{1,0:T(8,128)}, bf16[512,1536]{1,0:T(8,128)(2,1)}, /*index=5*/bf16[512,1536]{1,0:T(8,128)(2,1)}) conditional(s32[]{:T(128)} %convert_element_type.4, () %tuple.31, (f32[2,2,32,3072]{3,2,0,1:T(8,128)}, f32[2,32,3072]{2,1,0:T(8,128)}, ...), branch_computations={%region_0.1_spmd, %region_1.2_spmd} | conditional | flops 9371941 | bytes 168825712 | solution.py:440
  124.2 1.2 dynamic-slice_add_fusion.3
  126.5 1.2 dynamic-slice_add_fusion.2
  127.6 2.3 fusion.1
  130.0 2.0 pad_maximum_fusion
  133.9 7.4 %branch_1_fun.4 = f32[512,512]{1,0:T(8,128)S(1)} custom-call(f32[256,3072]{1,0:T(8,128)S(1)} %get-tuple-element.68.refs_1_.near_ref, f32[256,3072]{1,0:T(8,128)} %bitcast.2.refs_0_.far_ref, f32[3072,256]{1,0:T(8,128)S(1)} %copy-done.3, f32[3072,256]{1,0:T(8,128)S(1)} %copy-done.4), custom_call_target="tpu_custom_call" | custom-call | flops 1 | bytes 1 | tf_op jit(solution)/shard_map/cond/branch_1_fun/pallas_call | solution.py:137
  143.6 1.6 collective-permute-start.2
  145.9 1.5 collective-permute-start.4
  147.4 16.6 %branch_1_fun.3 = (f32[256,1536]{1,0:T(8,128)S(1)}, f32[256,256]{1,0:T(8,128)S(1)}, f32[256,256]{1,0:T(8,128)S(1)}, f32[256,256]{1,0:T(8,128)S(1)}) custom-call(f32[256,3072]{1,0:T(8,128)} %bitcast.2.refs_0_.far_ref, f32[256,3072]{1,0:T(8,128)S(1)} %get-tuple-element.68.refs_1_.near_ref, f32[3072,1536]{1,0:T(8,128)} %get-tuple-element.69.refs_2_), custom_call_target="tpu_custom_call" | custom-call | flops 1 | bytes 1 | tf_op jit(solution)/shard_map/cond/branch_1_fun/pallas_call | solution.py:77
  168.2 1.5 collective-permute-start.14
  170.6 1.6 collective-permute-start.8
  173.1 11.3 %collective-permute-done.7 = f32[64,1536]{1,0:T(8,128)S(1)} collective-permute-done((f32[64,1536]{1,0:T(8,128)S(1)}, f32[64,1536]{1,0:T(8,128)S(1)}, u32[]{:S(2)}, u32[]{:S(2)}) %collective-permute-start.7) | collective-permute-done | bytes 393248 | tf_op jit(solution)/shard_map/cond/branch_1_fun/ppermute | solution.py:259
  184.7 1.4 collective-permute-start.11
  186.1 1.6 collective-permute-start.10
  188.8 1.6 collective-permute-done.11
  190.4 1.3 collective-permute-done.10
  192.6 1.3 collective-permute-start.15
  194.0 1.6 collective-permute-start.12
  195.6 5.0 %collective-permute-done.13 = f32[2,32,1536]{2,1,0:T(8,128)S(1)} collective-permute-done((f32[2,32,1536]{2,1,0:T(8,128)S(1)}, f32[2,32,1536]{2,1,0:T(8,128)S(1)}, u32[]{:S(2)}, u32[]{:S(2)}) %collective-permute-start.13) | collective-permute-done | bytes 393248 | tf_op jit(solution)/shard_map/cond/branch_1_fun/ppermute | solution.py:259
  200.7 1.8 collective-permute-done.12
  204.5 3.6 %collective-permute-done.15 = f32[128,512]{1,0:T(8,128)S(1)} collective-permute-done((f32[128,512]{1,0:T(8,128)S(1)}, f32[128,512]{1,0:T(8,128)S(1)}, u32[]{:S(2)}, u32[]{:S(2)}) %collective-permute-start.15) | collective-permute-done | bytes 262176 | tf_op jit(solution)/shard_map/cond/branch_1_fun/ppermute | solution.py:422
  208.8 1.3 collective-permute-start.16
  210.1 1.1 add.254
  212.2 1.5 collective-permute-start.18
  213.7 1.9 collective-permute-start.19
  216.3 8.9 %collective-permute-done.16 = f32[2,64,1536]{2,1,0:T(8,128)} collective-permute-done((f32[2,64,1536]{2,1,0:T(8,128)}, f32[2,64,1536]{2,1,0:T(8,128)}, u32[]{:S(2)}, u32[]{:S(2)}) %collective-permute-start.16) | collective-permute-done | bytes 786464 | tf_op jit(solution)/shard_map/cond/branch_1_fun/ppermute | solution.py:259
  225.2 1.5 broadcast_select_fusion.3
  226.9 7.0 %collective-permute-done.17 = f32[2,64,1536]{2,1,0:T(8,128)S(1)} collective-permute-done((f32[2,64,1536]{2,1,0:T(8,128)}, f32[2,64,1536]{2,1,0:T(8,128)S(1)}, u32[]{:S(2)}, u32[]{:S(2)}) %collective-permute-start.17) | collective-permute-done | bytes 786464 | tf_op jit(solution)/shard_map/cond/branch_1_fun/ppermute | solution.py:259
  234.3 1.7 collective-permute-start.20
  236.2 1.7 copy-done.5
  237.9 7.9 %branch_1_fun.5 = (f32[512,512]{1,0:T(8,128)}, f32[512,1536]{1,0:T(8,128)}, bf16[512,1536]{1,0:T(8,128)(2,1)}, bf16[512,1536]{1,0:T(8,128)(2,1)}) custom-call(s32[1]{0:T(128)} %bitcast.7.lower_ref, f32[512,1536]{1,0:T(8,128)S(1)} %bitcast.160, f32[512,1536]{1,0:T(8,128)S(1)} %copy-done.5, f32[2,256,256]{2,1,0:T(8,128)S(1)} %copy-done.32, ...), custom_call_target="tpu_custom_call" | custom-call | flops 1 | bytes 1 | tf_op jit(solution)/shard_map/cond/branch_1_fun/pallas_call | solution.py:192
  246.3 1.1 collective-permute-start.23
  248.3 1.6 collective-permute-start.21
  250.0 5.8 %collective-permute-done.21 = f32[128,512]{1,0:T(8,128)S(1)} collective-permute-done((f32[128,512]{1,0:T(8,128)S(1)}, f32[128,512]{1,0:T(8,128)S(1)}, u32[]{:S(2)}, u32[]{:S(2)}) %collective-permute-start.21) | collective-permute-done | bytes 262176 | tf_op jit(solution)/shard_map/cond/branch_1_fun/ppermute | solution.py:259
  256.6 1.1 pad_maximum_fusion.4
  257.7 1.9 copy-done
  259.6 41.0 %shard_map.41 = f32[3072,1536]{1,0:T(8,128)} custom-call(f32[3072,1536]{1,0:T(8,128)} %window_ref.5, f32[256,3072]{1,0:T(8,128)S(1)} %bitcast.163, f32[256,3072]{1,0:T(8,128)} %get-tuple-element.195.far_ref, f32[512,512]{1,0:T(8,128)} %get-tuple-element.196.local_ref, f32[512,512]{1,0:T(8,128)} %get-tuple-element.197.crossed_ref, ...), custom_call_target="tpu_custom_call" | custom-call | flops 1 | bytes 1 | tf_op jit(solution)/shard_map/pallas_call | solution.py:230
  (226 shorter events, 35.9 us)
Async XLA Ops:
  6.5 251.2 %all-reduce.3.cloned.1.call-start = ((), (), s32[]{:S(2)}) async-start(), calls=%async_computation | async-start | bytes 12582912 | tf_op jit(solution)/shard_map/psum | solution.py:480
  7.6 6.0 %collective-permute-start.26 = (f32[2,32,1536]{2,1,0:T(8,128)S(1)}, f32[2,32,1536]{2,1,0:T(8,128)S(1)}, u32[]{:S(2)}, u32[]{:S(2)}) collective-permute-start(f32[2,32,1536]{2,1,0:T(8,128)S(1)} %dynamic-slice_bitcast_fusion), channel_id=1, source_target_pairs={{0,1},{1,0},{2,3},{3,2},{4,5},{5,4},{6,7},{7,6},{8,9},{9,8},{10,11... | collective-permute-start | bytes 1179656 | tf_op jit(solution)/shard_map/ppermute | solution.py:249
  7.6 22.0 %collective-permute-start.25 = (f32[2,32,3072]{2,1,0:T(8,128)}, f32[2,32,3072]{2,1,0:T(8,128)S(1)}, u32[]{:S(2)}, u32[]{:S(2)}) collective-permute-start(f32[2,32,3072]{2,1,0:T(8,128)} %bitcast.168), channel_id=1, source_target_pairs={{0,2},{1,3},{2,4},{3,5},{4,6},{5,7},{8,10},{9,11},{10,12},{11,13},... | collective-permute-start | bytes 2359304 | tf_op jit(solution)/shard_map/ppermute | solution.py:298
  11.1 21.8 %collective-permute-start.24 = (f32[2,32,3072]{2,1,0:T(8,128)}, f32[2,32,3072]{2,1,0:T(8,128)S(1)}, u32[]{:S(2)}, u32[]{:S(2)}) collective-permute-start(f32[2,32,3072]{2,1,0:T(8,128)} %bitcast.169), channel_id=1, source_target_pairs={{2,0},{3,1},{4,2},{5,3},{6,4},{7,5},{10,8},{11,9},{12,10},{13,11},... | collective-permute-start | bytes 2359304 | tf_op jit(solution)/shard_map/ppermute | solution.py:298
  15.5 14.1 %copy-start.12 = (f32[2,4,16,1536]{3,2,1,0:T(8,128)}, f32[2,4,16,1536]{3,2,1,0:T(8,128)S(1)}, u32[]{:S(2)}) copy-start(f32[2,4,16,1536]{3,2,1,0:T(8,128)S(1)} %get-tuple-element.251) | copy-start | bytes 2359300
  15.6 8.9 %collective-permute-start.29 = (f32[2,16,1536]{2,1,0:T(8,128)}, f32[2,16,1536]{2,1,0:T(8,128)S(1)}, u32[]{:S(2)}, u32[]{:S(2)}) collective-permute-start(f32[2,16,1536]{2,1,0:T(8,128)} %get-tuple-element.252), channel_id=1, source_target_pairs={{0,24},{8,16},{16,8},{24,0},{1,25},{9,17},{17,9},{25,1},{2,26},{10... | collective-permute-start | bytes 589832 | tf_op jit(solution)/shard_map/ppermute | solution.py:259
  18.0 9.6 %collective-permute-start.28 = (f32[2,16,1536]{2,1,0:T(8,128)S(1)}, f32[2,16,1536]{2,1,0:T(8,128)S(1)}, u32[]{:S(2)}, u32[]{:S(2)}) collective-permute-start(f32[2,16,1536]{2,1,0:T(8,128)S(1)} %get-tuple-element.253), channel_id=1, source_target_pairs={{0,16},{8,24},{16,0},{24,8},{1,17},{9,25},{17,1},{25,9},{2,18},{10... | collective-permute-start | bytes 589832 | tf_op jit(solution)/shard_map/ppermute | solution.py:259
  18.5 9.2 %collective-permute-start.27 = (f32[2,16,1536]{2,1,0:T(8,128)S(1)}, f32[2,16,1536]{2,1,0:T(8,128)S(1)}, u32[]{:S(2)}, u32[]{:S(2)}) collective-permute-start(f32[2,16,1536]{2,1,0:T(8,128)S(1)} %get-tuple-element.254), channel_id=1, source_target_pairs={{0,8},{8,0},{16,24},{24,16},{1,9},{9,1},{17,25},{25,17},{2,10},{10... | collective-permute-start | bytes 589832 | tf_op jit(solution)/shard_map/ppermute | solution.py:259
  24.5 5.2 %copy-start.36 = (f32[2,16,1536]{2,1,0:T(8,128)}, f32[2,16,1536]{2,1,0:T(8,128)S(1)}, u32[]{:S(2)}) copy-start(f32[2,16,1536]{2,1,0:T(8,128)S(1)} %collective-permute-done.29) | copy-start | bytes 589828
  29.7 26.2 %copy-start.6 = (f32[2,32,3072]{2,1,0:T(8,128)}, f32[2,32,3072]{2,1,0:T(8,128)S(1)}, u32[]{:S(2)}) copy-start(f32[2,32,3072]{2,1,0:T(8,128)S(1)} %collective-permute-done.25) | copy-start | bytes 2359300
  32.9 23.0 %copy-start.9 = (f32[2,32,3072]{2,1,0:T(8,128)}, f32[2,32,3072]{2,1,0:T(8,128)S(1)}, u32[]{:S(2)}) copy-start(f32[2,32,3072]{2,1,0:T(8,128)S(1)} %collective-permute-done.24) | copy-start | bytes 2359300
  34.7 17.5 %collective-permute-start.30 = (f32[2,2,32,3072]{3,2,0,1:T(8,128)S(1)}, f32[2,2,32,3072]{3,2,0,1:T(8,128)S(1)}, u32[]{:S(2)}, u32[]{:S(2)}) collective-permute-start(f32[2,2,32,3072]{3,2,0,1:T(8,128)S(1)} %pad_maximum_fusion.15), channel_id=1, source_target_pairs={{0,1},{1,0},{2,3},{3,2},{4,5},{5,4},{6,7},{7,6},{8,9},{9,8},{10,11... | collective-permute-start | bytes 4718600 | tf_op jit(solution)/shard_map/ppermute | solution.py:249
  35.9 10.5 %collective-permute-start.33 = (f32[16,1536]{1,0:T(8,128)S(1)}, f32[16,1536]{1,0:T(8,128)S(1)}, u32[]{:S(2)}, u32[]{:S(2)}) collective-permute-start(f32[16,1536]{1,0:T(8,128)S(1)} %get-tuple-element.260), channel_id=1, source_target_pairs={{0,6},{1,7},{2,4},{3,5},{4,2},{5,3},{6,0},{7,1},{8,14},{9,15},{10,... | collective-permute-start | bytes 294920 | tf_op jit(solution)/shard_map/ppermute | solution.py:254
  37.6 10.3 %collective-permute-start.32 = (f32[16,1536]{1,0:T(8,128)S(1)}, f32[16,1536]{1,0:T(8,128)S(1)}, u32[]{:S(2)}, u32[]{:S(2)}) collective-permute-start(f32[16,1536]{1,0:T(8,128)S(1)} %get-tuple-element.261), channel_id=1, source_target_pairs={{0,4},{1,5},{2,6},{3,7},{4,0},{5,1},{6,2},{7,3},{8,12},{9,13},{10,... | collective-permute-start | bytes 294920 | tf_op jit(solution)/shard_map/ppermute | solution.py:254
  38.9 13.3 %collective-permute-start.31 = (f32[16,1536]{1,0:T(8,128)S(1)}, f32[16,1536]{1,0:T(8,128)S(1)}, u32[]{:S(2)}, u32[]{:S(2)}) collective-permute-start(f32[16,1536]{1,0:T(8,128)S(1)} %get-tuple-element.262), channel_id=1, source_target_pairs={{0,2},{1,3},{2,0},{3,1},{4,6},{5,7},{6,4},{7,5},{8,10},{9,11},{10,... | collective-permute-start | bytes 294920 | tf_op jit(solution)/shard_map/ppermute | solution.py:254
  39.6 17.2 %collective-permute-start.39 = (f32[16,1536]{1,0:T(8,128)S(1)}, f32[16,1536]{1,0:T(8,128)S(1)}, u32[]{:S(2)}, u32[]{:S(2)}) collective-permute-start(f32[16,1536]{1,0:T(8,128)S(1)} %get-tuple-element.257), channel_id=1, source_target_pairs={{0,6},{1,7},{2,4},{3,5},{4,2},{5,3},{6,0},{7,1},{8,14},{9,15},{10,... | collective-permute-start | bytes 294920 | tf_op jit(solution)/shard_map/ppermute | solution.py:254
  46.4 25.1 %collective-permute-start.38 = (f32[16,1536]{1,0:T(8,128)S(1)}, f32[16,1536]{1,0:T(8,128)S(1)}, u32[]{:S(2)}, u32[]{:S(2)}) collective-permute-start(f32[16,1536]{1,0:T(8,128)S(1)} %get-tuple-element.258), channel_id=1, source_target_pairs={{0,4},{1,5},{2,6},{3,7},{4,0},{5,1},{6,2},{7,3},{8,12},{9,13},{10,... | collective-permute-start | bytes 294920 | tf_op jit(solution)/shard_map/ppermute | solution.py:254
  47.8 25.6 %collective-permute-start.37 = (f32[16,1536]{1,0:T(8,128)S(1)}, f32[16,1536]{1,0:T(8,128)S(1)}, u32[]{:S(2)}, u32[]{:S(2)}) collective-permute-start(f32[16,1536]{1,0:T(8,128)S(1)} %get-tuple-element.259), channel_id=1, source_target_pairs={{0,2},{1,3},{2,0},{3,1},{4,6},{5,7},{6,4},{7,5},{8,10},{9,11},{10,... | collective-permute-start | bytes 294920 | tf_op jit(solution)/shard_map/ppermute | solution.py:254
  52.9 24.6 %collective-permute-start.36 = (f32[4,16,1536]{2,1,0:T(8,128)S(1)}, f32[4,16,1536]{2,1,0:T(8,128)S(1)}, u32[]{:S(2)}, u32[]{:S(2)}) collective-permute-start(f32[4,16,1536]{2,1,0:T(8,128)S(1)} %bitcast_dynamic-update-slice_fusion.15), channel_id=1, source_target_pairs={{0,24},{8,16},{16,8},{24,0},{1,25},{9,17},{17,9},{25,1},{2,26},{10... | collective-permute-start | bytes 1179656 | tf_op jit(solution)/shard_map/ppermute | solution.py:259
  55.4 22.1 %collective-permute-start.35 = (f32[4,16,1536]{2,1,0:T(8,128)S(1)}, f32[4,16,1536]{2,1,0:T(8,128)S(1)}, u32[]{:S(2)}, u32[]{:S(2)}) collective-permute-start(f32[4,16,1536]{2,1,0:T(8,128)S(1)} %bitcast_dynamic-update-slice_fusion.15), channel_id=1, source_target_pairs={{0,16},{8,24},{16,0},{24,8},{1,17},{9,25},{17,1},{25,9},{2,18},{10... | collective-permute-start | bytes 1179656 | tf_op jit(solution)/shard_map/ppermute | solution.py:259
  56.9 20.6 %collective-permute-start.34 = (f32[4,16,1536]{2,1,0:T(8,128)S(1)}, f32[4,16,1536]{2,1,0:T(8,128)S(1)}, u32[]{:S(2)}, u32[]{:S(2)}) collective-permute-start(f32[4,16,1536]{2,1,0:T(8,128)S(1)} %bitcast_dynamic-update-slice_fusion.15), channel_id=1, source_target_pairs={{0,8},{8,0},{16,24},{24,16},{1,9},{9,1},{17,25},{25,17},{2,10},{10... | collective-permute-start | bytes 1179656 | tf_op jit(solution)/shard_map/ppermute | solution.py:259
  57.6 13.8 %copy-start.10 = (f32[2,32,3072]{2,1,0:T(8,128)S(1)}, f32[2,32,3072]{2,1,0:T(8,128)}, u32[]{:S(2)}) copy-start(f32[2,32,3072]{2,1,0:T(8,128)} %copy-done.9) | copy-start | bytes 2359300
  57.7 15.8 %copy-start.7 = (f32[2,32,3072]{2,1,0:T(8,128)S(1)}, f32[2,32,3072]{2,1,0:T(8,128)}, u32[]{:S(2)}) copy-start(f32[2,32,3072]{2,1,0:T(8,128)} %copy-done.6) | copy-start | bytes 2359300
  71.5 24.9 %collective-permute-start.43 = (f32[2,32,3072]{2,1,0:T(8,128)S(1)}, f32[2,32,3072]{2,1,0:T(8,128)S(1)}, u32[]{:S(2)}, u32[]{:S(2)}) collective-permute-start(f32[2,32,3072]{2,1,0:T(8,128)S(1)} %copy-done.10), channel_id=1, source_target_pairs={{2,0},{3,1},{4,2},{5,3},{10,8},{11,9},{12,10},{13,11},{18,16},{19,... | collective-permute-start | bytes 2359304 | tf_op jit(solution)/shard_map/ppermute | solution.py:298
  73.4 25.1 %collective-permute-start.44 = (f32[2,32,3072]{2,1,0:T(8,128)S(1)}, f32[2,32,3072]{2,1,0:T(8,128)S(1)}, u32[]{:S(2)}, u32[]{:S(2)}) collective-permute-start(f32[2,32,3072]{2,1,0:T(8,128)S(1)} %copy-done.7), channel_id=1, source_target_pairs={{2,4},{3,5},{4,6},{5,7},{10,12},{11,13},{12,14},{13,15},{18,20},{1... | collective-permute-start | bytes 2359304 | tf_op jit(solution)/shard_map/ppermute | solution.py:298
  77.6 22.5 %collective-permute-start.42 = (f32[4,16,1536]{2,1,0:T(8,128)S(1)}, f32[4,16,1536]{2,1,0:T(8,128)S(1)}, u32[]{:S(2)}, u32[]{:S(2)}) collective-permute-start(f32[4,16,1536]{2,1,0:T(8,128)S(1)} %bitcast_dynamic-update-slice_fusion.11), channel_id=1, source_target_pairs={{0,24},{8,16},{16,8},{24,0},{1,25},{9,17},{17,9},{25,1},{2,26},{10... | collective-permute-start | bytes 1179656 | tf_op jit(solution)/shard_map/ppermute | solution.py:259
  80.1 21.5 %collective-permute-start.41 = (f32[4,16,1536]{2,1,0:T(8,128)S(1)}, f32[4,16,1536]{2,1,0:T(8,128)S(1)}, u32[]{:S(2)}, u32[]{:S(2)}) collective-permute-start(f32[4,16,1536]{2,1,0:T(8,128)S(1)} %bitcast_dynamic-update-slice_fusion.11), channel_id=1, source_target_pairs={{0,16},{8,24},{16,0},{24,8},{1,17},{9,25},{17,1},{25,9},{2,18},{10... | collective-permute-start | bytes 1179656 | tf_op jit(solution)/shard_map/ppermute | solution.py:259
  80.6 21.0 %collective-permute-start.40 = (f32[4,16,1536]{2,1,0:T(8,128)S(1)}, f32[4,16,1536]{2,1,0:T(8,128)S(1)}, u32[]{:S(2)}, u32[]{:S(2)}) collective-permute-start(f32[4,16,1536]{2,1,0:T(8,128)S(1)} %bitcast_dynamic-update-slice_fusion.11), channel_id=1, source_target_pairs={{0,8},{8,0},{16,24},{24,16},{1,9},{9,1},{17,25},{25,17},{2,10},{10... | collective-permute-start | bytes 1179656 | tf_op jit(solution)/shard_map/ppermute | solution.py:259
  81.2 14.1 %copy-start.15 = (f32[128,1536]{1,0:T(8,128)}, f32[128,1536]{1,0:T(8,128)S(1)}, u32[]{:S(2)}) copy-start(f32[128,1536]{1,0:T(8,128)S(1)} %get-tuple-element.244) | copy-start | bytes 2359300
  96.4 5.3 %copy-start.28 = (f32[2,32,3072]{2,1,0:T(8,128)}, f32[2,32,3072]{2,1,0:T(8,128)S(1)}, u32[]{:S(2)}) copy-start(f32[2,32,3072]{2,1,0:T(8,128)S(1)} %collective-permute-done.43) | copy-start | bytes 2359300
  96.4 18.4 %collective-permute-start.45 = (f32[2,32,3072]{2,1,0:T(8,128)}, f32[2,32,3072]{2,1,0:T(8,128)}, u32[]{:S(2)}, u32[]{:S(2)}) collective-permute-start(f32[2,32,3072]{2,1,0:T(8,128)} %broadcast_select_fusion.9), channel_id=1, source_target_pairs={{4,0},{5,1},{2,6},{3,7},{12,8},{13,9},{10,14},{11,15},{20,16},{21,... | collective-permute-start | bytes 2359304 | tf_op jit(solution)/shard_map/ppermute | solution.py:389
  98.6 16.3 %collective-permute-start.46 = (f32[64,1536]{1,0:T(8,128)}, f32[64,1536]{1,0:T(8,128)S(1)}, u32[]{:S(2)}, u32[]{:S(2)}) collective-permute-start(f32[64,1536]{1,0:T(8,128)} %constant_dynamic-slice_fusion.10), channel_id=1, source_target_pairs={{0,8},{8,0},{16,24},{24,16},{1,9},{9,1},{17,25},{25,17},{2,10},{10... | collective-permute-start | bytes 1179656 | tf_op jit(solution)/shard_map/ppermute | solution.py:259
  100.1 14.8 %collective-permute-start.47 = (f32[64,1536]{1,0:T(8,128)}, f32[64,1536]{1,0:T(8,128)}, u32[]{:S(2)}, u32[]{:S(2)}) collective-permute-start(f32[64,1536]{1,0:T(8,128)} %constant_dynamic-slice_fusion.11), channel_id=1, source_target_pairs={{0,16},{8,24},{16,0},{24,8},{1,17},{9,25},{17,1},{25,9},{2,18},{10... | collective-permute-start | bytes 1179656 | tf_op jit(solution)/shard_map/ppermute | solution.py:259
  123.4 4.2 %collective-permute-start = (f32[2,2,32,3072]{3,2,0,1:T(8,128)}, f32[2,2,32,3072]{3,2,0,1:T(8,128)}, u32[]{:S(2)}, u32[]{:S(2)}) collective-permute-start(f32[2,2,32,3072]{3,2,0,1:T(8,128)} %get-tuple-element.66), channel_id=1, source_target_pairs={{0,1},{1,0},{2,3},{3,2},{4,5},{5,4},{6,7},{7,6},{8,9},{9,8},{10,11... | collective-permute-start | bytes 4718600 | tf_op jit(solution)/shard_map/cond/branch_1_fun/ppermute | solution.py:249
  126.0 38.0 %collective-permute-start.3 = (f32[32,1536]{1,0:T(8,128)}, f32[32,1536]{1,0:T(8,128)}, u32[]{:S(2)}, u32[]{:S(2)}) collective-permute-start(f32[32,1536]{1,0:T(8,128)} %constant_dynamic-slice_fusion.7), channel_id=1, source_target_pairs={{0,16},{8,24},{16,0},{24,8},{1,17},{9,25},{17,1},{25,9},{2,18},{10... | collective-permute-start | bytes 589832 | tf_op jit(solution)/shard_map/cond/branch_1_fun/ppermute | solution.py:259
  127.6 17.6 %copy-start.21 = (f32[64,1536]{1,0:T(8,128)}, f32[64,1536]{1,0:T(8,128)S(1)}, u32[]{:S(2)}) copy-start(f32[64,1536]{1,0:T(8,128)S(1)} %dynamic-slice_add_fusion.2) | copy-start | bytes 1179652 | tf_op jit(solution)/shard_map/cond
  142.3 21.8 %collective-permute-start.1 = (f32[128,512]{1,0:T(8,128)}, f32[128,512]{1,0:T(8,128)}, u32[]{:S(2)}, u32[]{:S(2)}) collective-permute-start(f32[128,512]{1,0:T(8,128)} %constant_dynamic-slice_fusion.9), channel_id=1, source_target_pairs={{0,8},{8,0},{16,24},{24,16},{1,9},{9,1},{17,25},{25,17},{2,10},{10... | collective-permute-start | bytes 786440 | tf_op jit(solution)/shard_map/cond/branch_1_fun/ppermute | solution.py:259
  143.6 20.4 %collective-permute-start.2 = (f32[128,512]{1,0:T(8,128)}, f32[128,512]{1,0:T(8,128)}, u32[]{:S(2)}, u32[]{:S(2)}) collective-permute-start(f32[128,512]{1,0:T(8,128)} %constant_dynamic-slice_fusion.8), channel_id=1, source_target_pairs={{0,16},{8,24},{16,0},{24,8},{1,17},{9,25},{17,1},{25,9},{2,18},{10... | collective-permute-start | bytes 786440 | tf_op jit(solution)/shard_map/cond/branch_1_fun/ppermute | solution.py:259
  145.9 18.1 %collective-permute-start.4 = (f32[32,1536]{1,0:T(8,128)}, f32[32,1536]{1,0:T(8,128)}, u32[]{:S(2)}, u32[]{:S(2)}) collective-permute-start(f32[32,1536]{1,0:T(8,128)} %constant_dynamic-slice_fusion.6), channel_id=1, source_target_pairs={{0,8},{8,0},{16,24},{24,16},{1,9},{9,1},{17,25},{25,17},{2,10},{10... | collective-permute-start | bytes 589832 | tf_op jit(solution)/shard_map/cond/branch_1_fun/ppermute | solution.py:259
  147.4 16.7 %copy-start.20 = (f32[256,512]{1,0:T(8,128)S(1)}, f32[256,512]{1,0:T(8,128)}, u32[]{:S(2)}) copy-start(f32[256,512]{1,0:T(8,128)} %copy-done.19) | copy-start | bytes 1572868 | tf_op jit(solution)/shard_map/cond
  147.4 18.2 %copy-start.18 = (f32[256,512]{1,0:T(8,128)S(1)}, f32[256,512]{1,0:T(8,128)}, u32[]{:S(2)}) copy-start(f32[256,512]{1,0:T(8,128)} %copy-done.17) | copy-start | bytes 1572868 | tf_op jit(solution)/shard_map/cond
  165.1 8.0 %collective-permute-start.5 = (f32[64,512]{1,0:T(8,128)S(1)}, f32[64,512]{1,0:T(8,128)S(1)}, u32[]{:S(2)}, u32[]{:S(2)}) collective-permute-start(f32[64,512]{1,0:T(8,128)S(1)} %constant_dynamic-slice_fusion.5), channel_id=1, source_target_pairs={{0,16},{8,24},{16,0},{24,8},{1,17},{9,25},{17,1},{25,9},{2,18},{10... | collective-permute-start | bytes 393224 | tf_op jit(solution)/shard_map/cond/branch_1_fun/ppermute | solution.py:259
  166.6 6.6 %collective-permute-start.6 = (f32[64,512]{1,0:T(8,128)S(1)}, f32[64,512]{1,0:T(8,128)S(1)}, u32[]{:S(2)}, u32[]{:S(2)}) collective-permute-start(f32[64,512]{1,0:T(8,128)S(1)} %constant_dynamic-slice_fusion.4), channel_id=1, source_target_pairs={{0,8},{8,0},{16,24},{24,16},{1,9},{9,1},{17,25},{25,17},{2,10},{10... | collective-permute-start | bytes 393224 | tf_op jit(solution)/shard_map/cond/branch_1_fun/ppermute | solution.py:259
  168.2 36.3 %collective-permute-start.14 = (f32[256,256]{1,0:T(8,128)S(1)}, f32[256,256]{1,0:T(8,128)S(1)}, u32[]{:S(2)}, u32[]{:S(2)}) collective-permute-start(f32[256,256]{1,0:T(8,128)S(1)} %pad_maximum_fusion.10), channel_id=1, source_target_pairs={{0,8},{8,0},{16,24},{24,16},{1,9},{9,1},{17,25},{25,17},{2,10},{10... | collective-permute-start | bytes 786440 | tf_op jit(solution)/shard_map/cond/branch_1_fun/ppermute | solution.py:259
  169.9 14.6 %collective-permute-start.7 = (f32[64,1536]{1,0:T(8,128)S(1)}, f32[64,1536]{1,0:T(8,128)S(1)}, u32[]{:S(2)}, u32[]{:S(2)}) collective-permute-start(f32[64,1536]{1,0:T(8,128)S(1)} %constant_dynamic-slice_fusion.3), channel_id=1, source_target_pairs={{0,8},{8,0},{16,24},{24,16},{1,9},{9,1},{17,25},{25,17},{2,10},{10... | collective-permute-start | bytes 1179656 | tf_op jit(solution)/shard_map/cond/branch_1_fun/ppermute | solution.py:259
  170.6 13.9 %collective-permute-start.8 = (f32[64,1536]{1,0:T(8,128)S(1)}, f32[64,1536]{1,0:T(8,128)S(1)}, u32[]{:S(2)}, u32[]{:S(2)}) collective-permute-start(f32[64,1536]{1,0:T(8,128)S(1)} %constant_dynamic-slice_fusion.2), channel_id=1, source_target_pairs={{0,16},{8,24},{16,0},{24,8},{1,17},{9,25},{17,1},{25,9},{2,18},{10... | collective-permute-start | bytes 1179656 | tf_op jit(solution)/shard_map/cond/branch_1_fun/ppermute | solution.py:259
  184.7 5.7 %collective-permute-start.11 = (f32[32,1536]{1,0:T(8,128)S(1)}, f32[32,1536]{1,0:T(8,128)S(1)}, u32[]{:S(2)}, u32[]{:S(2)}) collective-permute-start(f32[32,1536]{1,0:T(8,128)S(1)} %constant_dynamic-slice_fusion), channel_id=1, source_target_pairs={{0,8},{8,0},{16,24},{24,16},{1,9},{9,1},{17,25},{25,17},{2,10},{10... | collective-permute-start | bytes 589832 | tf_op jit(solution)/shard_map/cond/branch_1_fun/ppermute | solution.py:259
  186.1 5.7 %collective-permute-start.10 = (f32[32,1536]{1,0:T(8,128)S(1)}, f32[32,1536]{1,0:T(8,128)S(1)}, u32[]{:S(2)}, u32[]{:S(2)}) collective-permute-start(f32[32,1536]{1,0:T(8,128)S(1)} %constant_dynamic-slice_fusion.1), channel_id=1, source_target_pairs={{0,16},{8,24},{16,0},{24,8},{1,17},{9,25},{17,1},{25,9},{2,18},{10... | collective-permute-start | bytes 589832 | tf_op jit(solution)/shard_map/cond/branch_1_fun/ppermute | solution.py:259
  187.7 4.0 %collective-permute-start.9 = (f32[128,512]{1,0:T(8,128)S(1)}, f32[128,512]{1,0:T(8,128)S(1)}, u32[]{:S(2)}, u32[]{:S(2)}) collective-permute-start(f32[128,512]{1,0:T(8,128)S(1)} %pad_maximum_fusion.9), channel_id=1, source_target_pairs={{0,1},{1,0},{2,3},{3,2},{4,5},{5,4},{6,7},{7,6},{8,9},{9,8},{10,11... | collective-permute-start | bytes 786440 | tf_op jit(solution)/shard_map/cond/branch_1_fun/ppermute | solution.py:249
  191.8 8.8 %collective-permute-start.13 = (f32[2,32,1536]{2,1,0:T(8,128)S(1)}, f32[2,32,1536]{2,1,0:T(8,128)S(1)}, u32[]{:S(2)}, u32[]{:S(2)}) collective-permute-start(f32[2,32,1536]{2,1,0:T(8,128)S(1)} %pad_maximum_fusion.8), channel_id=1, source_target_pairs={{0,8},{8,0},{16,24},{24,16},{1,9},{9,1},{17,25},{25,17},{2,10},{10... | collective-permute-start | bytes 1179656 | tf_op jit(solution)/shard_map/cond/branch_1_fun/ppermute | solution.py:259
  192.6 9.9 %copy-start.27 = (f32[128,512]{1,0:T(8,128)}, f32[128,512]{1,0:T(8,128)S(1)}, u32[]{:S(2)}) copy-start(f32[128,512]{1,0:T(8,128)S(1)} %fusion.15) | copy-start | bytes 786436 | tf_op jit(solution)/shard_map/cond
  192.6 15.5 %collective-permute-start.15 = (f32[128,512]{1,0:T(8,128)S(1)}, f32[128,512]{1,0:T(8,128)S(1)}, u32[]{:S(2)}, u32[]{:S(2)}) collective-permute-start(f32[128,512]{1,0:T(8,128)S(1)} %fusion.15), channel_id=1, source_target_pairs={{0,2},{1,3},{6,4},{7,5},{8,10},{9,11},{14,12},{15,13},{16,18},{17,... | collective-permute-start | bytes 786440 | tf_op jit(solution)/shard_map/cond/branch_1_fun/ppermute | solution.py:422
  194.0 8.5 %collective-permute-start.12 = (f32[2,32,1536]{2,1,0:T(8,128)S(1)}, f32[2,32,1536]{2,1,0:T(8,128)S(1)}, u32[]{:S(2)}, u32[]{:S(2)}) collective-permute-start(f32[2,32,1536]{2,1,0:T(8,128)S(1)} %pad_maximum_fusion.7), channel_id=1, source_target_pairs={{0,16},{8,24},{16,0},{24,8},{1,17},{9,25},{17,1},{25,9},{2,18},{10... | collective-permute-start | bytes 1179656 | tf_op jit(solution)/shard_map/cond/branch_1_fun/ppermute | solution.py:259
  203.5 7.7 %copy-start.24 = (f32[128,256]{1,0:T(8,128)S(1)}, f32[128,256]{1,0:T(8,128)}, u32[]{:S(2)}) copy-start(f32[128,256]{1,0:T(8,128)} %copy-done.23) | copy-start | bytes 393220 | tf_op jit(solution)/shard_map/cond
  203.5 7.7 %copy-start.26 = (f32[128,256]{1,0:T(8,128)S(1)}, f32[128,256]{1,0:T(8,128)}, u32[]{:S(2)}) copy-start(f32[128,256]{1,0:T(8,128)} %copy-done.25) | copy-start | bytes 393220 | tf_op jit(solution)/shard_map/cond
  208.8 16.4 %collective-permute-start.16 = (f32[2,64,1536]{2,1,0:T(8,128)}, f32[2,64,1536]{2,1,0:T(8,128)}, u32[]{:S(2)}, u32[]{:S(2)}) collective-permute-start(f32[2,64,1536]{2,1,0:T(8,128)} %pad_maximum_fusion.5), channel_id=1, source_target_pairs={{0,8},{8,0},{16,24},{24,16},{1,9},{9,1},{17,25},{25,17},{2,10},{10... | collective-permute-start | bytes 2359304 | tf_op jit(solution)/shard_map/cond/branch_1_fun/ppermute | solution.py:259
  212.2 21.9 %collective-permute-start.18 = (f32[256,256]{1,0:T(8,128)S(1)}, f32[256,256]{1,0:T(8,128)S(1)}, u32[]{:S(2)}, u32[]{:S(2)}) collective-permute-start(f32[256,256]{1,0:T(8,128)S(1)} %fusion.14), channel_id=1, source_target_pairs={{0,16},{8,24},{16,0},{24,8},{1,17},{9,25},{17,1},{25,9},{2,18},{10... | collective-permute-start | bytes 786440 | tf_op jit(solution)/shard_map/cond/branch_1_fun/ppermute | solution.py:259
  213.7 20.4 %collective-permute-start.19 = (f32[128,512]{1,0:T(8,128)S(1)}, f32[128,512]{1,0:T(8,128)S(1)}, u32[]{:S(2)}, u32[]{:S(2)}) collective-permute-start(f32[128,512]{1,0:T(8,128)S(1)} %add.254), channel_id=1, source_target_pairs={{2,4},{3,5},{4,2},{5,3},{10,12},{11,13},{12,10},{13,11},{18,20},{1... | collective-permute-start | bytes 786440 | tf_op jit(solution)/shard_map/cond/branch_1_fun/ppermute | solution.py:422
  215.6 18.2 %collective-permute-start.17 = (f32[2,64,1536]{2,1,0:T(8,128)}, f32[2,64,1536]{2,1,0:T(8,128)S(1)}, u32[]{:S(2)}, u32[]{:S(2)}) collective-permute-start(f32[2,64,1536]{2,1,0:T(8,128)} %pad_maximum_fusion.6), channel_id=1, source_target_pairs={{0,16},{8,24},{16,0},{24,8},{1,17},{9,25},{17,1},{25,9},{2,18},{10... | collective-permute-start | bytes 2359304 | tf_op jit(solution)/shard_map/cond/branch_1_fun/ppermute | solution.py:259
  226.7 7.2 %copy-start.16 = (f32[2,64,1536]{2,1,0:T(8,128)S(1)}, f32[2,64,1536]{2,1,0:T(8,128)}, u32[]{:S(2)}) copy-start(f32[2,64,1536]{2,1,0:T(8,128)} %pad_maximum_fusion.6) | copy-start | bytes 2359300 | tf_op jit(solution)/shard_map/cond
  234.3 12.0 %collective-permute-start.20 = (f32[128,512]{1,0:T(8,128)S(1)}, f32[128,512]{1,0:T(8,128)S(1)}, u32[]{:S(2)}, u32[]{:S(2)}) collective-permute-start(f32[128,512]{1,0:T(8,128)S(1)} %add.256), channel_id=1, source_target_pairs={{2,0},{3,1},{4,6},{5,7},{10,8},{11,9},{12,14},{13,15},{18,16},{19,... | collective-permute-start | bytes 786440 | tf_op jit(solution)/shard_map/cond/branch_1_fun/ppermute | solution.py:422
  246.3 10.2 %collective-permute-start.23 = (f32[128,512]{1,0:T(8,128)S(1)}, f32[128,512]{1,0:T(8,128)S(1)}, u32[]{:S(2)}, u32[]{:S(2)}) collective-permute-start(f32[128,512]{1,0:T(8,128)S(1)} %broadcast_select_fusion.8), channel_id=1, source_target_pairs={{0,24},{8,16},{16,8},{24,0},{1,25},{9,17},{17,9},{25,1},{2,26},{10... | collective-permute-start | bytes 786440 | tf_op jit(solution)/shard_map/cond/branch_1_fun/ppermute | solution.py:259
  247.4 9.1 %collective-permute-start.22 = (f32[128,512]{1,0:T(8,128)S(1)}, f32[128,512]{1,0:T(8,128)S(1)}, u32[]{:S(2)}, u32[]{:S(2)}) collective-permute-start(f32[128,512]{1,0:T(8,128)S(1)} %broadcast_select_fusion.8), channel_id=1, source_target_pairs={{0,16},{8,24},{16,0},{24,8},{1,17},{9,25},{17,1},{25,9},{2,18},{10... | collective-permute-start | bytes 786440 | tf_op jit(solution)/shard_map/cond/branch_1_fun/ppermute | solution.py:259
  248.3 7.5 %collective-permute-start.21 = (f32[128,512]{1,0:T(8,128)S(1)}, f32[128,512]{1,0:T(8,128)S(1)}, u32[]{:S(2)}, u32[]{:S(2)}) collective-permute-start(f32[128,512]{1,0:T(8,128)S(1)} %broadcast_select_fusion.8), channel_id=1, source_target_pairs={{0,8},{8,0},{16,24},{24,16},{1,9},{9,1},{17,25},{25,17},{2,10},{10... | collective-permute-start | bytes 786440 | tf_op jit(solution)/shard_map/cond/branch_1_fun/ppermute | solution.py:259
  (27 other events, 57.2 us)
Sparse Core Ops, SparseCore 0:
  115.0 141.1 all-reduce.2

commit v4 on v3

--- a/solution.py
+++ b/solution.py
@@ -9,7 +9,7 @@
 
 f32 = jnp.float32
 bf16 = jnp.bfloat16
-VMEM_BYTES = 50 * 1024 * 1024
+MIB = 1024 * 1024
 
 
 def halves(value):
@@ -33,7 +33,7 @@
     )
 
 
-def call(kernel, grid, in_specs, out_specs, out_shape, scratch=(), aliases=None):
+def call(kernel, mebibytes, grid, in_specs, out_specs, out_shape, scratch=()):
     return pl.pallas_call(
         kernel,
         grid=grid,
@@ -41,8 +41,7 @@
         out_specs=out_specs,
         out_shape=out_shape,
         scratch_shapes=scratch,
-        input_output_aliases=aliases or {},
-        compiler_params=pltpu.CompilerParams(vmem_limit_bytes=VMEM_BYTES),
+        compiler_params=pltpu.CompilerParams(vmem_limit_bytes=mebibytes * MIB),
         cost_estimate=pl.CostEstimate(flops=1, bytes_accessed=1, transcendentals=0),
     )
 
@@ -76,6 +75,7 @@
     cols = window.shape[1]
     return call(
         functools.partial(project_kernel, pairs, len(vectors)),
+        36,
         (cols // block,),
         [pl.BlockSpec((width, rows), lambda i: (0, 0))] * len(vectors)
         + [pl.BlockSpec((rows, block), lambda i: (0, i))],
@@ -107,6 +107,7 @@
     block = min(block, rows)
     return call(
         image_kernel,
+        22,
         (rows // block,),
         [
             pl.BlockSpec((block, cols), lambda i: (i, 0)),
@@ -136,6 +137,7 @@
     width = sum(one.shape[1] for one in images)
     return call(
         cross_kernel,
+        16,
         (rows // block,),
         [pl.BlockSpec((part, block), lambda i: (0, i))] * 2
         + [pl.BlockSpec((block, one.shape[1]), lambda i: (i, 0)) for one in images],
@@ -191,6 +193,7 @@
     total, cols = projected.shape
     return call(
         functools.partial(prepare_kernel, factors.shape[0]),
+        36,
         (),
         [pl.BlockSpec(memory_space=pltpu.SMEM)]
         + [pl.BlockSpec(memory_space=pltpu.VMEM)] * (3 + len(inner)),
@@ -229,6 +232,7 @@
     block = min(block, rows)
     return call(
         finish_kernel,
+        52,
         (rows // block,),
         [
             pl.BlockSpec((block, cols), lambda i: (i, 0)),

time: 312 us -> 304 us (0.974)
  Pallas kernels: 113 us -> 105 us
    pallas_call x7, Pallas kernels: 113 us -> 105 us  [the longest x1 41.2 us: finish(): call(finish_kernel, 52, (rows // block,), [pl.BlockSpec((block, cols), la...]
  transfers between devices with their start and end apart: 49 -> 49, of which waited for: 18 -> 18; matrix products, arithmetic and copies ran while one was open for 12% -> 12% of each run, Pallas kernels for 23% -> 21%
where the time goes in v4:
time: 304 us; the launch traced here: 300 us
  Pallas kernels  105 us (35%)
  waiting for transfers between devices  69.1 us (23%)
  starting transfers between devices  64.6 us (21%)
  other arithmetic  31 us (10%)
  local copies, waits for them, and re-layouts  15.9 us (5%)
  between operations  14 us (5%)
    ppermute x30, waiting for transfers between devices, swap_rows(): lax.ppermute(value, 'row', [(row, row ^ distance) for row in range(count)])  53 us
    pallas_call x1, Pallas kernels, finish(): call(finish_kernel, 52, (rows // block,), [pl.BlockSpec((block, cols), la...  41.2 us
    ppermute x30, starting transfers between devices, swap_rows(): lax.ppermute(value, 'row', [(row, row ^ distance) for row in range(count)])  35 us
    pallas_call x2, Pallas kernels, project(): call(functools.partial(project_kernel, pairs, len(vectors)), 36, (cols //...  28.5 us
    pallas_call x2, Pallas kernels, image(): call(image_kernel, 22, (rows // block,), [pl.BlockSpec((block, cols), lam...  19.3 us
    ppermute x4, starting transfers between devices, send_along(): lax.ppermute(value, 'col', [(2 * (chip - step) + core, 2 * chip + core) f...  11.8 us
    ppermute x6, starting transfers between devices, swap_chips(): lax.ppermute(value, 'col', [(col, col ^ 2 * distance) for col in range(co...  9.53 us
    pallas_call x1, Pallas kernels, prepare(): call(functools.partial(prepare_kernel, factors.shape[0]), 36, (), [pl.Blo...  7.94 us
  transfers between devices with their start and end apart: 49, of which 18 were waited for; matrix products, arithmetic and copies ran while one was open for 12% of the time, Pallas kernels for 21%

profile of v4, /device:TPU:8, one launch (start us, length us, event | category | flops | bytes accessed | tf_op | source)
XLA Modules:
  0.0 299.8 jit_solution(11399203134453603480)
XLA Ops:
  7.6 3.5 %collective-permute-start.25 = (f32[2,32,3072]{2,1,0:T(8,128)}, f32[2,32,3072]{2,1,0:T(8,128)S(1)}, u32[]{:S(2)}, u32[]{:S(2)}) collective-permute-start(f32[2,32,3072]{2,1,0:T(8,128)} %bitcast.168), channel_id=1, source_target_pairs={{0,2},{1,3},{2,4},{3,5},{4,6},{5,7},{8,10},{9,11},{10,12},{11,13},... | collective-permute-start | bytes 2359304 | tf_op jit(solution)/shard_map/ppermute | solution.py:302
  11.1 2.4 collective-permute-start.24
  13.6 1.1 bitcast_select_fusion.5
  15.6 2.4 collective-permute-start.29
  19.0 5.4 %collective-permute-done.29 = f32[2,16,1536]{2,1,0:T(8,128)S(1)} collective-permute-done((f32[2,16,1536]{2,1,0:T(8,128)}, f32[2,16,1536]{2,1,0:T(8,128)S(1)}, u32[]{:S(2)}, u32[]{:S(2)}) %collective-permute-start.29) | collective-permute-done | bytes 196640 | tf_op jit(solution)/shard_map/ppermute | solution.py:263
  24.5 3.1 %collective-permute-done.28 = f32[2,16,1536]{2,1,0:T(8,128)S(1)} collective-permute-done((f32[2,16,1536]{2,1,0:T(8,128)S(1)}, f32[2,16,1536]{2,1,0:T(8,128)S(1)}, u32[]{:S(2)}, u32[]{:S(2)}) %collective-permute-start.28) | collective-permute-done | bytes 196640 | tf_op jit(solution)/shard_map/ppermute | solution.py:263
  27.7 2.0 collective-permute-done.25
  29.7 3.2 %collective-permute-done.24 = f32[2,32,3072]{2,1,0:T(8,128)S(1)} collective-permute-done((f32[2,32,3072]{2,1,0:T(8,128)}, f32[2,32,3072]{2,1,0:T(8,128)S(1)}, u32[]{:S(2)}, u32[]{:S(2)}) %collective-permute-start.24) | collective-permute-done | bytes 786464 | tf_op jit(solution)/shard_map/ppermute | solution.py:302
  32.9 1.6 fusion.17
  35.9 1.6 collective-permute-start.33
  37.6 1.3 collective-permute-start.32
  39.7 1.6 collective-permute-start.39
  41.3 5.1 %collective-permute-done.33 = f32[16,1536]{1,0:T(8,128)S(1)} collective-permute-done((f32[16,1536]{1,0:T(8,128)S(1)}, f32[16,1536]{1,0:T(8,128)S(1)}, u32[]{:S(2)}, u32[]{:S(2)}) %collective-permute-start.33) | collective-permute-done | bytes 98336 | tf_op jit(solution)/shard_map/ppermute | solution.py:258
  46.4 1.4 collective-permute-done.32
  47.8 4.3 %collective-permute-start.37 = (f32[16,1536]{1,0:T(8,128)S(1)}, f32[16,1536]{1,0:T(8,128)S(1)}, u32[]{:S(2)}, u32[]{:S(2)}) collective-permute-start(f32[16,1536]{1,0:T(8,128)S(1)} %get-tuple-element.259), channel_id=1, source_target_pairs={{0,2},{1,3},{2,0},{3,1},{4,6},{5,7},{6,4},{7,5},{8,10},{9,11},{10,... | collective-permute-start | bytes 294920 | tf_op jit(solution)/shard_map/ppermute | solution.py:258
  52.9 2.5 collective-permute-start.36
  57.8 11.9 %shard_map.38 = (f32[256,1536]{1,0:T(8,128)S(1)}, f32[256,256]{1,0:T(8,128)}) custom-call(f32[256,3072]{1,0:T(8,128)S(1)} %bitcast.161, f32[3072,1536]{1,0:T(8,128)S(1)} %copy-done), custom_call_target="tpu_custom_call" | custom-call | flops 1 | bytes 1 | tf_op jit(solution)/shard_map/pallas_call | solution.py:76
  69.7 1.9 collective-permute-start.43
  71.6 4.0 %collective-permute-start.44 = (f32[2,32,3072]{2,1,0:T(8,128)S(1)}, f32[2,32,3072]{2,1,0:T(8,128)S(1)}, u32[]{:S(2)}, u32[]{:S(2)}) collective-permute-start(f32[2,32,3072]{2,1,0:T(8,128)S(1)} %copy-done.7), channel_id=1, source_target_pairs={{2,4},{3,5},{4,6},{5,7},{10,12},{11,13},{12,14},{13,15},{18,20},{1... | collective-permute-start | bytes 2359304 | tf_op jit(solution)/shard_map/ppermute | solution.py:302
  75.7 2.5 collective-permute-start.42
  80.5 9.6 %shard_map.39 = f32[3072,256]{1,0:T(8,128)} custom-call(f32[3072,1536]{1,0:T(8,128)S(1)} %copy-done, f32[256,1536]{1,0:T(8,128)S(1)} %bitcast.158), custom_call_target="tpu_custom_call" | custom-call | flops 1 | bytes 1 | tf_op jit(solution)/shard_map/pallas_call | solution.py:108
  91.1 2.2 collective-permute-start.45
  93.3 1.5 collective-permute-start.46
  94.8 1.5 collective-permute-start.47
  96.4 9.7 %shard_map.40 = f32[3072,256]{1,0:T(8,128)} custom-call(f32[3072,1536]{1,0:T(8,128)S(1)} %copy-done, f32[256,1536]{1,0:T(8,128)S(1)} %bitcast.156), custom_call_target="tpu_custom_call" | custom-call | flops 1 | bytes 1 | tf_op jit(solution)/shard_map/pallas_call | solution.py:108
  106.2 1.8 pad_maximum_fusion.14
  109.1 2.5 select_select_fusion.3
  111.7 3.0 pad_maximum_fusion.16
  115.1 136.6 %conditional.1 = (f32[256,3072]{1,0:T(8,128)}, f32[512,512]{1,0:T(8,128)}, f32[512,512]{1,0:T(8,128)}, f32[512,1536]{1,0:T(8,128)}, bf16[512,1536]{1,0:T(8,128)(2,1)}, /*index=5*/bf16[512,1536]{1,0:T(8,128)(2,1)}) conditional(s32[]{:T(128)} %convert_element_type.4, () %tuple.31, (f32[2,2,32,3072]{3,2,0,1:T(8,128)}, f32[2,32,3072]{2,1,0:T(8,128)}, ...), branch_computations={%region_0.1_spmd, %region_1.2_spmd} | conditional | flops 9371941 | bytes 168825712 | solution.py:444
  115.8 1.2 dynamic-slice_add_fusion.3
  117.7 1.4 collective-permute-start.3
  119.1 1.2 dynamic-slice_add_fusion.2
  120.3 2.3 fusion.1
  122.6 2.0 pad_maximum_fusion
  126.6 7.5 %branch_1_fun.4 = f32[512,512]{1,0:T(8,128)S(1)} custom-call(f32[256,3072]{1,0:T(8,128)S(1)} %get-tuple-element.68.refs_1_.near_ref, f32[256,3072]{1,0:T(8,128)} %bitcast.2.refs_0_.far_ref, f32[3072,256]{1,0:T(8,128)S(1)} %copy-done.3, f32[3072,256]{1,0:T(8,128)S(1)} %copy-done.4), custom_call_target="tpu_custom_call" | custom-call | flops 1 | bytes 1 | tf_op jit(solution)/shard_map/cond/branch_1_fun/pallas_call | solution.py:138
  136.1 1.9 collective-permute-start.2
  139.3 16.6 %branch_1_fun.3 = (f32[256,1536]{1,0:T(8,128)S(1)}, f32[256,256]{1,0:T(8,128)S(1)}, f32[256,256]{1,0:T(8,128)S(1)}, f32[256,256]{1,0:T(8,128)S(1)}) custom-call(f32[256,3072]{1,0:T(8,128)} %bitcast.2.refs_0_.far_ref, f32[256,3072]{1,0:T(8,128)S(1)} %get-tuple-element.68.refs_1_.near_ref, f32[3072,1536]{1,0:T(8,128)} %get-tuple-element.69.refs_2_), custom_call_target="tpu_custom_call" | custom-call | flops 1 | bytes 1 | tf_op jit(solution)/shard_map/cond/branch_1_fun/pallas_call | solution.py:76
  157.1 1.3 collective-permute-start.5
  160.7 1.8 collective-permute-start.14
  163.3 1.8 collective-permute-start.8
  166.0 11.3 %collective-permute-done.7 = f32[64,1536]{1,0:T(8,128)S(1)} collective-permute-done((f32[64,1536]{1,0:T(8,128)S(1)}, f32[64,1536]{1,0:T(8,128)S(1)}, u32[]{:S(2)}, u32[]{:S(2)}) %collective-permute-start.7) | collective-permute-done | bytes 393248 | tf_op jit(solution)/shard_map/cond/branch_1_fun/ppermute | solution.py:263
  177.5 1.4 collective-permute-start.11
  180.8 2.4 collective-permute-done.11
  183.3 1.3 collective-permute-done.10
  185.5 1.3 collective-permute-start.15
  186.9 1.5 collective-permute-start.12
  188.4 4.9 %collective-permute-done.13 = f32[2,32,1536]{2,1,0:T(8,128)S(1)} collective-permute-done((f32[2,32,1536]{2,1,0:T(8,128)S(1)}, f32[2,32,1536]{2,1,0:T(8,128)S(1)}, u32[]{:S(2)}, u32[]{:S(2)}) %collective-permute-start.13) | collective-permute-done | bytes 393248 | tf_op jit(solution)/shard_map/cond/branch_1_fun/ppermute | solution.py:263
  193.4 1.9 collective-permute-done.12
  197.2 3.7 %collective-permute-done.15 = f32[128,512]{1,0:T(8,128)S(1)} collective-permute-done((f32[128,512]{1,0:T(8,128)S(1)}, f32[128,512]{1,0:T(8,128)S(1)}, u32[]{:S(2)}, u32[]{:S(2)}) %collective-permute-start.15) | collective-permute-done | bytes 262176 | tf_op jit(solution)/shard_map/cond/branch_1_fun/ppermute | solution.py:426
  201.6 1.3 collective-permute-start.16
  203.0 1.1 add.254
  205.8 3.0 collective-permute-start.19
  208.8 1.3 collective-permute-start.17
  210.1 7.8 %collective-permute-done.16 = f32[2,64,1536]{2,1,0:T(8,128)} collective-permute-done((f32[2,64,1536]{2,1,0:T(8,128)}, f32[2,64,1536]{2,1,0:T(8,128)}, u32[]{:S(2)}, u32[]{:S(2)}) %collective-permute-start.16) | collective-permute-done | bytes 786464 | tf_op jit(solution)/shard_map/cond/branch_1_fun/ppermute | solution.py:263
  218.0 1.5 broadcast_select_fusion.3
  219.6 7.7 %collective-permute-done.17 = f32[2,64,1536]{2,1,0:T(8,128)S(1)} collective-permute-done((f32[2,64,1536]{2,1,0:T(8,128)}, f32[2,64,1536]{2,1,0:T(8,128)S(1)}, u32[]{:S(2)}, u32[]{:S(2)}) %collective-permute-start.17) | collective-permute-done | bytes 786464 | tf_op jit(solution)/shard_map/cond/branch_1_fun/ppermute | solution.py:263
  227.7 1.7 collective-permute-start.20
  229.6 1.7 copy-done.5
  231.3 7.9 %branch_1_fun.5 = (f32[512,512]{1,0:T(8,128)}, f32[512,1536]{1,0:T(8,128)}, bf16[512,1536]{1,0:T(8,128)(2,1)}, bf16[512,1536]{1,0:T(8,128)(2,1)}) custom-call(s32[1]{0:T(128)} %bitcast.7.lower_ref, f32[512,1536]{1,0:T(8,128)S(1)} %bitcast.160, f32[512,1536]{1,0:T(8,128)S(1)} %copy-done.5, f32[2,256,256]{2,1,0:T(8,128)S(1)} %copy-done.32, ...), custom_call_target="tpu_custom_call" | custom-call | flops 1 | bytes 1 | tf_op jit(solution)/shard_map/cond/branch_1_fun/pallas_call | solution.py:194
  239.9 1.5 collective-permute-start.23
  241.3 1.2 collective-permute-start.22
  243.6 6.3 %collective-permute-done.21 = f32[128,512]{1,0:T(8,128)S(1)} collective-permute-done((f32[128,512]{1,0:T(8,128)S(1)}, f32[128,512]{1,0:T(8,128)S(1)}, u32[]{:S(2)}, u32[]{:S(2)}) %collective-permute-start.21) | collective-permute-done | bytes 262176 | tf_op jit(solution)/shard_map/cond/branch_1_fun/ppermute | solution.py:263
  250.6 1.1 pad_maximum_fusion.4
  251.7 41.2 %shard_map.41 = f32[3072,1536]{1,0:T(8,128)} custom-call(f32[3072,1536]{1,0:T(8,128)} %window_ref.5, f32[256,3072]{1,0:T(8,128)S(1)} %bitcast.163, f32[256,3072]{1,0:T(8,128)} %get-tuple-element.195.far_ref, f32[512,512]{1,0:T(8,128)} %get-tuple-element.196.local_ref, f32[512,512]{1,0:T(8,128)} %get-tuple-element.197.crossed_ref, ...), custom_call_target="tpu_custom_call" | custom-call | flops 1 | bytes 1 | tf_op jit(solution)/shard_map/pallas_call | solution.py:233
  (226 shorter events, 35.3 us)
Async XLA Ops:
  6.5 245.2 %all-reduce.3.cloned.1.call-start = ((), (), s32[]{:S(2)}) async-start(), calls=%async_computation | async-start | bytes 12582912 | tf_op jit(solution)/shard_map/psum | solution.py:484
  7.6 6.0 %collective-permute-start.26 = (f32[2,32,1536]{2,1,0:T(8,128)S(1)}, f32[2,32,1536]{2,1,0:T(8,128)S(1)}, u32[]{:S(2)}, u32[]{:S(2)}) collective-permute-start(f32[2,32,1536]{2,1,0:T(8,128)S(1)} %dynamic-slice_bitcast_fusion), channel_id=1, source_target_pairs={{0,1},{1,0},{2,3},{3,2},{4,5},{5,4},{6,7},{7,6},{8,9},{9,8},{10,11... | collective-permute-start | bytes 1179656 | tf_op jit(solution)/shard_map/ppermute | solution.py:253
  7.6 22.0 %collective-permute-start.25 = (f32[2,32,3072]{2,1,0:T(8,128)}, f32[2,32,3072]{2,1,0:T(8,128)S(1)}, u32[]{:S(2)}, u32[]{:S(2)}) collective-permute-start(f32[2,32,3072]{2,1,0:T(8,128)} %bitcast.168), channel_id=1, source_target_pairs={{0,2},{1,3},{2,4},{3,5},{4,6},{5,7},{8,10},{9,11},{10,12},{11,13},... | collective-permute-start | bytes 2359304 | tf_op jit(solution)/shard_map/ppermute | solution.py:302
  11.1 21.8 %collective-permute-start.24 = (f32[2,32,3072]{2,1,0:T(8,128)}, f32[2,32,3072]{2,1,0:T(8,128)S(1)}, u32[]{:S(2)}, u32[]{:S(2)}) collective-permute-start(f32[2,32,3072]{2,1,0:T(8,128)} %bitcast.169), channel_id=1, source_target_pairs={{2,0},{3,1},{4,2},{5,3},{6,4},{7,5},{10,8},{11,9},{12,10},{13,11},... | collective-permute-start | bytes 2359304 | tf_op jit(solution)/shard_map/ppermute | solution.py:302
  15.5 14.1 %copy-start.12 = (f32[2,4,16,1536]{3,2,1,0:T(8,128)}, f32[2,4,16,1536]{3,2,1,0:T(8,128)S(1)}, u32[]{:S(2)}) copy-start(f32[2,4,16,1536]{3,2,1,0:T(8,128)S(1)} %get-tuple-element.251) | copy-start | bytes 2359300
  15.6 8.9 %collective-permute-start.29 = (f32[2,16,1536]{2,1,0:T(8,128)}, f32[2,16,1536]{2,1,0:T(8,128)S(1)}, u32[]{:S(2)}, u32[]{:S(2)}) collective-permute-start(f32[2,16,1536]{2,1,0:T(8,128)} %get-tuple-element.252), channel_id=1, source_target_pairs={{0,24},{8,16},{16,8},{24,0},{1,25},{9,17},{17,9},{25,1},{2,26},{10... | collective-permute-start | bytes 589832 | tf_op jit(solution)/shard_map/ppermute | solution.py:263
  18.0 9.6 %collective-permute-start.28 = (f32[2,16,1536]{2,1,0:T(8,128)S(1)}, f32[2,16,1536]{2,1,0:T(8,128)S(1)}, u32[]{:S(2)}, u32[]{:S(2)}) collective-permute-start(f32[2,16,1536]{2,1,0:T(8,128)S(1)} %get-tuple-element.253), channel_id=1, source_target_pairs={{0,16},{8,24},{16,0},{24,8},{1,17},{9,25},{17,1},{25,9},{2,18},{10... | collective-permute-start | bytes 589832 | tf_op jit(solution)/shard_map/ppermute | solution.py:263
  18.5 9.2 %collective-permute-start.27 = (f32[2,16,1536]{2,1,0:T(8,128)S(1)}, f32[2,16,1536]{2,1,0:T(8,128)S(1)}, u32[]{:S(2)}, u32[]{:S(2)}) collective-permute-start(f32[2,16,1536]{2,1,0:T(8,128)S(1)} %get-tuple-element.254), channel_id=1, source_target_pairs={{0,8},{8,0},{16,24},{24,16},{1,9},{9,1},{17,25},{25,17},{2,10},{10... | collective-permute-start | bytes 589832 | tf_op jit(solution)/shard_map/ppermute | solution.py:263
  29.7 26.3 %copy-start.6 = (f32[2,32,3072]{2,1,0:T(8,128)}, f32[2,32,3072]{2,1,0:T(8,128)S(1)}, u32[]{:S(2)}) copy-start(f32[2,32,3072]{2,1,0:T(8,128)S(1)} %collective-permute-done.25) | copy-start | bytes 2359300
  32.9 23.1 %copy-start.9 = (f32[2,32,3072]{2,1,0:T(8,128)}, f32[2,32,3072]{2,1,0:T(8,128)S(1)}, u32[]{:S(2)}) copy-start(f32[2,32,3072]{2,1,0:T(8,128)S(1)} %collective-permute-done.24) | copy-start | bytes 2359300
  34.7 17.5 %collective-permute-start.30 = (f32[2,2,32,3072]{3,2,0,1:T(8,128)S(1)}, f32[2,2,32,3072]{3,2,0,1:T(8,128)S(1)}, u32[]{:S(2)}, u32[]{:S(2)}) collective-permute-start(f32[2,2,32,3072]{3,2,0,1:T(8,128)S(1)} %pad_maximum_fusion.15), channel_id=1, source_target_pairs={{0,1},{1,0},{2,3},{3,2},{4,5},{5,4},{6,7},{7,6},{8,9},{9,8},{10,11... | collective-permute-start | bytes 4718600 | tf_op jit(solution)/shard_map/ppermute | solution.py:253
  35.9 10.5 %collective-permute-start.33 = (f32[16,1536]{1,0:T(8,128)S(1)}, f32[16,1536]{1,0:T(8,128)S(1)}, u32[]{:S(2)}, u32[]{:S(2)}) collective-permute-start(f32[16,1536]{1,0:T(8,128)S(1)} %get-tuple-element.260), channel_id=1, source_target_pairs={{0,6},{1,7},{2,4},{3,5},{4,2},{5,3},{6,0},{7,1},{8,14},{9,15},{10,... | collective-permute-start | bytes 294920 | tf_op jit(solution)/shard_map/ppermute | solution.py:258
  37.6 10.3 %collective-permute-start.32 = (f32[16,1536]{1,0:T(8,128)S(1)}, f32[16,1536]{1,0:T(8,128)S(1)}, u32[]{:S(2)}, u32[]{:S(2)}) collective-permute-start(f32[16,1536]{1,0:T(8,128)S(1)} %get-tuple-element.261), channel_id=1, source_target_pairs={{0,4},{1,5},{2,6},{3,7},{4,0},{5,1},{6,2},{7,3},{8,12},{9,13},{10,... | collective-permute-start | bytes 294920 | tf_op jit(solution)/shard_map/ppermute | solution.py:258
  38.9 13.3 %collective-permute-start.31 = (f32[16,1536]{1,0:T(8,128)S(1)}, f32[16,1536]{1,0:T(8,128)S(1)}, u32[]{:S(2)}, u32[]{:S(2)}) collective-permute-start(f32[16,1536]{1,0:T(8,128)S(1)} %get-tuple-element.262), channel_id=1, source_target_pairs={{0,2},{1,3},{2,0},{3,1},{4,6},{5,7},{6,4},{7,5},{8,10},{9,11},{10,... | collective-permute-start | bytes 294920 | tf_op jit(solution)/shard_map/ppermute | solution.py:258
  39.5 18.2 %copy-start = (f32[3072,1536]{1,0:T(8,128)S(1)}, f32[3072,1536]{1,0:T(8,128)}, u32[]{:S(2)}) copy-start(f32[3072,1536]{1,0:T(8,128)} %window_ref.5) | copy-start | bytes 56623108
  39.7 17.3 %collective-permute-start.39 = (f32[16,1536]{1,0:T(8,128)S(1)}, f32[16,1536]{1,0:T(8,128)S(1)}, u32[]{:S(2)}, u32[]{:S(2)}) collective-permute-start(f32[16,1536]{1,0:T(8,128)S(1)} %get-tuple-element.257), channel_id=1, source_target_pairs={{0,6},{1,7},{2,4},{3,5},{4,2},{5,3},{6,0},{7,1},{8,14},{9,15},{10,... | collective-permute-start | bytes 294920 | tf_op jit(solution)/shard_map/ppermute | solution.py:258
  46.4 23.3 %collective-permute-start.38 = (f32[16,1536]{1,0:T(8,128)S(1)}, f32[16,1536]{1,0:T(8,128)S(1)}, u32[]{:S(2)}, u32[]{:S(2)}) collective-permute-start(f32[16,1536]{1,0:T(8,128)S(1)} %get-tuple-element.258), channel_id=1, source_target_pairs={{0,4},{1,5},{2,6},{3,7},{4,0},{5,1},{6,2},{7,3},{8,12},{9,13},{10,... | collective-permute-start | bytes 294920 | tf_op jit(solution)/shard_map/ppermute | solution.py:258
  47.8 23.8 %collective-permute-start.37 = (f32[16,1536]{1,0:T(8,128)S(1)}, f32[16,1536]{1,0:T(8,128)S(1)}, u32[]{:S(2)}, u32[]{:S(2)}) collective-permute-start(f32[16,1536]{1,0:T(8,128)S(1)} %get-tuple-element.259), channel_id=1, source_target_pairs={{0,2},{1,3},{2,0},{3,1},{4,6},{5,7},{6,4},{7,5},{8,10},{9,11},{10,... | collective-permute-start | bytes 294920 | tf_op jit(solution)/shard_map/ppermute | solution.py:258
  52.9 22.7 %collective-permute-start.36 = (f32[4,16,1536]{2,1,0:T(8,128)S(1)}, f32[4,16,1536]{2,1,0:T(8,128)S(1)}, u32[]{:S(2)}, u32[]{:S(2)}) collective-permute-start(f32[4,16,1536]{2,1,0:T(8,128)S(1)} %bitcast_dynamic-update-slice_fusion.15), channel_id=1, source_target_pairs={{0,24},{8,16},{16,8},{24,0},{1,25},{9,17},{17,9},{25,1},{2,26},{10... | collective-permute-start | bytes 1179656 | tf_op jit(solution)/shard_map/ppermute | solution.py:263
  55.5 20.2 %collective-permute-start.35 = (f32[4,16,1536]{2,1,0:T(8,128)S(1)}, f32[4,16,1536]{2,1,0:T(8,128)S(1)}, u32[]{:S(2)}, u32[]{:S(2)}) collective-permute-start(f32[4,16,1536]{2,1,0:T(8,128)S(1)} %bitcast_dynamic-update-slice_fusion.15), channel_id=1, source_target_pairs={{0,16},{8,24},{16,0},{24,8},{1,17},{9,25},{17,1},{25,9},{2,18},{10... | collective-permute-start | bytes 1179656 | tf_op jit(solution)/shard_map/ppermute | solution.py:263
  57.0 18.7 %collective-permute-start.34 = (f32[4,16,1536]{2,1,0:T(8,128)S(1)}, f32[4,16,1536]{2,1,0:T(8,128)S(1)}, u32[]{:S(2)}, u32[]{:S(2)}) collective-permute-start(f32[4,16,1536]{2,1,0:T(8,128)S(1)} %bitcast_dynamic-update-slice_fusion.15), channel_id=1, source_target_pairs={{0,8},{8,0},{16,24},{24,16},{1,9},{9,1},{17,25},{25,17},{2,10},{10... | collective-permute-start | bytes 1179656 | tf_op jit(solution)/shard_map/ppermute | solution.py:263
  57.7 11.9 %copy-start.10 = (f32[2,32,3072]{2,1,0:T(8,128)S(1)}, f32[2,32,3072]{2,1,0:T(8,128)}, u32[]{:S(2)}) copy-start(f32[2,32,3072]{2,1,0:T(8,128)} %copy-done.9) | copy-start | bytes 2359300
  57.7 13.8 %copy-start.7 = (f32[2,32,3072]{2,1,0:T(8,128)S(1)}, f32[2,32,3072]{2,1,0:T(8,128)}, u32[]{:S(2)}) copy-start(f32[2,32,3072]{2,1,0:T(8,128)} %copy-done.6) | copy-start | bytes 2359300
  69.7 21.4 %collective-permute-start.43 = (f32[2,32,3072]{2,1,0:T(8,128)S(1)}, f32[2,32,3072]{2,1,0:T(8,128)S(1)}, u32[]{:S(2)}, u32[]{:S(2)}) collective-permute-start(f32[2,32,3072]{2,1,0:T(8,128)S(1)} %copy-done.10), channel_id=1, source_target_pairs={{2,0},{3,1},{4,2},{5,3},{10,8},{11,9},{12,10},{13,11},{18,16},{19,... | collective-permute-start | bytes 2359304 | tf_op jit(solution)/shard_map/ppermute | solution.py:302
  71.6 21.7 %collective-permute-start.44 = (f32[2,32,3072]{2,1,0:T(8,128)S(1)}, f32[2,32,3072]{2,1,0:T(8,128)S(1)}, u32[]{:S(2)}, u32[]{:S(2)}) collective-permute-start(f32[2,32,3072]{2,1,0:T(8,128)S(1)} %copy-done.7), channel_id=1, source_target_pairs={{2,4},{3,5},{4,6},{5,7},{10,12},{11,13},{12,14},{13,15},{18,20},{1... | collective-permute-start | bytes 2359304 | tf_op jit(solution)/shard_map/ppermute | solution.py:302
  75.7 19.1 %collective-permute-start.42 = (f32[4,16,1536]{2,1,0:T(8,128)S(1)}, f32[4,16,1536]{2,1,0:T(8,128)S(1)}, u32[]{:S(2)}, u32[]{:S(2)}) collective-permute-start(f32[4,16,1536]{2,1,0:T(8,128)S(1)} %bitcast_dynamic-update-slice_fusion.11), channel_id=1, source_target_pairs={{0,24},{8,16},{16,8},{24,0},{1,25},{9,17},{17,9},{25,1},{2,26},{10... | collective-permute-start | bytes 1179656 | tf_op jit(solution)/shard_map/ppermute | solution.py:263
  78.2 18.1 %collective-permute-start.41 = (f32[4,16,1536]{2,1,0:T(8,128)S(1)}, f32[4,16,1536]{2,1,0:T(8,128)S(1)}, u32[]{:S(2)}, u32[]{:S(2)}) collective-permute-start(f32[4,16,1536]{2,1,0:T(8,128)S(1)} %bitcast_dynamic-update-slice_fusion.11), channel_id=1, source_target_pairs={{0,16},{8,24},{16,0},{24,8},{1,17},{9,25},{17,1},{25,9},{2,18},{10... | collective-permute-start | bytes 1179656 | tf_op jit(solution)/shard_map/ppermute | solution.py:263
  78.7 17.5 %collective-permute-start.40 = (f32[4,16,1536]{2,1,0:T(8,128)S(1)}, f32[4,16,1536]{2,1,0:T(8,128)S(1)}, u32[]{:S(2)}, u32[]{:S(2)}) collective-permute-start(f32[4,16,1536]{2,1,0:T(8,128)S(1)} %bitcast_dynamic-update-slice_fusion.11), channel_id=1, source_target_pairs={{0,8},{8,0},{16,24},{24,16},{1,9},{9,1},{17,25},{25,17},{2,10},{10... | collective-permute-start | bytes 1179656 | tf_op jit(solution)/shard_map/ppermute | solution.py:263
  79.4 10.7 %copy-start.15 = (f32[128,1536]{1,0:T(8,128)}, f32[128,1536]{1,0:T(8,128)S(1)}, u32[]{:S(2)}) copy-start(f32[128,1536]{1,0:T(8,128)S(1)} %get-tuple-element.244) | copy-start | bytes 2359300
  91.1 5.3 %copy-start.28 = (f32[2,32,3072]{2,1,0:T(8,128)}, f32[2,32,3072]{2,1,0:T(8,128)S(1)}, u32[]{:S(2)}) copy-start(f32[2,32,3072]{2,1,0:T(8,128)S(1)} %collective-permute-done.43) | copy-start | bytes 2359300
  91.1 15.0 %collective-permute-start.45 = (f32[2,32,3072]{2,1,0:T(8,128)}, f32[2,32,3072]{2,1,0:T(8,128)}, u32[]{:S(2)}, u32[]{:S(2)}) collective-permute-start(f32[2,32,3072]{2,1,0:T(8,128)} %broadcast_select_fusion.9), channel_id=1, source_target_pairs={{4,0},{5,1},{2,6},{3,7},{12,8},{13,9},{10,14},{11,15},{20,16},{21,... | collective-permute-start | bytes 2359304 | tf_op jit(solution)/shard_map/ppermute | solution.py:393
  93.3 12.8 %collective-permute-start.46 = (f32[64,1536]{1,0:T(8,128)}, f32[64,1536]{1,0:T(8,128)S(1)}, u32[]{:S(2)}, u32[]{:S(2)}) collective-permute-start(f32[64,1536]{1,0:T(8,128)} %constant_dynamic-slice_fusion.10), channel_id=1, source_target_pairs={{0,8},{8,0},{16,24},{24,16},{1,9},{9,1},{17,25},{25,17},{2,10},{10... | collective-permute-start | bytes 1179656 | tf_op jit(solution)/shard_map/ppermute | solution.py:263
  94.8 11.3 %collective-permute-start.47 = (f32[64,1536]{1,0:T(8,128)}, f32[64,1536]{1,0:T(8,128)}, u32[]{:S(2)}, u32[]{:S(2)}) collective-permute-start(f32[64,1536]{1,0:T(8,128)} %constant_dynamic-slice_fusion.11), channel_id=1, source_target_pairs={{0,16},{8,24},{16,0},{24,8},{1,17},{9,25},{17,1},{25,9},{2,18},{10... | collective-permute-start | bytes 1179656 | tf_op jit(solution)/shard_map/ppermute | solution.py:263
  115.1 5.2 %collective-permute-start = (f32[2,2,32,3072]{3,2,0,1:T(8,128)}, f32[2,2,32,3072]{3,2,0,1:T(8,128)}, u32[]{:S(2)}, u32[]{:S(2)}) collective-permute-start(f32[2,2,32,3072]{3,2,0,1:T(8,128)} %get-tuple-element.66), channel_id=1, source_target_pairs={{0,1},{1,0},{2,3},{3,2},{4,5},{5,4},{6,7},{7,6},{8,9},{9,8},{10,11... | collective-permute-start | bytes 4718600 | tf_op jit(solution)/shard_map/cond/branch_1_fun/ppermute | solution.py:253
  117.7 38.3 %collective-permute-start.3 = (f32[32,1536]{1,0:T(8,128)}, f32[32,1536]{1,0:T(8,128)}, u32[]{:S(2)}, u32[]{:S(2)}) collective-permute-start(f32[32,1536]{1,0:T(8,128)} %constant_dynamic-slice_fusion.7), channel_id=1, source_target_pairs={{0,16},{8,24},{16,0},{24,8},{1,17},{9,25},{17,1},{25,9},{2,18},{10... | collective-permute-start | bytes 589832 | tf_op jit(solution)/shard_map/cond/branch_1_fun/ppermute | solution.py:263
  120.3 17.8 %copy-start.21 = (f32[64,1536]{1,0:T(8,128)}, f32[64,1536]{1,0:T(8,128)S(1)}, u32[]{:S(2)}) copy-start(f32[64,1536]{1,0:T(8,128)S(1)} %dynamic-slice_add_fusion.2) | copy-start | bytes 1179652 | tf_op jit(solution)/shard_map/cond
  135.1 20.9 %collective-permute-start.1 = (f32[128,512]{1,0:T(8,128)}, f32[128,512]{1,0:T(8,128)}, u32[]{:S(2)}, u32[]{:S(2)}) collective-permute-start(f32[128,512]{1,0:T(8,128)} %constant_dynamic-slice_fusion.9), channel_id=1, source_target_pairs={{0,8},{8,0},{16,24},{24,16},{1,9},{9,1},{17,25},{25,17},{2,10},{10... | collective-permute-start | bytes 786440 | tf_op jit(solution)/shard_map/cond/branch_1_fun/ppermute | solution.py:263
  136.1 19.9 %collective-permute-start.2 = (f32[128,512]{1,0:T(8,128)}, f32[128,512]{1,0:T(8,128)}, u32[]{:S(2)}, u32[]{:S(2)}) collective-permute-start(f32[128,512]{1,0:T(8,128)} %constant_dynamic-slice_fusion.8), channel_id=1, source_target_pairs={{0,16},{8,24},{16,0},{24,8},{1,17},{9,25},{17,1},{25,9},{2,18},{10... | collective-permute-start | bytes 786440 | tf_op jit(solution)/shard_map/cond/branch_1_fun/ppermute | solution.py:263
  138.8 17.2 %collective-permute-start.4 = (f32[32,1536]{1,0:T(8,128)}, f32[32,1536]{1,0:T(8,128)}, u32[]{:S(2)}, u32[]{:S(2)}) collective-permute-start(f32[32,1536]{1,0:T(8,128)} %constant_dynamic-slice_fusion.6), channel_id=1, source_target_pairs={{0,8},{8,0},{16,24},{24,16},{1,9},{9,1},{17,25},{25,17},{2,10},{10... | collective-permute-start | bytes 589832 | tf_op jit(solution)/shard_map/cond/branch_1_fun/ppermute | solution.py:263
  139.3 16.7 %copy-start.20 = (f32[256,512]{1,0:T(8,128)S(1)}, f32[256,512]{1,0:T(8,128)}, u32[]{:S(2)}) copy-start(f32[256,512]{1,0:T(8,128)} %copy-done.19) | copy-start | bytes 1572868 | tf_op jit(solution)/shard_map/cond
  139.3 19.1 %copy-start.18 = (f32[256,512]{1,0:T(8,128)S(1)}, f32[256,512]{1,0:T(8,128)}, u32[]{:S(2)}) copy-start(f32[256,512]{1,0:T(8,128)} %copy-done.17) | copy-start | bytes 1572868 | tf_op jit(solution)/shard_map/cond
  157.1 8.9 %collective-permute-start.5 = (f32[64,512]{1,0:T(8,128)S(1)}, f32[64,512]{1,0:T(8,128)S(1)}, u32[]{:S(2)}, u32[]{:S(2)}) collective-permute-start(f32[64,512]{1,0:T(8,128)S(1)} %constant_dynamic-slice_fusion.5), channel_id=1, source_target_pairs={{0,16},{8,24},{16,0},{24,8},{1,17},{9,25},{17,1},{25,9},{2,18},{10... | collective-permute-start | bytes 393224 | tf_op jit(solution)/shard_map/cond/branch_1_fun/ppermute | solution.py:263
  159.4 6.6 %collective-permute-start.6 = (f32[64,512]{1,0:T(8,128)S(1)}, f32[64,512]{1,0:T(8,128)S(1)}, u32[]{:S(2)}, u32[]{:S(2)}) collective-permute-start(f32[64,512]{1,0:T(8,128)S(1)} %constant_dynamic-slice_fusion.4), channel_id=1, source_target_pairs={{0,8},{8,0},{16,24},{24,16},{1,9},{9,1},{17,25},{25,17},{2,10},{10... | collective-permute-start | bytes 393224 | tf_op jit(solution)/shard_map/cond/branch_1_fun/ppermute | solution.py:263
  160.7 36.5 %collective-permute-start.14 = (f32[256,256]{1,0:T(8,128)S(1)}, f32[256,256]{1,0:T(8,128)S(1)}, u32[]{:S(2)}, u32[]{:S(2)}) collective-permute-start(f32[256,256]{1,0:T(8,128)S(1)} %pad_maximum_fusion.10), channel_id=1, source_target_pairs={{0,8},{8,0},{16,24},{24,16},{1,9},{9,1},{17,25},{25,17},{2,10},{10... | collective-permute-start | bytes 786440 | tf_op jit(solution)/shard_map/cond/branch_1_fun/ppermute | solution.py:263
  162.7 14.6 %collective-permute-start.7 = (f32[64,1536]{1,0:T(8,128)S(1)}, f32[64,1536]{1,0:T(8,128)S(1)}, u32[]{:S(2)}, u32[]{:S(2)}) collective-permute-start(f32[64,1536]{1,0:T(8,128)S(1)} %constant_dynamic-slice_fusion.3), channel_id=1, source_target_pairs={{0,8},{8,0},{16,24},{24,16},{1,9},{9,1},{17,25},{25,17},{2,10},{10... | collective-permute-start | bytes 1179656 | tf_op jit(solution)/shard_map/cond/branch_1_fun/ppermute | solution.py:263
  163.3 14.1 %collective-permute-start.8 = (f32[64,1536]{1,0:T(8,128)S(1)}, f32[64,1536]{1,0:T(8,128)S(1)}, u32[]{:S(2)}, u32[]{:S(2)}) collective-permute-start(f32[64,1536]{1,0:T(8,128)S(1)} %constant_dynamic-slice_fusion.2), channel_id=1, source_target_pairs={{0,16},{8,24},{16,0},{24,8},{1,17},{9,25},{17,1},{25,9},{2,18},{10... | collective-permute-start | bytes 1179656 | tf_op jit(solution)/shard_map/cond/branch_1_fun/ppermute | solution.py:263
  177.5 5.7 %collective-permute-start.11 = (f32[32,1536]{1,0:T(8,128)S(1)}, f32[32,1536]{1,0:T(8,128)S(1)}, u32[]{:S(2)}, u32[]{:S(2)}) collective-permute-start(f32[32,1536]{1,0:T(8,128)S(1)} %constant_dynamic-slice_fusion), channel_id=1, source_target_pairs={{0,8},{8,0},{16,24},{24,16},{1,9},{9,1},{17,25},{25,17},{2,10},{10... | collective-permute-start | bytes 589832 | tf_op jit(solution)/shard_map/cond/branch_1_fun/ppermute | solution.py:263
  178.9 5.7 %collective-permute-start.10 = (f32[32,1536]{1,0:T(8,128)S(1)}, f32[32,1536]{1,0:T(8,128)S(1)}, u32[]{:S(2)}, u32[]{:S(2)}) collective-permute-start(f32[32,1536]{1,0:T(8,128)S(1)} %constant_dynamic-slice_fusion.1), channel_id=1, source_target_pairs={{0,16},{8,24},{16,0},{24,8},{1,17},{9,25},{17,1},{25,9},{2,18},{10... | collective-permute-start | bytes 589832 | tf_op jit(solution)/shard_map/cond/branch_1_fun/ppermute | solution.py:263
  179.8 4.8 %collective-permute-start.9 = (f32[128,512]{1,0:T(8,128)S(1)}, f32[128,512]{1,0:T(8,128)S(1)}, u32[]{:S(2)}, u32[]{:S(2)}) collective-permute-start(f32[128,512]{1,0:T(8,128)S(1)} %pad_maximum_fusion.9), channel_id=1, source_target_pairs={{0,1},{1,0},{2,3},{3,2},{4,5},{5,4},{6,7},{7,6},{8,9},{9,8},{10,11... | collective-permute-start | bytes 786440 | tf_op jit(solution)/shard_map/cond/branch_1_fun/ppermute | solution.py:253
  184.7 8.6 %collective-permute-start.13 = (f32[2,32,1536]{2,1,0:T(8,128)S(1)}, f32[2,32,1536]{2,1,0:T(8,128)S(1)}, u32[]{:S(2)}, u32[]{:S(2)}) collective-permute-start(f32[2,32,1536]{2,1,0:T(8,128)S(1)} %pad_maximum_fusion.8), channel_id=1, source_target_pairs={{0,8},{8,0},{16,24},{24,16},{1,9},{9,1},{17,25},{25,17},{2,10},{10... | collective-permute-start | bytes 1179656 | tf_op jit(solution)/shard_map/cond/branch_1_fun/ppermute | solution.py:263
  185.5 9.8 %copy-start.27 = (f32[128,512]{1,0:T(8,128)}, f32[128,512]{1,0:T(8,128)S(1)}, u32[]{:S(2)}) copy-start(f32[128,512]{1,0:T(8,128)S(1)} %fusion.15) | copy-start | bytes 786436 | tf_op jit(solution)/shard_map/cond
  185.5 15.4 %collective-permute-start.15 = (f32[128,512]{1,0:T(8,128)S(1)}, f32[128,512]{1,0:T(8,128)S(1)}, u32[]{:S(2)}, u32[]{:S(2)}) collective-permute-start(f32[128,512]{1,0:T(8,128)S(1)} %fusion.15), channel_id=1, source_target_pairs={{0,2},{1,3},{6,4},{7,5},{8,10},{9,11},{14,12},{15,13},{16,18},{17,... | collective-permute-start | bytes 786440 | tf_op jit(solution)/shard_map/cond/branch_1_fun/ppermute | solution.py:426
  186.9 8.4 %collective-permute-start.12 = (f32[2,32,1536]{2,1,0:T(8,128)S(1)}, f32[2,32,1536]{2,1,0:T(8,128)S(1)}, u32[]{:S(2)}, u32[]{:S(2)}) collective-permute-start(f32[2,32,1536]{2,1,0:T(8,128)S(1)} %pad_maximum_fusion.7), channel_id=1, source_target_pairs={{0,16},{8,24},{16,0},{24,8},{1,17},{9,25},{17,1},{25,9},{2,18},{10... | collective-permute-start | bytes 1179656 | tf_op jit(solution)/shard_map/cond/branch_1_fun/ppermute | solution.py:263
  196.3 7.8 %copy-start.24 = (f32[128,256]{1,0:T(8,128)S(1)}, f32[128,256]{1,0:T(8,128)}, u32[]{:S(2)}) copy-start(f32[128,256]{1,0:T(8,128)} %copy-done.23) | copy-start | bytes 393220 | tf_op jit(solution)/shard_map/cond
  196.3 7.8 %copy-start.26 = (f32[128,256]{1,0:T(8,128)S(1)}, f32[128,256]{1,0:T(8,128)}, u32[]{:S(2)}) copy-start(f32[128,256]{1,0:T(8,128)} %copy-done.25) | copy-start | bytes 393220 | tf_op jit(solution)/shard_map/cond
  201.6 16.3 %collective-permute-start.16 = (f32[2,64,1536]{2,1,0:T(8,128)}, f32[2,64,1536]{2,1,0:T(8,128)}, u32[]{:S(2)}, u32[]{:S(2)}) collective-permute-start(f32[2,64,1536]{2,1,0:T(8,128)} %pad_maximum_fusion.5), channel_id=1, source_target_pairs={{0,8},{8,0},{16,24},{24,16},{1,9},{9,1},{17,25},{25,17},{2,10},{10... | collective-permute-start | bytes 2359304 | tf_op jit(solution)/shard_map/cond/branch_1_fun/ppermute | solution.py:263
  205.0 22.5 %collective-permute-start.18 = (f32[256,256]{1,0:T(8,128)S(1)}, f32[256,256]{1,0:T(8,128)S(1)}, u32[]{:S(2)}, u32[]{:S(2)}) collective-permute-start(f32[256,256]{1,0:T(8,128)S(1)} %fusion.14), channel_id=1, source_target_pairs={{0,16},{8,24},{16,0},{24,8},{1,17},{9,25},{17,1},{25,9},{2,18},{10... | collective-permute-start | bytes 786440 | tf_op jit(solution)/shard_map/cond/branch_1_fun/ppermute | solution.py:263
  205.8 21.7 %collective-permute-start.19 = (f32[128,512]{1,0:T(8,128)S(1)}, f32[128,512]{1,0:T(8,128)S(1)}, u32[]{:S(2)}, u32[]{:S(2)}) collective-permute-start(f32[128,512]{1,0:T(8,128)S(1)} %add.254), channel_id=1, source_target_pairs={{2,4},{3,5},{4,2},{5,3},{10,12},{11,13},{12,10},{13,11},{18,20},{1... | collective-permute-start | bytes 786440 | tf_op jit(solution)/shard_map/cond/branch_1_fun/ppermute | solution.py:426
  208.8 18.5 %collective-permute-start.17 = (f32[2,64,1536]{2,1,0:T(8,128)}, f32[2,64,1536]{2,1,0:T(8,128)S(1)}, u32[]{:S(2)}, u32[]{:S(2)}) collective-permute-start(f32[2,64,1536]{2,1,0:T(8,128)} %pad_maximum_fusion.6), channel_id=1, source_target_pairs={{0,16},{8,24},{16,0},{24,8},{1,17},{9,25},{17,1},{25,9},{2,18},{10... | collective-permute-start | bytes 2359304 | tf_op jit(solution)/shard_map/cond/branch_1_fun/ppermute | solution.py:263
  219.4 7.9 %copy-start.16 = (f32[2,64,1536]{2,1,0:T(8,128)S(1)}, f32[2,64,1536]{2,1,0:T(8,128)}, u32[]{:S(2)}) copy-start(f32[2,64,1536]{2,1,0:T(8,128)} %pad_maximum_fusion.6) | copy-start | bytes 2359300 | tf_op jit(solution)/shard_map/cond
  227.7 12.1 %collective-permute-start.20 = (f32[128,512]{1,0:T(8,128)S(1)}, f32[128,512]{1,0:T(8,128)S(1)}, u32[]{:S(2)}, u32[]{:S(2)}) collective-permute-start(f32[128,512]{1,0:T(8,128)S(1)} %add.256), channel_id=1, source_target_pairs={{2,0},{3,1},{4,6},{5,7},{10,8},{11,9},{12,14},{13,15},{18,16},{19,... | collective-permute-start | bytes 786440 | tf_op jit(solution)/shard_map/cond/branch_1_fun/ppermute | solution.py:426
  239.9 10.6 %collective-permute-start.23 = (f32[128,512]{1,0:T(8,128)S(1)}, f32[128,512]{1,0:T(8,128)S(1)}, u32[]{:S(2)}, u32[]{:S(2)}) collective-permute-start(f32[128,512]{1,0:T(8,128)S(1)} %broadcast_select_fusion.8), channel_id=1, source_target_pairs={{0,24},{8,16},{16,8},{24,0},{1,25},{9,17},{17,9},{25,1},{2,26},{10... | collective-permute-start | bytes 786440 | tf_op jit(solution)/shard_map/cond/branch_1_fun/ppermute | solution.py:263
  241.3 9.1 %collective-permute-start.22 = (f32[128,512]{1,0:T(8,128)S(1)}, f32[128,512]{1,0:T(8,128)S(1)}, u32[]{:S(2)}, u32[]{:S(2)}) collective-permute-start(f32[128,512]{1,0:T(8,128)S(1)} %broadcast_select_fusion.8), channel_id=1, source_target_pairs={{0,16},{8,24},{16,0},{24,8},{1,17},{9,25},{17,1},{25,9},{2,18},{10... | collective-permute-start | bytes 786440 | tf_op jit(solution)/shard_map/cond/branch_1_fun/ppermute | solution.py:263
  242.5 7.4 %collective-permute-start.21 = (f32[128,512]{1,0:T(8,128)S(1)}, f32[128,512]{1,0:T(8,128)S(1)}, u32[]{:S(2)}, u32[]{:S(2)}) collective-permute-start(f32[128,512]{1,0:T(8,128)S(1)} %broadcast_select_fusion.8), channel_id=1, source_target_pairs={{0,8},{8,0},{16,24},{24,16},{1,9},{9,1},{17,25},{25,17},{2,10},{10... | collective-permute-start | bytes 786440 | tf_op jit(solution)/shard_map/cond/branch_1_fun/ppermute | solution.py:263
  (27 other events, 61.1 us)
Sparse Core Ops, SparseCore 0:
  106.3 144.9 all-reduce.2

commit v5 on v4

--- a/solution.py
+++ b/solution.py
@@ -207,28 +207,39 @@
     )(lower.astype(jnp.int32).reshape(1), projected, columns, factors, *inner)
 
 
-def finish_kernel(
-    window_ref, near_ref, far_ref, local_ref, crossed_ref, left_ref, right_high, right_low, *refs
+def weights_kernel(
+    local_ref, crossed_ref, left_ref, right_high, right_low, high_ref, low_ref
 ):
-    *image_refs, out_ref, high_ref, low_ref = refs
     width = left_ref.shape[0]
-
-    @pl.when(pl.program_id(0) == 0)
-    def _():
-        middle = three_products(halves(local_ref[...]), halves(crossed_ref[...]), 0, 0)
-        left = left_ref[...] - three_products(halves(middle), (right_high[...], right_low[...]))
-        high_ref[:width], low_ref[:width] = halves(left)
-        high_ref[width:], low_ref[width:] = right_high[...], right_low[...]
-
+    middle = three_products(halves(local_ref[...]), halves(crossed_ref[...]), 0, 0)
+    left = left_ref[...] - three_products(halves(middle), (right_high[...], right_low[...]))
+    high_ref[:width], low_ref[:width] = halves(left)
+    high_ref[width:], low_ref[width:] = right_high[...], right_low[...]
+
+
+def weights(local, crossed, left, right):
+    width, cols = left.shape
+    return call(
+        weights_kernel,
+        30,
+        (),
+        [pl.BlockSpec(memory_space=pltpu.VMEM)] * 5,
+        [pl.BlockSpec(memory_space=pltpu.VMEM)] * 2,
+        [jax.ShapeDtypeStruct((2 * width, cols), bf16)] * 2,
+    )(local, crossed, left, *right)
+
+
+def finish_kernel(window_ref, near_ref, far_ref, high_ref, low_ref, *refs):
+    *image_refs, out_ref = refs
     both = jnp.concatenate(
         [near_ref[...].T, far_ref[...].T] + [one[...] for one in image_refs], 1
     )
     out_ref[...] = window_ref[...] - three_products(halves(both), (high_ref[...], low_ref[...]))
 
 
-def finish(window, near, far, local, crossed, left, right, images, block=512):
+def finish(window, near, far, high, low, images, block=512):
     rows, cols = window.shape
-    part, width = near.shape[0], local.shape[0]
+    part, width = near.shape[0], high.shape[0]
     block = min(block, rows)
     return call(
         finish_kernel,
@@ -239,13 +250,11 @@
             pl.BlockSpec((part, block), lambda i: (0, i)),
             pl.BlockSpec((part, block), lambda i: (0, i)),
         ]
-        + [pl.BlockSpec((width, width), lambda i: (0, 0))] * 2
-        + [pl.BlockSpec((width, cols), lambda i: (0, 0))] * 3
+        + [pl.BlockSpec((width, cols), lambda i: (0, 0))] * 2
         + [pl.BlockSpec((block, one.shape[1]), lambda i: (i, 0)) for one in images],
         pl.BlockSpec((block, cols), lambda i: (i, 0)),
         jax.ShapeDtypeStruct((rows, cols), f32),
-        [pltpu.VMEM((2 * width, cols), bf16)] * 2,
-    )(window, near, far, local, crossed, left, *right, *images)
+    )(window, near, far, high, low, *images)
 
 
 def swap_cores(value):
@@ -314,10 +323,9 @@
 def both_cores(mine, other):
     core = lax.axis_index("col") % 2
     pairs = []
-    for place in range(mine.shape[1]):
-        one, two = mine[:, place], other[:, place]
+    for one, two in zip(mine, other):
         pairs += [jnp.where(core == 0, one, two), jnp.where(core == 0, two, one)]
-    return jnp.concatenate(pairs, 1).reshape(-1, mine.shape[-1])
+    return jnp.concatenate(pairs, 1).reshape(-1, mine[0].shape[-1])
 
 
 def gather_vectors(slivers, row_count, chips, window):
@@ -366,6 +374,9 @@
         return whole.reshape(2 * chips * piece, cols)
 
     other, arrived = together(swap_cores(near), along_line(0))
+    near, other = (
+        [value[:, place] for place in range(half)] for value in (near, other)
+    )
     near = both_cores(near, other)
     shares = [line_shares(0, arrived)]
     last = (held[half - 1], held[1 - half])
@@ -472,20 +483,16 @@
     )
     held[chips - 1], held[1 - chips] = ends, ends
     half = chips // 2
-    far = jnp.stack(
-        [
-            by_chip(lambda one: held[(1 - one // half) * half + place - one])
-            for place in range(half)
-        ],
-        1,
-    )
+    far = [
+        by_chip(lambda one: held[(1 - one // half) * half + place - one]) for place in range(half)
+    ]
     images.append(last_image)
     near_parts = [one + kept for one, (_, kept) in zip(arrived, steps)]
     summed = [lax.psum(one, "col") for one in images]
     columns = jnp.concatenate(columns, 0)
 
     def factors_of(window, near, far, same, columns, factors, images, near_parts):
-        far = both_cores(far, swap_cores(far))
+        far = both_cores(far, [swap_cores(one) for one in far])
         crossed = cross(near, far, images)
         crossed = ordered(lower, crossed[: total // 2], crossed[total // 2 :], 0)
         sums = [crossed[: total // 2], crossed[total // 2 :]]
@@ -569,12 +576,12 @@
         crossed = jnp.concatenate(
             [crossed[other, panel] for panel in range(panels) for other in range(2)], 0
         )
-        return far, local, crossed, left, right
-
-    far, local, crossed, left, right = region(
+        return far, *weights(local, crossed, left, right)
+
+    far, high, low = region(
         factors_of, window, near, far, same, columns, factors, images, near_parts
     )
-    return finish(window, near, far, local, crossed, left, right, summed)
+    return finish(window, near, far, high, low, summed)
 
 
 def solution(mesh):

time: 304 us -> 302 us (level)
  waiting for transfers between devices: 69.1 us -> 80.6 us
  other arithmetic: 31 us -> 23.2 us
  local copies, waits for them, and re-layouts: 15.9 us -> 12.2 us
    pallas_call x0 -> x1, Pallas kernels: none -> 6.28 us  [weights(): call(weights_kernel, 30, (), [pl.BlockSpec(memory_space=pltpu.VMEM)] * 5,...]
    pallas_call x1, Pallas kernels: 41.2 us -> 37.3 us  [finish(): call(finish_kernel, 52, (rows // block,), [pl.BlockSpec((block, cols), la...]
    ppermute x30, waiting for transfers between devices: 53 us -> 56.2 us  [swap_rows(): lax.ppermute(value, 'row', [(row, row ^ distance) for row in range(count)])]
    ppermute x3, waiting for transfers between devices: 4.36 us -> 7.42 us  [line_step(): lax.ppermute(value, 'col', [(2 * one + core, 2 * two + core) for one, two...]
  transfers between devices with their start and end apart: 49 -> 50, of which waited for: 18 -> 20; matrix products, arithmetic and copies ran while one was open for 12% -> 9% of each run, Pallas kernels for 21% -> 23%
where the time goes in v5:
time: 302 us; the launch traced here: 298 us
  Pallas kernels  105 us (35%)
  waiting for transfers between devices  80.6 us (27%)
  starting transfers between devices  62.3 us (21%)
  other arithmetic  23.2 us (8%)
  between operations  13.9 us (5%)
  local copies, waits for them, and re-layouts  12.2 us (4%)
    ppermute x30, waiting for transfers between devices, swap_rows(): lax.ppermute(value, 'row', [(row, row ^ distance) for row in range(count)])  56.2 us
    pallas_call x1, Pallas kernels, finish(): call(finish_kernel, 52, (rows // block,), [pl.BlockSpec((block, cols), la...  37.3 us
    ppermute x30, starting transfers between devices, swap_rows(): lax.ppermute(value, 'row', [(row, row ^ distance) for row in range(count)])  33.4 us
    pallas_call x2, Pallas kernels, project(): call(functools.partial(project_kernel, pairs, len(vectors)), 36, (cols //...  28.6 us
    pallas_call x2, Pallas kernels, image(): call(image_kernel, 22, (rows // block,), [pl.BlockSpec((block, cols), lam...  19.2 us
    ppermute x4, starting transfers between devices, send_along(): lax.ppermute(value, 'col', [(2 * (chip - step) + core, 2 * chip + core) f...  12.7 us
    ppermute x6, waiting for transfers between devices, swap_chips(): lax.ppermute(value, 'col', [(col, col ^ 2 * distance) for col in range(co...  9.29 us
    ppermute x6, starting transfers between devices, swap_chips(): lax.ppermute(value, 'col', [(col, col ^ 2 * distance) for col in range(co...  8.21 us
  transfers between devices with their start and end apart: 50, of which 20 were waited for; matrix products, arithmetic and copies ran while one was open for 9% of the time, Pallas kernels for 23%

profile of v5, /device:TPU:8, one launch (start us, length us, event | category | flops | bytes accessed | tf_op | source)
XLA Modules:
  0.0 297.6 jit_solution(13980166280644954770)
XLA Ops:
  6.5 1.0 dynamic-slice_bitcast_fusion
  7.6 3.5 %collective-permute-start.26 = (f32[2,32,3072]{2,1,0:T(8,128)}, f32[2,32,3072]{2,1,0:T(8,128)}, u32[]{:S(2)}, u32[]{:S(2)}) collective-permute-start(f32[2,32,3072]{2,1,0:T(8,128)} %bitcast.154), channel_id=1, source_target_pairs={{0,2},{1,3},{2,4},{3,5},{4,6},{5,7},{8,10},{9,11},{10,12},{11,13},... | collective-permute-start | bytes 2359304 | tf_op jit(solution)/shard_map/ppermute | solution.py:311
  11.1 3.3 %collective-permute-start.25 = (f32[2,32,3072]{2,1,0:T(8,128)}, f32[2,32,3072]{2,1,0:T(8,128)}, u32[]{:S(2)}, u32[]{:S(2)}) collective-permute-start(f32[2,32,3072]{2,1,0:T(8,128)} %bitcast.155), channel_id=1, source_target_pairs={{2,0},{3,1},{4,2},{5,3},{6,4},{7,5},{10,8},{11,9},{12,10},{13,11},... | collective-permute-start | bytes 2359304 | tf_op jit(solution)/shard_map/ppermute | solution.py:311
  14.4 1.1 bitcast_select_fusion.5
  15.7 2.5 collective-permute-start.30
  19.3 5.2 %collective-permute-done.30 = f32[2,16,1536]{2,1,0:T(8,128)S(1)} collective-permute-done((f32[2,16,1536]{2,1,0:T(8,128)S(1)}, f32[2,16,1536]{2,1,0:T(8,128)S(1)}, u32[]{:S(2)}, u32[]{:S(2)}) %collective-permute-start.30) | collective-permute-done | bytes 196640 | tf_op jit(solution)/shard_map/ppermute | solution.py:272
  24.5 3.1 %collective-permute-done.29 = f32[2,16,1536]{2,1,0:T(8,128)S(1)} collective-permute-done((f32[2,16,1536]{2,1,0:T(8,128)S(1)}, f32[2,16,1536]{2,1,0:T(8,128)S(1)}, u32[]{:S(2)}, u32[]{:S(2)}) %collective-permute-start.29) | collective-permute-done | bytes 196640 | tf_op jit(solution)/shard_map/ppermute | solution.py:272
  27.8 2.0 collective-permute-done.26
  29.8 3.2 %collective-permute-done.25 = f32[2,32,3072]{2,1,0:T(8,128)} collective-permute-done((f32[2,32,3072]{2,1,0:T(8,128)}, f32[2,32,3072]{2,1,0:T(8,128)}, u32[]{:S(2)}, u32[]{:S(2)}) %collective-permute-start.25) | collective-permute-done | bytes 786464 | tf_op jit(solution)/shard_map/ppermute | solution.py:311
  33.0 1.6 fusion.13
  35.0 1.6 collective-permute-start.34
  36.6 2.1 collective-permute-start.33
  38.9 1.4 collective-permute-start.40
  40.3 4.5 %collective-permute-done.34 = f32[16,1536]{1,0:T(8,128)S(1)} collective-permute-done((f32[16,1536]{1,0:T(8,128)S(1)}, f32[16,1536]{1,0:T(8,128)S(1)}, u32[]{:S(2)}, u32[]{:S(2)}) %collective-permute-start.34) | collective-permute-done | bytes 98336 | tf_op jit(solution)/shard_map/ppermute | solution.py:267
  44.9 4.8 %collective-permute-done.33 = f32[16,1536]{1,0:T(8,128)S(1)} collective-permute-done((f32[16,1536]{1,0:T(8,128)S(1)}, f32[16,1536]{1,0:T(8,128)S(1)}, u32[]{:S(2)}, u32[]{:S(2)}) %collective-permute-start.33) | collective-permute-done | bytes 98336 | tf_op jit(solution)/shard_map/ppermute | solution.py:267
  49.6 3.0 %collective-permute-start.38 = (f32[16,1536]{1,0:T(8,128)S(1)}, f32[16,1536]{1,0:T(8,128)S(1)}, u32[]{:S(2)}, u32[]{:S(2)}) collective-permute-start(f32[16,1536]{1,0:T(8,128)S(1)} %get-tuple-element.280), channel_id=1, source_target_pairs={{0,2},{1,3},{2,0},{3,1},{4,6},{5,7},{6,4},{7,5},{8,10},{9,11},{10,... | collective-permute-start | bytes 294920 | tf_op jit(solution)/shard_map/ppermute | solution.py:267
  53.3 2.5 collective-permute-start.37
  56.3 2.1 broadcast_select_fusion.13
  59.2 11.9 %shard_map.38 = (f32[256,1536]{1,0:T(8,128)S(1)}, f32[256,256]{1,0:T(8,128)}) custom-call(f32[256,3072]{1,0:T(8,128)S(1)} %bitcast.147, f32[3072,1536]{1,0:T(8,128)S(1)} %copy-done), custom_call_target="tpu_custom_call" | custom-call | flops 1 | bytes 1 | tf_op jit(solution)/shard_map/pallas_call | solution.py:76
  71.1 1.9 collective-permute-start.44
  73.0 4.0 %collective-permute-start.45 = (f32[2,32,3072]{2,1,0:T(8,128)}, f32[2,32,3072]{2,1,0:T(8,128)S(1)}, u32[]{:S(2)}, u32[]{:S(2)}) collective-permute-start(f32[2,32,3072]{2,1,0:T(8,128)} %collective-permute-done.26), channel_id=1, source_target_pairs={{2,4},{3,5},{4,6},{5,7},{10,12},{11,13},{12,14},{13,15},{18,20},{1... | collective-permute-start | bytes 2359304 | tf_op jit(solution)/shard_map/ppermute | solution.py:311
  77.2 2.5 collective-permute-start.43
  81.9 9.6 %shard_map.39 = f32[3072,256]{1,0:T(8,128)} custom-call(f32[3072,1536]{1,0:T(8,128)S(1)} %copy-done, f32[256,1536]{1,0:T(8,128)S(1)} %bitcast.144), custom_call_target="tpu_custom_call" | custom-call | flops 1 | bytes 1 | tf_op jit(solution)/shard_map/pallas_call | solution.py:108
  92.5 2.2 collective-permute-start.46
  94.7 1.5 collective-permute-start.47
  96.2 1.5 collective-permute-start.48
  97.9 9.6 %shard_map.40 = f32[3072,256]{1,0:T(8,128)} custom-call(f32[3072,1536]{1,0:T(8,128)S(1)} %copy-done, f32[256,1536]{1,0:T(8,128)S(1)} %bitcast.142), custom_call_target="tpu_custom_call" | custom-call | flops 1 | bytes 1 | tf_op jit(solution)/shard_map/pallas_call | solution.py:108
  108.5 1.8 pad_maximum_fusion.14
  110.5 141.4 %conditional.1 = (f32[256,3072]{1,0:T(8,128)}, bf16[1024,1536]{1,0:T(8,128)(2,1)}, bf16[1024,1536]{1,0:T(8,128)(2,1)}) conditional(s32[]{:T(128)} %convert_element_type.4, () %tuple.31, (pred[2,32,3072]{2,1,0:T(8,128)(4,1)S(1)}, f32[2,32,3072]{2,1,0:T(8,128)}, f32[2,32,3072]{2,1,0:T(8,128)S(1)}, pred[2,32,3072]{2,1,0:T(8,128)(4,1)S(1)}, ...), branch_computations={%region_0.1_spmd, %region_1.2_spmd} | conditional | flops 10551590 | bytes 186454752 | solution.py:455
  110.6 2.1 select_select_fusion.1
  112.8 1.1 dynamic-slice_add_fusion.3
  114.7 1.5 collective-permute-start.4
  116.3 1.9 dynamic-slice_add_fusion.2
  118.3 1.3 broadcast_select_fusion.7
  119.7 2.0 pad_maximum_fusion
  122.4 1.1 copy-done.2
  124.5 7.5 %branch_1_fun.5 = f32[512,512]{1,0:T(8,128)S(1)} custom-call(f32[256,3072]{1,0:T(8,128)S(1)} %copy-done.2, f32[256,3072]{1,0:T(8,128)} %bitcast.refs_0_.far_ref, f32[3072,256]{1,0:T(8,128)S(1)} %copy-done.3, f32[3072,256]{1,0:T(8,128)S(1)} %copy-done.4), custom_call_target="tpu_custom_call" | custom-call | flops 1 | bytes 1 | tf_op jit(solution)/shard_map/cond/branch_1_fun/pallas_call | solution.py:138
  133.0 1.5 collective-permute-start.2
  137.0 16.7 %branch_1_fun.4 = (f32[256,1536]{1,0:T(8,128)S(1)}, f32[256,256]{1,0:T(8,128)S(1)}, f32[256,256]{1,0:T(8,128)S(1)}, f32[256,256]{1,0:T(8,128)S(1)}) custom-call(f32[256,3072]{1,0:T(8,128)} %bitcast.refs_0_.far_ref, f32[256,3072]{1,0:T(8,128)S(1)} %copy-done.2, f32[3072,1536]{1,0:T(8,128)} %get-tuple-element.96.refs_2_), custom_call_target="tpu_custom_call" | custom-call | flops 1 | bytes 1 | tf_op jit(solution)/shard_map/cond/branch_1_fun/pallas_call | solution.py:76
  153.7 1.0 dynamic-slice_add_fusion.5
  154.7 1.6 collective-permute-start.6
  157.3 1.5 collective-permute-start.7
  160.6 1.5 collective-permute-start.8
  163.6 12.8 %collective-permute-done.8 = f32[64,1536]{1,0:T(8,128)S(1)} collective-permute-done((f32[64,1536]{1,0:T(8,128)S(1)}, f32[64,1536]{1,0:T(8,128)S(1)}, u32[]{:S(2)}, u32[]{:S(2)}) %collective-permute-start.8) | collective-permute-done | bytes 393248 | tf_op jit(solution)/shard_map/cond/branch_1_fun/ppermute | solution.py:272
  176.6 1.2 collective-permute-start.12
  179.5 3.1 %collective-permute-done.12 = f32[32,1536]{1,0:T(8,128)S(1)} collective-permute-done((f32[32,1536]{1,0:T(8,128)S(1)}, f32[32,1536]{1,0:T(8,128)S(1)}, u32[]{:S(2)}, u32[]{:S(2)}) %collective-permute-start.12) | collective-permute-done | bytes 196640 | tf_op jit(solution)/shard_map/cond/branch_1_fun/ppermute | solution.py:272
  184.6 1.3 collective-permute-start.16
  186.5 5.5 %collective-permute-done.14 = f32[2,32,1536]{2,1,0:T(8,128)S(1)} collective-permute-done((f32[2,32,1536]{2,1,0:T(8,128)S(1)}, f32[2,32,1536]{2,1,0:T(8,128)S(1)}, u32[]{:S(2)}, u32[]{:S(2)}) %collective-permute-start.14) | collective-permute-done | bytes 393248 | tf_op jit(solution)/shard_map/cond/branch_1_fun/ppermute | solution.py:272
  192.0 2.6 collective-permute-done.13
  194.9 5.1 %collective-permute-done.16 = f32[128,512]{1,0:T(8,128)S(1)} collective-permute-done((f32[128,512]{1,0:T(8,128)S(1)}, f32[128,512]{1,0:T(8,128)S(1)}, u32[]{:S(2)}, u32[]{:S(2)}) %collective-permute-start.16) | collective-permute-done | bytes 262176 | tf_op jit(solution)/shard_map/cond/branch_1_fun/ppermute | solution.py:437
  200.7 1.0 fusion.10
  202.0 2.4 collective-permute-start.20
  204.4 2.1 collective-permute-start.18
  206.5 9.6 %collective-permute-done.17 = f32[2,64,1536]{2,1,0:T(8,128)S(1)} collective-permute-done((f32[2,64,1536]{2,1,0:T(8,128)S(1)}, f32[2,64,1536]{2,1,0:T(8,128)S(1)}, u32[]{:S(2)}, u32[]{:S(2)}) %collective-permute-start.17) | collective-permute-done | bytes 786464 | tf_op jit(solution)/shard_map/cond/branch_1_fun/ppermute | solution.py:272
  216.3 6.4 %collective-permute-done.18 = f32[2,64,1536]{2,1,0:T(8,128)S(1)} collective-permute-done((f32[2,64,1536]{2,1,0:T(8,128)S(1)}, f32[2,64,1536]{2,1,0:T(8,128)S(1)}, u32[]{:S(2)}, u32[]{:S(2)}) %collective-permute-start.18) | collective-permute-done | bytes 786464 | tf_op jit(solution)/shard_map/cond/branch_1_fun/ppermute | solution.py:272
  223.1 1.7 collective-permute-start.21
  225.1 1.7 copy-done.5
  226.8 5.8 %branch_1_fun.6 = (f32[512,512]{1,0:T(8,128)S(1)}, f32[512,1536]{1,0:T(8,128)S(1)}, bf16[512,1536]{1,0:T(8,128)(2,1)S(1)}, bf16[512,1536]{1,0:T(8,128)(2,1)S(1)}) custom-call(s32[1]{0:T(128)} %bitcast.5.lower_ref, f32[512,1536]{1,0:T(8,128)S(1)} %bitcast.146, f32[512,1536]{1,0:T(8,128)S(1)} %copy-done.5, f32[2,256,256]{2,1,0:T(8,128)S(1)} %copy-done.21, ...), custom_call_target="tpu_custom_call" | custom-call | flops 1 | bytes 1 | tf_op jit(solution)/shard_map/cond/branch_1_fun/pallas_call | solution.py:194
  232.6 2.3 collective-permute-done.21
  234.9 2.9 collective-permute-start.24
  238.6 6.5 %collective-permute-done.22 = f32[128,512]{1,0:T(8,128)S(1)} collective-permute-done((f32[128,512]{1,0:T(8,128)S(1)}, f32[128,512]{1,0:T(8,128)S(1)}, u32[]{:S(2)}, u32[]{:S(2)}) %collective-permute-start.22) | collective-permute-done | bytes 262176 | tf_op jit(solution)/shard_map/cond/branch_1_fun/ppermute | solution.py:272
  245.7 6.3 %branch_1_fun.7 = (bf16[1024,1536]{1,0:T(8,128)(2,1)}, bf16[1024,1536]{1,0:T(8,128)(2,1)}) custom-call(f32[512,512]{1,0:T(8,128)S(1)} %get-tuple-element.140.local_ref, f32[512,512]{1,0:T(8,128)S(1)} %pad_maximum_fusion.4.crossed_ref, f32[512,1536]{1,0:T(8,128)S(1)} %get-tuple-element.143.left_ref, bf16[512,1536]{1,0:T(8,128)(2,1)S(1)} %get-tuple-element.144.right_high, ...), custom_call_target="tpu_custom_call" | custom-call | flops 1 | bytes 1 | tf_op jit(solution)/shard_map/cond/branch_1_fun/pallas_call | solution.py:222
  252.0 1.5 all-reduce.3.cloned.1.call-done
  253.5 37.3 %shard_map.41 = f32[3072,1536]{1,0:T(8,128)} custom-call(f32[3072,1536]{1,0:T(8,128)} %window_ref.5, f32[256,3072]{1,0:T(8,128)} %bitcast.149, f32[256,3072]{1,0:T(8,128)} %get-tuple-element.221.far_ref, bf16[1024,1536]{1,0:T(8,128)(2,1)} %get-tuple-element.222.high_ref, bf16[1024,1536]{1,0:T(8,128)(2,1)} %get-tuple-element.223.low_ref, ...), custom_call_target="tpu_custom_call" | custom-call | flops 1 | bytes 1 | tf_op jit(solution)/shard_map/pallas_call | solution.py:244
  (196 shorter events, 26.3 us)
Async XLA Ops:
  6.5 247.0 %all-reduce.3.cloned.1.call-start = ((), (), s32[]{:S(2)}) async-start(), calls=%async_computation | async-start | bytes 12582912 | tf_op jit(solution)/shard_map/psum | solution.py:491
  7.6 6.9 %collective-permute-start.27 = (f32[2,32,1536]{2,1,0:T(8,128)S(1)}, f32[2,32,1536]{2,1,0:T(8,128)S(1)}, u32[]{:S(2)}, u32[]{:S(2)}) collective-permute-start(f32[2,32,1536]{2,1,0:T(8,128)S(1)} %dynamic-slice_bitcast_fusion), channel_id=1, source_target_pairs={{0,1},{1,0},{2,3},{3,2},{4,5},{5,4},{6,7},{7,6},{8,9},{9,8},{10,11... | collective-permute-start | bytes 1179656 | tf_op jit(solution)/shard_map/ppermute | solution.py:262
  7.6 22.1 %collective-permute-start.26 = (f32[2,32,3072]{2,1,0:T(8,128)}, f32[2,32,3072]{2,1,0:T(8,128)}, u32[]{:S(2)}, u32[]{:S(2)}) collective-permute-start(f32[2,32,3072]{2,1,0:T(8,128)} %bitcast.154), channel_id=1, source_target_pairs={{0,2},{1,3},{2,4},{3,5},{4,6},{5,7},{8,10},{9,11},{10,12},{11,13},... | collective-permute-start | bytes 2359304 | tf_op jit(solution)/shard_map/ppermute | solution.py:311
  11.1 21.9 %collective-permute-start.25 = (f32[2,32,3072]{2,1,0:T(8,128)}, f32[2,32,3072]{2,1,0:T(8,128)}, u32[]{:S(2)}, u32[]{:S(2)}) collective-permute-start(f32[2,32,3072]{2,1,0:T(8,128)} %bitcast.155), channel_id=1, source_target_pairs={{2,0},{3,1},{4,2},{5,3},{6,4},{7,5},{10,8},{11,9},{12,10},{13,11},... | collective-permute-start | bytes 2359304 | tf_op jit(solution)/shard_map/ppermute | solution.py:311
  15.6 17.4 %copy-start.6 = (f32[2,3072,32]{1,2,0:T(8,128)S(1)}, f32[2,3072,32]{1,2,0:T(8,128)}, u32[]{:S(2)}) copy-start(f32[2,3072,32]{1,2,0:T(8,128)} %param.6) | copy-start | bytes 2359300
  15.7 8.8 %collective-permute-start.30 = (f32[2,16,1536]{2,1,0:T(8,128)S(1)}, f32[2,16,1536]{2,1,0:T(8,128)S(1)}, u32[]{:S(2)}, u32[]{:S(2)}) collective-permute-start(f32[2,16,1536]{2,1,0:T(8,128)S(1)} %get-tuple-element.273), channel_id=1, source_target_pairs={{0,24},{8,16},{16,8},{24,0},{1,25},{9,17},{17,9},{25,1},{2,26},{10... | collective-permute-start | bytes 589832 | tf_op jit(solution)/shard_map/ppermute | solution.py:272
  18.3 9.4 %collective-permute-start.29 = (f32[2,16,1536]{2,1,0:T(8,128)S(1)}, f32[2,16,1536]{2,1,0:T(8,128)S(1)}, u32[]{:S(2)}, u32[]{:S(2)}) collective-permute-start(f32[2,16,1536]{2,1,0:T(8,128)S(1)} %get-tuple-element.274), channel_id=1, source_target_pairs={{0,16},{8,24},{16,0},{24,8},{1,17},{9,25},{17,1},{25,9},{2,18},{10... | collective-permute-start | bytes 589832 | tf_op jit(solution)/shard_map/ppermute | solution.py:272
  18.8 9.0 %collective-permute-start.28 = (f32[2,16,1536]{2,1,0:T(8,128)S(1)}, f32[2,16,1536]{2,1,0:T(8,128)S(1)}, u32[]{:S(2)}, u32[]{:S(2)}) collective-permute-start(f32[2,16,1536]{2,1,0:T(8,128)S(1)} %get-tuple-element.275), channel_id=1, source_target_pairs={{0,8},{8,0},{16,24},{24,16},{1,9},{9,1},{17,25},{25,17},{2,10},{10... | collective-permute-start | bytes 589832 | tf_op jit(solution)/shard_map/ppermute | solution.py:272
  34.7 17.9 %collective-permute-start.31 = (f32[2,2,32,3072]{3,2,0,1:T(8,128)S(1)}, f32[2,2,32,3072]{3,2,0,1:T(8,128)S(1)}, u32[]{:S(2)}, u32[]{:S(2)}) collective-permute-start(f32[2,2,32,3072]{3,2,0,1:T(8,128)S(1)} %pad_maximum_fusion.15), channel_id=1, source_target_pairs={{0,1},{1,0},{2,3},{3,2},{4,5},{5,4},{6,7},{7,6},{8,9},{9,8},{10,11... | collective-permute-start | bytes 4718600 | tf_op jit(solution)/shard_map/ppermute | solution.py:262
  35.0 9.9 %collective-permute-start.34 = (f32[16,1536]{1,0:T(8,128)S(1)}, f32[16,1536]{1,0:T(8,128)S(1)}, u32[]{:S(2)}, u32[]{:S(2)}) collective-permute-start(f32[16,1536]{1,0:T(8,128)S(1)} %get-tuple-element.281), channel_id=1, source_target_pairs={{0,6},{1,7},{2,4},{3,5},{4,2},{5,3},{6,0},{7,1},{8,14},{9,15},{10,... | collective-permute-start | bytes 294920 | tf_op jit(solution)/shard_map/ppermute | solution.py:267
  36.6 13.0 %collective-permute-start.33 = (f32[16,1536]{1,0:T(8,128)S(1)}, f32[16,1536]{1,0:T(8,128)S(1)}, u32[]{:S(2)}, u32[]{:S(2)}) collective-permute-start(f32[16,1536]{1,0:T(8,128)S(1)} %get-tuple-element.282), channel_id=1, source_target_pairs={{0,4},{1,5},{2,6},{3,7},{4,0},{5,1},{6,2},{7,3},{8,12},{9,13},{10,... | collective-permute-start | bytes 294920 | tf_op jit(solution)/shard_map/ppermute | solution.py:267
  38.8 13.9 %collective-permute-start.32 = (f32[16,1536]{1,0:T(8,128)S(1)}, f32[16,1536]{1,0:T(8,128)S(1)}, u32[]{:S(2)}, u32[]{:S(2)}) collective-permute-start(f32[16,1536]{1,0:T(8,128)S(1)} %get-tuple-element.283), channel_id=1, source_target_pairs={{0,2},{1,3},{2,0},{3,1},{4,6},{5,7},{6,4},{7,5},{8,10},{9,11},{10,... | collective-permute-start | bytes 294920 | tf_op jit(solution)/shard_map/ppermute | solution.py:267
  38.8 20.4 %copy-start = (f32[3072,1536]{1,0:T(8,128)S(1)}, f32[3072,1536]{1,0:T(8,128)}, u32[]{:S(2)}) copy-start(f32[3072,1536]{1,0:T(8,128)} %window_ref.5) | copy-start | bytes 56623108
  38.9 19.5 %collective-permute-start.40 = (f32[16,1536]{1,0:T(8,128)S(1)}, f32[16,1536]{1,0:T(8,128)S(1)}, u32[]{:S(2)}, u32[]{:S(2)}) collective-permute-start(f32[16,1536]{1,0:T(8,128)S(1)} %get-tuple-element.278), channel_id=1, source_target_pairs={{0,6},{1,7},{2,4},{3,5},{4,2},{5,3},{6,0},{7,1},{8,14},{9,15},{10,... | collective-permute-start | bytes 294920 | tf_op jit(solution)/shard_map/ppermute | solution.py:267
  44.8 26.3 %collective-permute-start.39 = (f32[16,1536]{1,0:T(8,128)S(1)}, f32[16,1536]{1,0:T(8,128)S(1)}, u32[]{:S(2)}, u32[]{:S(2)}) collective-permute-start(f32[16,1536]{1,0:T(8,128)S(1)} %get-tuple-element.279), channel_id=1, source_target_pairs={{0,4},{1,5},{2,6},{3,7},{4,0},{5,1},{6,2},{7,3},{8,12},{9,13},{10,... | collective-permute-start | bytes 294920 | tf_op jit(solution)/shard_map/ppermute | solution.py:267
  49.6 23.4 %collective-permute-start.38 = (f32[16,1536]{1,0:T(8,128)S(1)}, f32[16,1536]{1,0:T(8,128)S(1)}, u32[]{:S(2)}, u32[]{:S(2)}) collective-permute-start(f32[16,1536]{1,0:T(8,128)S(1)} %get-tuple-element.280), channel_id=1, source_target_pairs={{0,2},{1,3},{2,0},{3,1},{4,6},{5,7},{6,4},{7,5},{8,10},{9,11},{10,... | collective-permute-start | bytes 294920 | tf_op jit(solution)/shard_map/ppermute | solution.py:267
  53.3 5.9 %copy-start.1 = (f32[2,128,3072]{2,1,0:T(8,128)}, f32[2,128,3072]{2,1,0:T(8,128)S(1)}, u32[]{:S(2)}) copy-start(f32[2,128,3072]{2,1,0:T(8,128)S(1)} %pad_maximum_fusion.13) | copy-start | bytes 9437188
  53.3 23.8 %collective-permute-start.37 = (f32[4,16,1536]{2,1,0:T(8,128)S(1)}, f32[4,16,1536]{2,1,0:T(8,128)S(1)}, u32[]{:S(2)}, u32[]{:S(2)}) collective-permute-start(f32[4,16,1536]{2,1,0:T(8,128)S(1)} %bitcast_dynamic-update-slice_fusion.15), channel_id=1, source_target_pairs={{0,24},{8,16},{16,8},{24,0},{1,25},{9,17},{17,9},{25,1},{2,26},{10... | collective-permute-start | bytes 1179656 | tf_op jit(solution)/shard_map/ppermute | solution.py:272
  55.8 21.3 %collective-permute-start.36 = (f32[4,16,1536]{2,1,0:T(8,128)S(1)}, f32[4,16,1536]{2,1,0:T(8,128)S(1)}, u32[]{:S(2)}, u32[]{:S(2)}) collective-permute-start(f32[4,16,1536]{2,1,0:T(8,128)S(1)} %bitcast_dynamic-update-slice_fusion.15), channel_id=1, source_target_pairs={{0,16},{8,24},{16,0},{24,8},{1,17},{9,25},{17,1},{25,9},{2,18},{10... | collective-permute-start | bytes 1179656 | tf_op jit(solution)/shard_map/ppermute | solution.py:272
  58.4 18.6 %collective-permute-start.35 = (f32[4,16,1536]{2,1,0:T(8,128)S(1)}, f32[4,16,1536]{2,1,0:T(8,128)S(1)}, u32[]{:S(2)}, u32[]{:S(2)}) collective-permute-start(f32[4,16,1536]{2,1,0:T(8,128)S(1)} %bitcast_dynamic-update-slice_fusion.15), channel_id=1, source_target_pairs={{0,8},{8,0},{16,24},{24,16},{1,9},{9,1},{17,25},{25,17},{2,10},{10... | collective-permute-start | bytes 1179656 | tf_op jit(solution)/shard_map/ppermute | solution.py:272
  71.1 21.4 %collective-permute-start.44 = (f32[2,32,3072]{2,1,0:T(8,128)}, f32[2,32,3072]{2,1,0:T(8,128)S(1)}, u32[]{:S(2)}, u32[]{:S(2)}) collective-permute-start(f32[2,32,3072]{2,1,0:T(8,128)} %collective-permute-done.25), channel_id=1, source_target_pairs={{2,0},{3,1},{4,2},{5,3},{10,8},{11,9},{12,10},{13,11},{18,16},{19,... | collective-permute-start | bytes 2359304 | tf_op jit(solution)/shard_map/ppermute | solution.py:311
  73.0 21.7 %collective-permute-start.45 = (f32[2,32,3072]{2,1,0:T(8,128)}, f32[2,32,3072]{2,1,0:T(8,128)S(1)}, u32[]{:S(2)}, u32[]{:S(2)}) collective-permute-start(f32[2,32,3072]{2,1,0:T(8,128)} %collective-permute-done.26), channel_id=1, source_target_pairs={{2,4},{3,5},{4,6},{5,7},{10,12},{11,13},{12,14},{13,15},{18,20},{1... | collective-permute-start | bytes 2359304 | tf_op jit(solution)/shard_map/ppermute | solution.py:311
  77.2 19.1 %collective-permute-start.43 = (f32[4,16,1536]{2,1,0:T(8,128)S(1)}, f32[4,16,1536]{2,1,0:T(8,128)S(1)}, u32[]{:S(2)}, u32[]{:S(2)}) collective-permute-start(f32[4,16,1536]{2,1,0:T(8,128)S(1)} %bitcast_dynamic-update-slice_fusion.11), channel_id=1, source_target_pairs={{0,24},{8,16},{16,8},{24,0},{1,25},{9,17},{17,9},{25,1},{2,26},{10... | collective-permute-start | bytes 1179656 | tf_op jit(solution)/shard_map/ppermute | solution.py:272
  79.7 18.1 %collective-permute-start.42 = (f32[4,16,1536]{2,1,0:T(8,128)S(1)}, f32[4,16,1536]{2,1,0:T(8,128)S(1)}, u32[]{:S(2)}, u32[]{:S(2)}) collective-permute-start(f32[4,16,1536]{2,1,0:T(8,128)S(1)} %bitcast_dynamic-update-slice_fusion.11), channel_id=1, source_target_pairs={{0,16},{8,24},{16,0},{24,8},{1,17},{9,25},{17,1},{25,9},{2,18},{10... | collective-permute-start | bytes 1179656 | tf_op jit(solution)/shard_map/ppermute | solution.py:272
  80.2 17.6 %collective-permute-start.41 = (f32[4,16,1536]{2,1,0:T(8,128)S(1)}, f32[4,16,1536]{2,1,0:T(8,128)S(1)}, u32[]{:S(2)}, u32[]{:S(2)}) collective-permute-start(f32[4,16,1536]{2,1,0:T(8,128)S(1)} %bitcast_dynamic-update-slice_fusion.11), channel_id=1, source_target_pairs={{0,8},{8,0},{16,24},{24,16},{1,9},{9,1},{17,25},{25,17},{2,10},{10... | collective-permute-start | bytes 1179656 | tf_op jit(solution)/shard_map/ppermute | solution.py:272
  80.8 10.7 %copy-start.9 = (f32[128,1536]{1,0:T(8,128)}, f32[128,1536]{1,0:T(8,128)S(1)}, u32[]{:S(2)}) copy-start(f32[128,1536]{1,0:T(8,128)S(1)} %get-tuple-element.265) | copy-start | bytes 2359300
  92.5 5.4 %copy-start.17 = (f32[2,32,3072]{2,1,0:T(8,128)}, f32[2,32,3072]{2,1,0:T(8,128)S(1)}, u32[]{:S(2)}) copy-start(f32[2,32,3072]{2,1,0:T(8,128)S(1)} %collective-permute-done.44) | copy-start | bytes 2359300
  92.5 15.9 %collective-permute-start.46 = (f32[2,32,3072]{2,1,0:T(8,128)}, f32[2,32,3072]{2,1,0:T(8,128)}, u32[]{:S(2)}, u32[]{:S(2)}) collective-permute-start(f32[2,32,3072]{2,1,0:T(8,128)} %broadcast_select_fusion.13), channel_id=1, source_target_pairs={{4,0},{5,1},{2,6},{3,7},{12,8},{13,9},{10,14},{11,15},{20,16},{21,... | collective-permute-start | bytes 2359304 | tf_op jit(solution)/shard_map/ppermute | solution.py:404
  94.7 3.2 %copy-start.19 = (f32[2,32,3072]{2,1,0:T(8,128)}, f32[2,32,3072]{2,1,0:T(8,128)S(1)}, u32[]{:S(2)}) copy-start(f32[2,32,3072]{2,1,0:T(8,128)S(1)} %collective-permute-done.45) | copy-start | bytes 2359300
  94.7 13.7 %collective-permute-start.47 = (f32[64,1536]{1,0:T(8,128)}, f32[64,1536]{1,0:T(8,128)S(1)}, u32[]{:S(2)}, u32[]{:S(2)}) collective-permute-start(f32[64,1536]{1,0:T(8,128)} %constant_dynamic-slice_fusion.10), channel_id=1, source_target_pairs={{0,8},{8,0},{16,24},{24,16},{1,9},{9,1},{17,25},{25,17},{2,10},{10... | collective-permute-start | bytes 1179656 | tf_op jit(solution)/shard_map/ppermute | solution.py:272
  96.2 12.2 %collective-permute-start.48 = (f32[64,1536]{1,0:T(8,128)}, f32[64,1536]{1,0:T(8,128)}, u32[]{:S(2)}, u32[]{:S(2)}) collective-permute-start(f32[64,1536]{1,0:T(8,128)} %constant_dynamic-slice_fusion.11), channel_id=1, source_target_pairs={{0,16},{8,24},{16,0},{24,8},{1,17},{9,25},{17,1},{25,9},{2,18},{10... | collective-permute-start | bytes 1179656 | tf_op jit(solution)/shard_map/ppermute | solution.py:272
  112.7 3.6 %copy-start.8 = (f32[128,1536]{1,0:T(8,128)S(1)}, f32[128,1536]{1,0:T(8,128)}, u32[]{:S(2)}) copy-start(f32[128,1536]{1,0:T(8,128)} %get-tuple-element.108) | copy-start | bytes 2359300 | tf_op jit(solution)/shard_map/cond
  112.7 5.5 %collective-permute-start = (f32[2,32,3072]{2,1,0:T(8,128)S(1)}, f32[2,32,3072]{2,1,0:T(8,128)}, u32[]{:S(2)}, u32[]{:S(2)}) collective-permute-start(f32[2,32,3072]{2,1,0:T(8,128)S(1)} %get-tuple-element.228), channel_id=1, source_target_pairs={{0,1},{1,0},{2,3},{3,2},{4,5},{5,4},{6,7},{7,6},{8,9},{9,8},{10,11... | collective-permute-start | bytes 2359304 | tf_op jit(solution)/shard_map/cond/branch_1_fun/ppermute | solution.py:262
  114.7 39.0 %collective-permute-start.4 = (f32[32,1536]{1,0:T(8,128)}, f32[32,1536]{1,0:T(8,128)}, u32[]{:S(2)}, u32[]{:S(2)}) collective-permute-start(f32[32,1536]{1,0:T(8,128)} %constant_dynamic-slice_fusion.7), channel_id=1, source_target_pairs={{0,16},{8,24},{16,0},{24,8},{1,17},{9,25},{17,1},{25,9},{2,18},{10... | collective-permute-start | bytes 589832 | tf_op jit(solution)/shard_map/cond/branch_1_fun/ppermute | solution.py:272
  116.2 3.3 %collective-permute-start.1 = (f32[2,32,3072]{2,1,0:T(8,128)S(1)}, f32[2,32,3072]{2,1,0:T(8,128)S(1)}, u32[]{:S(2)}, u32[]{:S(2)}) collective-permute-start(f32[2,32,3072]{2,1,0:T(8,128)S(1)} %get-tuple-element.229), channel_id=1, source_target_pairs={{0,1},{1,0},{2,3},{3,2},{4,5},{5,4},{6,7},{7,6},{8,9},{9,8},{10,11... | collective-permute-start | bytes 2359304 | tf_op jit(solution)/shard_map/cond/branch_1_fun/ppermute | solution.py:262
  119.7 3.9 %copy-start.2 = (f32[256,3072]{1,0:T(8,128)S(1)}, f32[256,3072]{1,0:T(8,128)}, u32[]{:S(2)}) copy-start(f32[256,3072]{1,0:T(8,128)} %get-tuple-element.95.refs_1_.near_ref) | copy-start | bytes 9437188 | tf_op jit(solution)/shard_map/cond
  119.7 4.8 %copy-start.3 = (f32[3072,256]{1,0:T(8,128)S(1)}, f32[3072,256]{1,0:T(8,128)}, u32[]{:S(2)}) copy-start(f32[3072,256]{1,0:T(8,128)} %get-tuple-element.102.refs_0_) | copy-start | bytes 9437188 | tf_op jit(solution)/shard_map/cond
  132.1 3.7 %copy-start.15 = (f32[64,1536]{1,0:T(8,128)S(1)}, f32[64,1536]{1,0:T(8,128)}, u32[]{:S(2)}) copy-start(f32[64,1536]{1,0:T(8,128)} %dynamic-slice_add_fusion.2) | copy-start | bytes 1179652 | tf_op jit(solution)/shard_map/cond
  132.2 3.0 %copy-start.13 = (f32[256,512]{1,0:T(8,128)}, f32[256,512]{1,0:T(8,128)S(1)}, u32[]{:S(2)}) copy-start(f32[256,512]{1,0:T(8,128)S(1)} %get-tuple-element.245) | copy-start | bytes 1572868 | tf_op jit(solution)/shard_map/cond
  133.0 20.7 %collective-permute-start.2 = (f32[128,512]{1,0:T(8,128)}, f32[128,512]{1,0:T(8,128)}, u32[]{:S(2)}, u32[]{:S(2)}) collective-permute-start(f32[128,512]{1,0:T(8,128)} %constant_dynamic-slice_fusion.9), channel_id=1, source_target_pairs={{0,8},{8,0},{16,24},{24,16},{1,9},{9,1},{17,25},{25,17},{2,10},{10... | collective-permute-start | bytes 786440 | tf_op jit(solution)/shard_map/cond/branch_1_fun/ppermute | solution.py:272
  135.2 18.4 %collective-permute-start.3 = (f32[128,512]{1,0:T(8,128)}, f32[128,512]{1,0:T(8,128)}, u32[]{:S(2)}, u32[]{:S(2)}) collective-permute-start(f32[128,512]{1,0:T(8,128)} %constant_dynamic-slice_fusion.8), channel_id=1, source_target_pairs={{0,16},{8,24},{16,0},{24,8},{1,17},{9,25},{17,1},{25,9},{2,18},{10... | collective-permute-start | bytes 786440 | tf_op jit(solution)/shard_map/cond/branch_1_fun/ppermute | solution.py:272
  136.4 17.2 %collective-permute-start.5 = (f32[32,1536]{1,0:T(8,128)}, f32[32,1536]{1,0:T(8,128)}, u32[]{:S(2)}, u32[]{:S(2)}) collective-permute-start(f32[32,1536]{1,0:T(8,128)} %constant_dynamic-slice_fusion.6), channel_id=1, source_target_pairs={{0,8},{8,0},{16,24},{24,16},{1,9},{9,1},{17,25},{25,17},{2,10},{10... | collective-permute-start | bytes 589832 | tf_op jit(solution)/shard_map/cond/branch_1_fun/ppermute | solution.py:272
  137.0 16.7 %copy-start.14 = (f32[256,512]{1,0:T(8,128)S(1)}, f32[256,512]{1,0:T(8,128)}, u32[]{:S(2)}) copy-start(f32[256,512]{1,0:T(8,128)} %copy-done.13) | copy-start | bytes 1572868 | tf_op jit(solution)/shard_map/cond
  137.0 19.4 %copy-start.12 = (f32[256,512]{1,0:T(8,128)S(1)}, f32[256,512]{1,0:T(8,128)}, u32[]{:S(2)}) copy-start(f32[256,512]{1,0:T(8,128)} %copy-done.11) | copy-start | bytes 1572868 | tf_op jit(solution)/shard_map/cond
  154.7 8.9 %collective-permute-start.6 = (f32[64,512]{1,0:T(8,128)S(1)}, f32[64,512]{1,0:T(8,128)S(1)}, u32[]{:S(2)}, u32[]{:S(2)}) collective-permute-start(f32[64,512]{1,0:T(8,128)S(1)} %constant_dynamic-slice_fusion.5), channel_id=1, source_target_pairs={{0,16},{8,24},{16,0},{24,8},{1,17},{9,25},{17,1},{25,9},{2,18},{10... | collective-permute-start | bytes 393224 | tf_op jit(solution)/shard_map/cond/branch_1_fun/ppermute | solution.py:272
  157.3 6.3 %collective-permute-start.7 = (f32[64,512]{1,0:T(8,128)S(1)}, f32[64,512]{1,0:T(8,128)S(1)}, u32[]{:S(2)}, u32[]{:S(2)}) collective-permute-start(f32[64,512]{1,0:T(8,128)S(1)} %constant_dynamic-slice_fusion.4), channel_id=1, source_target_pairs={{0,8},{8,0},{16,24},{24,16},{1,9},{9,1},{17,25},{25,17},{2,10},{10... | collective-permute-start | bytes 393224 | tf_op jit(solution)/shard_map/cond/branch_1_fun/ppermute | solution.py:272
  159.8 35.1 %collective-permute-start.15 = (f32[256,256]{1,0:T(8,128)S(1)}, f32[256,256]{1,0:T(8,128)S(1)}, u32[]{:S(2)}, u32[]{:S(2)}) collective-permute-start(f32[256,256]{1,0:T(8,128)S(1)} %pad_maximum_fusion.10), channel_id=1, source_target_pairs={{0,8},{8,0},{16,24},{24,16},{1,9},{9,1},{17,25},{25,17},{2,10},{10... | collective-permute-start | bytes 786440 | tf_op jit(solution)/shard_map/cond/branch_1_fun/ppermute | solution.py:272
  160.6 15.8 %collective-permute-start.8 = (f32[64,1536]{1,0:T(8,128)S(1)}, f32[64,1536]{1,0:T(8,128)S(1)}, u32[]{:S(2)}, u32[]{:S(2)}) collective-permute-start(f32[64,1536]{1,0:T(8,128)S(1)} %constant_dynamic-slice_fusion.3), channel_id=1, source_target_pairs={{0,8},{8,0},{16,24},{24,16},{1,9},{9,1},{17,25},{25,17},{2,10},{10... | collective-permute-start | bytes 1179656 | tf_op jit(solution)/shard_map/cond/branch_1_fun/ppermute | solution.py:272
  162.2 14.2 %collective-permute-start.9 = (f32[64,1536]{1,0:T(8,128)S(1)}, f32[64,1536]{1,0:T(8,128)S(1)}, u32[]{:S(2)}, u32[]{:S(2)}) collective-permute-start(f32[64,1536]{1,0:T(8,128)S(1)} %constant_dynamic-slice_fusion.2), channel_id=1, source_target_pairs={{0,16},{8,24},{16,0},{24,8},{1,17},{9,25},{17,1},{25,9},{2,18},{10... | collective-permute-start | bytes 1179656 | tf_op jit(solution)/shard_map/cond/branch_1_fun/ppermute | solution.py:272
  176.6 6.0 %collective-permute-start.12 = (f32[32,1536]{1,0:T(8,128)S(1)}, f32[32,1536]{1,0:T(8,128)S(1)}, u32[]{:S(2)}, u32[]{:S(2)}) collective-permute-start(f32[32,1536]{1,0:T(8,128)S(1)} %constant_dynamic-slice_fusion), channel_id=1, source_target_pairs={{0,8},{8,0},{16,24},{24,16},{1,9},{9,1},{17,25},{25,17},{2,10},{10... | collective-permute-start | bytes 589832 | tf_op jit(solution)/shard_map/cond/branch_1_fun/ppermute | solution.py:272
  177.8 5.7 %collective-permute-start.11 = (f32[32,1536]{1,0:T(8,128)S(1)}, f32[32,1536]{1,0:T(8,128)S(1)}, u32[]{:S(2)}, u32[]{:S(2)}) collective-permute-start(f32[32,1536]{1,0:T(8,128)S(1)} %constant_dynamic-slice_fusion.1), channel_id=1, source_target_pairs={{0,16},{8,24},{16,0},{24,8},{1,17},{9,25},{17,1},{25,9},{2,18},{10... | collective-permute-start | bytes 589832 | tf_op jit(solution)/shard_map/cond/branch_1_fun/ppermute | solution.py:272
  178.5 5.0 %collective-permute-start.10 = (f32[128,512]{1,0:T(8,128)S(1)}, f32[128,512]{1,0:T(8,128)S(1)}, u32[]{:S(2)}, u32[]{:S(2)}) collective-permute-start(f32[128,512]{1,0:T(8,128)S(1)} %pad_maximum_fusion.9), channel_id=1, source_target_pairs={{0,1},{1,0},{2,3},{3,2},{4,5},{5,4},{6,7},{7,6},{8,9},{9,8},{10,11... | collective-permute-start | bytes 786440 | tf_op jit(solution)/shard_map/cond/branch_1_fun/ppermute | solution.py:262
  183.6 8.4 %collective-permute-start.14 = (f32[2,32,1536]{2,1,0:T(8,128)S(1)}, f32[2,32,1536]{2,1,0:T(8,128)S(1)}, u32[]{:S(2)}, u32[]{:S(2)}) collective-permute-start(f32[2,32,1536]{2,1,0:T(8,128)S(1)} %pad_maximum_fusion.8), channel_id=1, source_target_pairs={{0,8},{8,0},{16,24},{24,16},{1,9},{9,1},{17,25},{25,17},{2,10},{10... | collective-permute-start | bytes 1179656 | tf_op jit(solution)/shard_map/cond/branch_1_fun/ppermute | solution.py:272
  184.6 15.4 %collective-permute-start.16 = (f32[128,512]{1,0:T(8,128)S(1)}, f32[128,512]{1,0:T(8,128)S(1)}, u32[]{:S(2)}, u32[]{:S(2)}) collective-permute-start(f32[128,512]{1,0:T(8,128)S(1)} %fusion.11), channel_id=1, source_target_pairs={{0,2},{1,3},{6,4},{7,5},{8,10},{9,11},{14,12},{15,13},{16,18},{17,... | collective-permute-start | bytes 786440 | tf_op jit(solution)/shard_map/cond/branch_1_fun/ppermute | solution.py:437
  185.9 8.8 %collective-permute-start.13 = (f32[2,32,1536]{2,1,0:T(8,128)S(1)}, f32[2,32,1536]{2,1,0:T(8,128)S(1)}, u32[]{:S(2)}, u32[]{:S(2)}) collective-permute-start(f32[2,32,1536]{2,1,0:T(8,128)S(1)} %pad_maximum_fusion.7), channel_id=1, source_target_pairs={{0,16},{8,24},{16,0},{24,8},{1,17},{9,25},{17,1},{25,9},{2,18},{10... | collective-permute-start | bytes 1179656 | tf_op jit(solution)/shard_map/cond/branch_1_fun/ppermute | solution.py:272
  194.9 5.1 %copy-start.23 = (f32[256,256]{1,0:T(8,128)}, f32[256,256]{1,0:T(8,128)S(1)}, u32[]{:S(2)}) copy-start(f32[256,256]{1,0:T(8,128)S(1)} %collective-permute-done.15) | copy-start | bytes 786436 | tf_op jit(solution)/shard_map/cond
  200.0 16.0 %collective-permute-start.17 = (f32[2,64,1536]{2,1,0:T(8,128)S(1)}, f32[2,64,1536]{2,1,0:T(8,128)S(1)}, u32[]{:S(2)}, u32[]{:S(2)}) collective-permute-start(f32[2,64,1536]{2,1,0:T(8,128)S(1)} %pad_maximum_fusion.5), channel_id=1, source_target_pairs={{0,8},{8,0},{16,24},{24,16},{1,9},{9,1},{17,25},{25,17},{2,10},{10... | collective-permute-start | bytes 2359304 | tf_op jit(solution)/shard_map/cond/branch_1_fun/ppermute | solution.py:272
  201.7 21.3 %collective-permute-start.19 = (f32[256,256]{1,0:T(8,128)S(1)}, f32[256,256]{1,0:T(8,128)S(1)}, u32[]{:S(2)}, u32[]{:S(2)}) collective-permute-start(f32[256,256]{1,0:T(8,128)S(1)} %fusion.10), channel_id=1, source_target_pairs={{0,16},{8,24},{16,0},{24,8},{1,17},{9,25},{17,1},{25,9},{2,18},{10... | collective-permute-start | bytes 786440 | tf_op jit(solution)/shard_map/cond/branch_1_fun/ppermute | solution.py:272
  202.0 21.0 %collective-permute-start.20 = (f32[128,512]{1,0:T(8,128)S(1)}, f32[128,512]{1,0:T(8,128)S(1)}, u32[]{:S(2)}, u32[]{:S(2)}) collective-permute-start(f32[128,512]{1,0:T(8,128)S(1)} %add.254), channel_id=1, source_target_pairs={{2,4},{3,5},{4,2},{5,3},{10,12},{11,13},{12,10},{13,11},{18,20},{1... | collective-permute-start | bytes 786440 | tf_op jit(solution)/shard_map/cond/branch_1_fun/ppermute | solution.py:437
  204.4 18.4 %collective-permute-start.18 = (f32[2,64,1536]{2,1,0:T(8,128)S(1)}, f32[2,64,1536]{2,1,0:T(8,128)S(1)}, u32[]{:S(2)}, u32[]{:S(2)}) collective-permute-start(f32[2,64,1536]{2,1,0:T(8,128)S(1)} %pad_maximum_fusion.6), channel_id=1, source_target_pairs={{0,16},{8,24},{16,0},{24,8},{1,17},{9,25},{17,1},{25,9},{2,18},{10... | collective-permute-start | bytes 2359304 | tf_op jit(solution)/shard_map/cond/branch_1_fun/ppermute | solution.py:272
  223.1 11.7 %collective-permute-start.21 = (f32[128,512]{1,0:T(8,128)S(1)}, f32[128,512]{1,0:T(8,128)S(1)}, u32[]{:S(2)}, u32[]{:S(2)}) collective-permute-start(f32[128,512]{1,0:T(8,128)S(1)} %add.256), channel_id=1, source_target_pairs={{2,0},{3,1},{4,6},{5,7},{10,8},{11,9},{12,14},{13,15},{18,16},{19,... | collective-permute-start | bytes 786440 | tf_op jit(solution)/shard_map/cond/branch_1_fun/ppermute | solution.py:437
  234.9 10.6 %collective-permute-start.24 = (f32[128,512]{1,0:T(8,128)S(1)}, f32[128,512]{1,0:T(8,128)S(1)}, u32[]{:S(2)}, u32[]{:S(2)}) collective-permute-start(f32[128,512]{1,0:T(8,128)S(1)} %broadcast_select_fusion.12), channel_id=1, source_target_pairs={{0,24},{8,16},{16,8},{24,0},{1,25},{9,17},{17,9},{25,1},{2,26},{10... | collective-permute-start | bytes 786440 | tf_op jit(solution)/shard_map/cond/branch_1_fun/ppermute | solution.py:272
  237.8 7.6 %collective-permute-start.23 = (f32[128,512]{1,0:T(8,128)S(1)}, f32[128,512]{1,0:T(8,128)S(1)}, u32[]{:S(2)}, u32[]{:S(2)}) collective-permute-start(f32[128,512]{1,0:T(8,128)S(1)} %broadcast_select_fusion.12), channel_id=1, source_target_pairs={{0,16},{8,24},{16,0},{24,8},{1,17},{9,25},{17,1},{25,9},{2,18},{10... | collective-permute-start | bytes 786440 | tf_op jit(solution)/shard_map/cond/branch_1_fun/ppermute | solution.py:272
  238.3 6.8 %collective-permute-start.22 = (f32[128,512]{1,0:T(8,128)S(1)}, f32[128,512]{1,0:T(8,128)S(1)}, u32[]{:S(2)}, u32[]{:S(2)}) collective-permute-start(f32[128,512]{1,0:T(8,128)S(1)} %broadcast_select_fusion.12), channel_id=1, source_target_pairs={{0,8},{8,0},{16,24},{24,16},{1,9},{9,1},{17,25},{25,17},{2,10},{10... | collective-permute-start | bytes 786440 | tf_op jit(solution)/shard_map/cond/branch_1_fun/ppermute | solution.py:272
  (10 other events, 20.8 us)
Sparse Core Ops, SparseCore 0:
  108.6 144.8 all-reduce.2

commit v6 on v5

--- a/solution.py
+++ b/solution.py
@@ -464,6 +464,7 @@
     chips = lax.axis_size("col") // 2
     row, chip = lax.axis_index("row"), lax.axis_index("col") // 2
     lower = chip < chips // 2
+    core = lax.axis_index("col") % 2
     rows, cols = window.shape
     panels = reflectors.shape[0]
     bits = [1 << bit for bit in range(row_count.bit_length() - 1)]
@@ -509,6 +510,19 @@
             steps = [scatter_step(one, order[step]) for one, order in zip(near_parts, orders)]
             near_parts = [one + kept for one, kept in steps]
         far_parts = [far_projected[part * panel : part * (panel + 1)] for panel in range(panels)]
+        def of(value, one, two):
+            return value[part * one : part * (one + 1), part * two : part * (two + 1)]
+
+        inner = [
+            ordered(
+                lower,
+                ordered(lower, of(same, one, two), of(mixed, one, two), 1),
+                ordered(lower, of(crossing, one, two), of(opposite, one, two), 1),
+                0,
+            )
+            for one in range(panels)
+            for two in range(one + 1, panels)
+        ]
         for step in range(len(bits)):
             far_steps = [scatter_step(one, order[step]) for one, order in zip(far_parts, orders)]
             steps = []
@@ -519,29 +533,23 @@
                 ]
             else:
                 crossed = jnp.concatenate(sums, 0)
-                steps = [(swap_cores(crossed), crossed)]
-            arrived, far_arrived = together([one for one, _ in steps], [one for one, _ in far_steps])
+                half = crossed.shape[0] // 2
+                sent = lax.dynamic_slice_in_dim(crossed, (1 - core) * half, half, 0)
+                kept = lax.dynamic_slice_in_dim(crossed, core * half, half, 0)
+                steps = [(swap_cores(sent), kept)]
+            others = [swap_rows(one, bits[step - 1]) for one in inner] if step else []
+            arrived, far_arrived, others = together(
+                [one for one, _ in steps], [one for one, _ in far_steps], others
+            )
+            inner = [one + two for one, two in zip(inner, others)] if step else inner
             sums = [one + kept for one, (_, kept) in zip(arrived, steps)]
             far_parts = [one + kept for one, (_, kept) in zip(far_arrived, far_steps)]
         (crossed,) = sums
 
-        def of(value, one, two):
-            return value[part * one : part * (one + 1), part * two : part * (two + 1)]
-
-        inner = [
-            ordered(
-                lower,
-                ordered(lower, of(same, one, two), of(mixed, one, two), 1),
-                ordered(lower, of(crossing, one, two), of(opposite, one, two), 1),
-                0,
-            )
-            for one in range(panels)
-            for two in range(one + 1, panels)
-        ]
         parts = [jnp.stack([one, two]) for one, two in zip(near_parts, far_parts)]
         hops = chips - 1
-        for step, bit in enumerate(bits):
-            others = [swap_rows(one, bit) for one in inner]
+        for step in range(len(bits)):
+            others = [swap_rows(one, bits[-1]) for one in inner] if step == 0 else []
             parts = [gather_step(one, order[-1 - step]) for one, order in zip(parts, orders)]
             if step < hops:
                 arrived, combine = line_step(crossed, step, chips)
@@ -549,7 +557,7 @@
                 crossed = combine(crossed, arrived)
             else:
                 parts, others = together(parts, others)
-            inner = [one + two for one, two in zip(inner, others)]
+            inner = [one + two for one, two in zip(inner, others)] if step == 0 else inner
         projected = jnp.concatenate(parts, 0).reshape(total, cols)
 
         for hop in range(len(bits), hops - 1):
@@ -561,6 +569,8 @@
             arrived, local, left, right = together(arrived, local, left, right)
             crossed = combine(crossed, arrived)
         everyone = [crossed] + [swap_rows(crossed, distance) for distance in range(1, row_count)]
+        others = swap_cores(jnp.stack(everyone))
+        everyone = [ordered(core == 0, one, others[place], 0) for place, one in enumerate(everyone)]
         crossed = jnp.zeros((2, total // 2, total), f32)
         for distance, value in enumerate(everyone):
             source = row ^ distance

time: 302 us -> 312 us (1.033)
  other arithmetic: 23.2 us -> 30.5 us
  local copies, waits for them, and re-layouts: 12.2 us -> 18.1 us
    dynamic_update_slice x0 -> x8, other arithmetic: none -> 7.44 us  [factors_of(): lax.dynamic_update_slice(crossed, value[other * size:(other + 1) * size][...]
    ppermute x3, waiting for transfers between devices: 7.42 us -> 0.01 us  [line_step(): lax.ppermute(value, 'col', [(2 * one + core, 2 * two + core) for one, two...]
    cond x30 -> x44, local copies, waits for them, and re-layouts: 4.54 us -> 10.6 us
    ppermute x30, waiting for transfers between devices: 56.2 us -> 60.7 us  [swap_rows(): lax.ppermute(value, 'row', [(row, row ^ distance) for row in range(count)])]
  transfers between devices with their start and end apart: 50 -> 51, of which waited for: 20 -> 19; matrix products, arithmetic and copies ran while one was open for 9% -> 11% of each run, Pallas kernels for 23% -> 22%
where the time goes in v6:
time: 312 us; the launch traced here: 310 us
  Pallas kernels  105 us (34%)
  waiting for transfers between devices  78.4 us (25%)
  starting transfers between devices  63.6 us (20%)
  other arithmetic  30.5 us (10%)
  local copies, waits for them, and re-layouts  18.1 us (6%)
  between operations  13.9 us (4%)
    ppermute x30, waiting for transfers between devices, swap_rows(): lax.ppermute(value, 'row', [(row, row ^ distance) for row in range(count)])  60.7 us
    pallas_call x1, Pallas kernels, finish(): call(finish_kernel, 52, (rows // block,), [pl.BlockSpec((block, cols), la...  37.4 us
    ppermute x30, starting transfers between devices, swap_rows(): lax.ppermute(value, 'row', [(row, row ^ distance) for row in range(count)])  33.8 us
    pallas_call x2, Pallas kernels, project(): call(functools.partial(project_kernel, pairs, len(vectors)), 36, (cols //...  28.5 us
    pallas_call x2, Pallas kernels, image(): call(image_kernel, 22, (rows // block,), [pl.BlockSpec((block, cols), lam...  19.3 us
    ppermute x4, starting transfers between devices, send_along(): lax.ppermute(value, 'col', [(2 * (chip - step) + core, 2 * chip + core) f...  12.7 us
    cond x44, local copies, waits for them, and re-layouts  10.6 us
    ppermute x6, waiting for transfers between devices, swap_chips(): lax.ppermute(value, 'col', [(col, col ^ 2 * distance) for col in range(co...  9.29 us
  transfers between devices with their start and end apart: 51, of which 19 were waited for; matrix products, arithmetic and copies ran while one was open for 11% of the time, Pallas kernels for 22%

profile of v6, /device:TPU:8, one launch (start us, length us, event | category | flops | bytes accessed | tf_op | source)
XLA Modules:
  0.0 310.2 jit_solution(1350844869574118639)
XLA Ops:
  7.6 3.5 %collective-permute-start.27 = (f32[2,32,3072]{2,1,0:T(8,128)}, f32[2,32,3072]{2,1,0:T(8,128)}, u32[]{:S(2)}, u32[]{:S(2)}) collective-permute-start(f32[2,32,3072]{2,1,0:T(8,128)} %bitcast.166), channel_id=1, source_target_pairs={{0,2},{1,3},{2,4},{3,5},{4,6},{5,7},{8,10},{9,11},{10,12},{11,13},... | collective-permute-start | bytes 2359304 | tf_op jit(solution)/shard_map/ppermute | solution.py:311
  11.1 3.3 %collective-permute-start.26 = (f32[2,32,3072]{2,1,0:T(8,128)}, f32[2,32,3072]{2,1,0:T(8,128)}, u32[]{:S(2)}, u32[]{:S(2)}) collective-permute-start(f32[2,32,3072]{2,1,0:T(8,128)} %bitcast.167), channel_id=1, source_target_pairs={{2,0},{3,1},{4,2},{5,3},{6,4},{7,5},{10,8},{11,9},{12,10},{13,11},... | collective-permute-start | bytes 2359304 | tf_op jit(solution)/shard_map/ppermute | solution.py:311
  15.7 2.5 collective-permute-start.31
  19.3 5.2 %collective-permute-done.31 = f32[2,16,1536]{2,1,0:T(8,128)S(1)} collective-permute-done((f32[2,16,1536]{2,1,0:T(8,128)S(1)}, f32[2,16,1536]{2,1,0:T(8,128)S(1)}, u32[]{:S(2)}, u32[]{:S(2)}) %collective-permute-start.31) | collective-permute-done | bytes 196640 | tf_op jit(solution)/shard_map/ppermute | solution.py:272
  24.5 3.1 %collective-permute-done.30 = f32[2,16,1536]{2,1,0:T(8,128)S(1)} collective-permute-done((f32[2,16,1536]{2,1,0:T(8,128)S(1)}, f32[2,16,1536]{2,1,0:T(8,128)S(1)}, u32[]{:S(2)}, u32[]{:S(2)}) %collective-permute-start.30) | collective-permute-done | bytes 196640 | tf_op jit(solution)/shard_map/ppermute | solution.py:272
  27.8 2.0 collective-permute-done.27
  29.8 3.2 %collective-permute-done.26 = f32[2,32,3072]{2,1,0:T(8,128)} collective-permute-done((f32[2,32,3072]{2,1,0:T(8,128)}, f32[2,32,3072]{2,1,0:T(8,128)}, u32[]{:S(2)}, u32[]{:S(2)}) %collective-permute-start.26) | collective-permute-done | bytes 786464 | tf_op jit(solution)/shard_map/ppermute | solution.py:311
  33.0 1.6 fusion.7
  35.0 1.6 collective-permute-start.35
  36.6 2.1 collective-permute-start.34
  38.9 1.4 collective-permute-start.41
  40.3 4.5 %collective-permute-done.35 = f32[16,1536]{1,0:T(8,128)S(1)} collective-permute-done((f32[16,1536]{1,0:T(8,128)S(1)}, f32[16,1536]{1,0:T(8,128)S(1)}, u32[]{:S(2)}, u32[]{:S(2)}) %collective-permute-start.35) | collective-permute-done | bytes 98336 | tf_op jit(solution)/shard_map/ppermute | solution.py:267
  44.9 4.8 %collective-permute-done.34 = f32[16,1536]{1,0:T(8,128)S(1)} collective-permute-done((f32[16,1536]{1,0:T(8,128)S(1)}, f32[16,1536]{1,0:T(8,128)S(1)}, u32[]{:S(2)}, u32[]{:S(2)}) %collective-permute-start.34) | collective-permute-done | bytes 98336 | tf_op jit(solution)/shard_map/ppermute | solution.py:267
  49.6 3.0 collective-permute-start.39
  53.3 2.5 collective-permute-start.38
  56.3 2.1 broadcast_select_fusion.13
  59.2 11.9 %shard_map.38 = (f32[256,1536]{1,0:T(8,128)S(1)}, f32[256,256]{1,0:T(8,128)}) custom-call(f32[256,3072]{1,0:T(8,128)S(1)} %bitcast.159, f32[3072,1536]{1,0:T(8,128)S(1)} %copy-done.6), custom_call_target="tpu_custom_call" | custom-call | flops 1 | bytes 1 | tf_op jit(solution)/shard_map/pallas_call | solution.py:76
  71.1 1.9 collective-permute-start.45
  73.0 4.0 %collective-permute-start.46 = (f32[2,32,3072]{2,1,0:T(8,128)}, f32[2,32,3072]{2,1,0:T(8,128)S(1)}, u32[]{:S(2)}, u32[]{:S(2)}) collective-permute-start(f32[2,32,3072]{2,1,0:T(8,128)} %collective-permute-done.27), channel_id=1, source_target_pairs={{2,4},{3,5},{4,6},{5,7},{10,12},{11,13},{12,14},{13,15},{18,20},{1... | collective-permute-start | bytes 2359304 | tf_op jit(solution)/shard_map/ppermute | solution.py:311
  77.1 2.5 collective-permute-start.44
  81.9 9.6 %shard_map.39 = f32[3072,256]{1,0:T(8,128)} custom-call(f32[3072,1536]{1,0:T(8,128)S(1)} %copy-done.6, f32[256,1536]{1,0:T(8,128)S(1)} %bitcast.156), custom_call_target="tpu_custom_call" | custom-call | flops 1 | bytes 1 | tf_op jit(solution)/shard_map/pallas_call | solution.py:108
  92.5 2.2 collective-permute-start.47
  94.7 1.5 collective-permute-start.48
  96.2 1.5 collective-permute-start.49
  97.9 9.7 %shard_map.40 = f32[3072,256]{1,0:T(8,128)} custom-call(f32[3072,1536]{1,0:T(8,128)S(1)} %copy-done.6, f32[256,1536]{1,0:T(8,128)S(1)} %bitcast.154), custom_call_target="tpu_custom_call" | custom-call | flops 1 | bytes 1 | tf_op jit(solution)/shard_map/pallas_call | solution.py:108
  108.5 1.8 pad_maximum_fusion.14
  110.5 155.4 %conditional.1 = (f32[256,3072]{1,0:T(8,128)}, bf16[1024,1536]{1,0:T(8,128)(2,1)}, bf16[1024,1536]{1,0:T(8,128)(2,1)}) conditional(s32[]{:T(128)} %convert_element_type.4, () %tuple.31, (pred[2,32,3072]{2,1,0:T(8,128)(4,1)S(1)}, f32[2,32,3072]{2,1,0:T(8,128)}, f32[2,32,3072]{2,1,0:T(8,128)S(1)}, pred[2,32,3072]{2,1,0:T(8,128)(4,1)S(1)}, ...), branch_computations={%region_0.1_spmd, %region_1.2_spmd} | conditional | flops 11010352 | bytes 218961056 | solution.py:455
  110.5 2.1 select_select_fusion.1
  112.8 1.1 dynamic-slice_add_fusion.3
  114.7 1.5 collective-permute-start.4
  116.3 1.9 dynamic-slice_add_fusion.2
  118.2 1.3 broadcast_select_fusion.7
  119.7 2.0 pad_maximum_fusion
  122.4 1.1 copy-done.8
  124.5 7.5 %branch_1_fun.5 = f32[512,512]{1,0:T(8,128)S(1)} custom-call(f32[256,3072]{1,0:T(8,128)S(1)} %copy-done.8, f32[256,3072]{1,0:T(8,128)} %bitcast.refs_0_.far_ref, f32[3072,256]{1,0:T(8,128)S(1)} %copy-done.9, f32[3072,256]{1,0:T(8,128)S(1)} %copy-done.10), custom_call_target="tpu_custom_call" | custom-call | flops 1 | bytes 1 | tf_op jit(solution)/shard_map/cond/branch_1_fun/pallas_call | solution.py:138
  133.0 1.5 collective-permute-start.2
  136.9 16.7 %branch_1_fun.4 = (f32[256,1536]{1,0:T(8,128)S(1)}, f32[256,256]{1,0:T(8,128)S(1)}, f32[256,256]{1,0:T(8,128)S(1)}, f32[256,256]{1,0:T(8,128)S(1)}) custom-call(f32[256,3072]{1,0:T(8,128)} %bitcast.refs_0_.far_ref, f32[256,3072]{1,0:T(8,128)S(1)} %copy-done.8, f32[3072,1536]{1,0:T(8,128)} %get-tuple-element.98.refs_2_), custom_call_target="tpu_custom_call" | custom-call | flops 1 | bytes 1 | tf_op jit(solution)/shard_map/cond/branch_1_fun/pallas_call | solution.py:76
  154.7 1.6 collective-permute-start.6
  157.3 1.5 collective-permute-start.7
  160.5 1.5 collective-permute-start.8
  163.6 12.7 %collective-permute-done.8 = f32[64,1536]{1,0:T(8,128)S(1)} collective-permute-done((f32[64,1536]{1,0:T(8,128)S(1)}, f32[64,1536]{1,0:T(8,128)S(1)}, u32[]{:S(2)}, u32[]{:S(2)}) %collective-permute-start.8) | collective-permute-done | bytes 393248 | tf_op jit(solution)/shard_map/cond/branch_1_fun/ppermute | solution.py:272
  176.7 1.2 collective-permute-start.12
  179.4 4.6 %collective-permute-done.12 = f32[32,1536]{1,0:T(8,128)S(1)} collective-permute-done((f32[32,1536]{1,0:T(8,128)S(1)}, f32[32,1536]{1,0:T(8,128)S(1)}, u32[]{:S(2)}, u32[]{:S(2)}) %collective-permute-start.12) | collective-permute-done | bytes 196640 | tf_op jit(solution)/shard_map/cond/branch_1_fun/ppermute | solution.py:272
  185.0 1.3 collective-permute-start.17
  188.0 1.6 collective-permute-start.14
  189.5 7.3 %collective-permute-done.15 = f32[2,32,1536]{2,1,0:T(8,128)S(1)} collective-permute-done((f32[2,32,1536]{2,1,0:T(8,128)S(1)}, f32[2,32,1536]{2,1,0:T(8,128)S(1)}, u32[]{:S(2)}, u32[]{:S(2)}) %collective-permute-start.15) | collective-permute-done | bytes 393248 | tf_op jit(solution)/shard_map/cond/branch_1_fun/ppermute | solution.py:272
  196.9 6.3 %collective-permute-done.14 = f32[2,32,1536]{2,1,0:T(8,128)S(1)} collective-permute-done((f32[2,32,1536]{2,1,0:T(8,128)S(1)}, f32[2,32,1536]{2,1,0:T(8,128)S(1)}, u32[]{:S(2)}, u32[]{:S(2)}) %collective-permute-start.14) | collective-permute-done | bytes 393248 | tf_op jit(solution)/shard_map/cond/branch_1_fun/ppermute | solution.py:272
  203.4 1.2 collective-permute-start.18
  204.6 1.9 collective-permute-start.20
  207.2 14.0 %collective-permute-done.18 = f32[2,64,1536]{2,1,0:T(8,128)S(1)} collective-permute-done((f32[2,64,1536]{2,1,0:T(8,128)S(1)}, f32[2,64,1536]{2,1,0:T(8,128)S(1)}, u32[]{:S(2)}, u32[]{:S(2)}) %collective-permute-start.18) | collective-permute-done | bytes 786464 | tf_op jit(solution)/shard_map/cond/branch_1_fun/ppermute | solution.py:272
  221.4 2.6 collective-permute-done.19
  224.4 3.1 collective-permute-start.21
  227.7 1.7 copy-done.11
  229.4 5.9 %branch_1_fun.6 = (f32[512,512]{1,0:T(8,128)S(1)}, f32[512,1536]{1,0:T(8,128)S(1)}, bf16[512,1536]{1,0:T(8,128)(2,1)S(1)}, bf16[512,1536]{1,0:T(8,128)(2,1)S(1)}) custom-call(s32[1]{0:T(128)} %bitcast.5.lower_ref, f32[512,1536]{1,0:T(8,128)S(1)} %bitcast.158, f32[512,1536]{1,0:T(8,128)S(1)} %copy-done.11, f32[2,256,256]{2,1,0:T(8,128)S(1)} %copy-done.29, ...), custom_call_target="tpu_custom_call" | custom-call | flops 1 | bytes 1 | tf_op jit(solution)/shard_map/cond/branch_1_fun/pallas_call | solution.py:194
  235.3 1.2 copy-done
  236.5 1.2 copy-done.2
  239.6 1.5 collective-permute-start.23
  241.1 1.1 collective-permute-start.22
  242.2 2.5 collective-permute-done.24
  244.7 1.2 collective-permute-done.23
  247.6 2.2 collective-permute-done.25
  257.6 1.2 copy-done.3
  259.7 6.3 %branch_1_fun.7 = (bf16[1024,1536]{1,0:T(8,128)(2,1)}, bf16[1024,1536]{1,0:T(8,128)(2,1)}) custom-call(f32[512,512]{1,0:T(8,128)S(1)} %copy-done.5, f32[512,512]{1,0:T(8,128)S(1)} %pad_maximum_fusion.4.crossed_ref, f32[512,1536]{1,0:T(8,128)S(1)} %get-tuple-element.146.left_ref, bf16[512,1536]{1,0:T(8,128)(2,1)S(1)} %copy-done.1, bf16[512,1536]{1,0:T(8,128)(2,1)S(1)} %copy-done.3), custom_call_target="tpu_custom_call" | custom-call | flops 1 | bytes 1 | tf_op jit(solution)/shard_map/cond/branch_1_fun/pallas_call | solution.py:222
  265.9 37.4 %shard_map.41 = f32[3072,1536]{1,0:T(8,128)} custom-call(f32[3072,1536]{1,0:T(8,128)} %window_ref.5, f32[256,3072]{1,0:T(8,128)} %bitcast.161, f32[256,3072]{1,0:T(8,128)} %get-tuple-element.224.far_ref, bf16[1024,1536]{1,0:T(8,128)(2,1)} %get-tuple-element.225.high_ref, bf16[1024,1536]{1,0:T(8,128)(2,1)} %get-tuple-element.226.low_ref, ...), custom_call_target="tpu_custom_call" | custom-call | flops 1 | bytes 1 | tf_op jit(solution)/shard_map/pallas_call | solution.py:244
  (213 shorter events, 39.8 us)
Async XLA Ops:
  6.5 259.4 %all-reduce.3.cloned.1.call-start = ((), (), s32[]{:S(2)}) async-start(), calls=%async_computation | async-start | bytes 12582912 | tf_op jit(solution)/shard_map/psum | solution.py:492
  7.6 6.9 %collective-permute-start.28 = (f32[2,32,1536]{2,1,0:T(8,128)S(1)}, f32[2,32,1536]{2,1,0:T(8,128)S(1)}, u32[]{:S(2)}, u32[]{:S(2)}) collective-permute-start(f32[2,32,1536]{2,1,0:T(8,128)S(1)} %dynamic-slice_bitcast_fusion), channel_id=1, source_target_pairs={{0,1},{1,0},{2,3},{3,2},{4,5},{5,4},{6,7},{7,6},{8,9},{9,8},{10,11... | collective-permute-start | bytes 1179656 | tf_op jit(solution)/shard_map/ppermute | solution.py:262
  7.6 22.1 %collective-permute-start.27 = (f32[2,32,3072]{2,1,0:T(8,128)}, f32[2,32,3072]{2,1,0:T(8,128)}, u32[]{:S(2)}, u32[]{:S(2)}) collective-permute-start(f32[2,32,3072]{2,1,0:T(8,128)} %bitcast.166), channel_id=1, source_target_pairs={{0,2},{1,3},{2,4},{3,5},{4,6},{5,7},{8,10},{9,11},{10,12},{11,13},... | collective-permute-start | bytes 2359304 | tf_op jit(solution)/shard_map/ppermute | solution.py:311
  11.1 21.9 %collective-permute-start.26 = (f32[2,32,3072]{2,1,0:T(8,128)}, f32[2,32,3072]{2,1,0:T(8,128)}, u32[]{:S(2)}, u32[]{:S(2)}) collective-permute-start(f32[2,32,3072]{2,1,0:T(8,128)} %bitcast.167), channel_id=1, source_target_pairs={{2,0},{3,1},{4,2},{5,3},{6,4},{7,5},{10,8},{11,9},{12,10},{13,11},... | collective-permute-start | bytes 2359304 | tf_op jit(solution)/shard_map/ppermute | solution.py:311
  15.6 17.4 %copy-start.12 = (f32[2,3072,32]{1,2,0:T(8,128)S(1)}, f32[2,3072,32]{1,2,0:T(8,128)}, u32[]{:S(2)}) copy-start(f32[2,3072,32]{1,2,0:T(8,128)} %param.6) | copy-start | bytes 2359300
  15.7 8.8 %collective-permute-start.31 = (f32[2,16,1536]{2,1,0:T(8,128)S(1)}, f32[2,16,1536]{2,1,0:T(8,128)S(1)}, u32[]{:S(2)}, u32[]{:S(2)}) collective-permute-start(f32[2,16,1536]{2,1,0:T(8,128)S(1)} %get-tuple-element.276), channel_id=1, source_target_pairs={{0,24},{8,16},{16,8},{24,0},{1,25},{9,17},{17,9},{25,1},{2,26},{10... | collective-permute-start | bytes 589832 | tf_op jit(solution)/shard_map/ppermute | solution.py:272
  18.3 9.4 %collective-permute-start.30 = (f32[2,16,1536]{2,1,0:T(8,128)S(1)}, f32[2,16,1536]{2,1,0:T(8,128)S(1)}, u32[]{:S(2)}, u32[]{:S(2)}) collective-permute-start(f32[2,16,1536]{2,1,0:T(8,128)S(1)} %get-tuple-element.277), channel_id=1, source_target_pairs={{0,16},{8,24},{16,0},{24,8},{1,17},{9,25},{17,1},{25,9},{2,18},{10... | collective-permute-start | bytes 589832 | tf_op jit(solution)/shard_map/ppermute | solution.py:272
  18.8 9.0 %collective-permute-start.29 = (f32[2,16,1536]{2,1,0:T(8,128)S(1)}, f32[2,16,1536]{2,1,0:T(8,128)S(1)}, u32[]{:S(2)}, u32[]{:S(2)}) collective-permute-start(f32[2,16,1536]{2,1,0:T(8,128)S(1)} %get-tuple-element.278), channel_id=1, source_target_pairs={{0,8},{8,0},{16,24},{24,16},{1,9},{9,1},{17,25},{25,17},{2,10},{10... | collective-permute-start | bytes 589832 | tf_op jit(solution)/shard_map/ppermute | solution.py:272
  34.7 17.9 %collective-permute-start.32 = (f32[2,2,32,3072]{3,2,0,1:T(8,128)S(1)}, f32[2,2,32,3072]{3,2,0,1:T(8,128)S(1)}, u32[]{:S(2)}, u32[]{:S(2)}) collective-permute-start(f32[2,2,32,3072]{3,2,0,1:T(8,128)S(1)} %pad_maximum_fusion.15), channel_id=1, source_target_pairs={{0,1},{1,0},{2,3},{3,2},{4,5},{5,4},{6,7},{7,6},{8,9},{9,8},{10,11... | collective-permute-start | bytes 4718600 | tf_op jit(solution)/shard_map/ppermute | solution.py:262
  35.0 9.9 %collective-permute-start.35 = (f32[16,1536]{1,0:T(8,128)S(1)}, f32[16,1536]{1,0:T(8,128)S(1)}, u32[]{:S(2)}, u32[]{:S(2)}) collective-permute-start(f32[16,1536]{1,0:T(8,128)S(1)} %get-tuple-element.284), channel_id=1, source_target_pairs={{0,6},{1,7},{2,4},{3,5},{4,2},{5,3},{6,0},{7,1},{8,14},{9,15},{10,... | collective-permute-start | bytes 294920 | tf_op jit(solution)/shard_map/ppermute | solution.py:267
  36.6 13.0 %collective-permute-start.34 = (f32[16,1536]{1,0:T(8,128)S(1)}, f32[16,1536]{1,0:T(8,128)S(1)}, u32[]{:S(2)}, u32[]{:S(2)}) collective-permute-start(f32[16,1536]{1,0:T(8,128)S(1)} %get-tuple-element.285), channel_id=1, source_target_pairs={{0,4},{1,5},{2,6},{3,7},{4,0},{5,1},{6,2},{7,3},{8,12},{9,13},{10,... | collective-permute-start | bytes 294920 | tf_op jit(solution)/shard_map/ppermute | solution.py:267
  38.7 13.9 %collective-permute-start.33 = (f32[16,1536]{1,0:T(8,128)S(1)}, f32[16,1536]{1,0:T(8,128)S(1)}, u32[]{:S(2)}, u32[]{:S(2)}) collective-permute-start(f32[16,1536]{1,0:T(8,128)S(1)} %get-tuple-element.286), channel_id=1, source_target_pairs={{0,2},{1,3},{2,0},{3,1},{4,6},{5,7},{6,4},{7,5},{8,10},{9,11},{10,... | collective-permute-start | bytes 294920 | tf_op jit(solution)/shard_map/ppermute | solution.py:267
  38.8 20.4 %copy-start.6 = (f32[3072,1536]{1,0:T(8,128)S(1)}, f32[3072,1536]{1,0:T(8,128)}, u32[]{:S(2)}) copy-start(f32[3072,1536]{1,0:T(8,128)} %window_ref.5) | copy-start | bytes 56623108
  38.9 19.5 %collective-permute-start.41 = (f32[16,1536]{1,0:T(8,128)S(1)}, f32[16,1536]{1,0:T(8,128)S(1)}, u32[]{:S(2)}, u32[]{:S(2)}) collective-permute-start(f32[16,1536]{1,0:T(8,128)S(1)} %get-tuple-element.281), channel_id=1, source_target_pairs={{0,6},{1,7},{2,4},{3,5},{4,2},{5,3},{6,0},{7,1},{8,14},{9,15},{10,... | collective-permute-start | bytes 294920 | tf_op jit(solution)/shard_map/ppermute | solution.py:267
  44.8 26.2 %collective-permute-start.40 = (f32[16,1536]{1,0:T(8,128)S(1)}, f32[16,1536]{1,0:T(8,128)S(1)}, u32[]{:S(2)}, u32[]{:S(2)}) collective-permute-start(f32[16,1536]{1,0:T(8,128)S(1)} %get-tuple-element.282), channel_id=1, source_target_pairs={{0,4},{1,5},{2,6},{3,7},{4,0},{5,1},{6,2},{7,3},{8,12},{9,13},{10,... | collective-permute-start | bytes 294920 | tf_op jit(solution)/shard_map/ppermute | solution.py:267
  49.6 23.4 %collective-permute-start.39 = (f32[16,1536]{1,0:T(8,128)S(1)}, f32[16,1536]{1,0:T(8,128)S(1)}, u32[]{:S(2)}, u32[]{:S(2)}) collective-permute-start(f32[16,1536]{1,0:T(8,128)S(1)} %get-tuple-element.283), channel_id=1, source_target_pairs={{0,2},{1,3},{2,0},{3,1},{4,6},{5,7},{6,4},{7,5},{8,10},{9,11},{10,... | collective-permute-start | bytes 294920 | tf_op jit(solution)/shard_map/ppermute | solution.py:267
  53.3 5.9 %copy-start.7 = (f32[2,128,3072]{2,1,0:T(8,128)}, f32[2,128,3072]{2,1,0:T(8,128)S(1)}, u32[]{:S(2)}) copy-start(f32[2,128,3072]{2,1,0:T(8,128)S(1)} %pad_maximum_fusion.13) | copy-start | bytes 9437188
  53.3 23.7 %collective-permute-start.38 = (f32[4,16,1536]{2,1,0:T(8,128)S(1)}, f32[4,16,1536]{2,1,0:T(8,128)S(1)}, u32[]{:S(2)}, u32[]{:S(2)}) collective-permute-start(f32[4,16,1536]{2,1,0:T(8,128)S(1)} %bitcast_dynamic-update-slice_fusion.23), channel_id=1, source_target_pairs={{0,24},{8,16},{16,8},{24,0},{1,25},{9,17},{17,9},{25,1},{2,26},{10... | collective-permute-start | bytes 1179656 | tf_op jit(solution)/shard_map/ppermute | solution.py:272
  55.8 21.2 %collective-permute-start.37 = (f32[4,16,1536]{2,1,0:T(8,128)S(1)}, f32[4,16,1536]{2,1,0:T(8,128)S(1)}, u32[]{:S(2)}, u32[]{:S(2)}) collective-permute-start(f32[4,16,1536]{2,1,0:T(8,128)S(1)} %bitcast_dynamic-update-slice_fusion.23), channel_id=1, source_target_pairs={{0,16},{8,24},{16,0},{24,8},{1,17},{9,25},{17,1},{25,9},{2,18},{10... | collective-permute-start | bytes 1179656 | tf_op jit(solution)/shard_map/ppermute | solution.py:272
  58.4 18.6 %collective-permute-start.36 = (f32[4,16,1536]{2,1,0:T(8,128)S(1)}, f32[4,16,1536]{2,1,0:T(8,128)S(1)}, u32[]{:S(2)}, u32[]{:S(2)}) collective-permute-start(f32[4,16,1536]{2,1,0:T(8,128)S(1)} %bitcast_dynamic-update-slice_fusion.23), channel_id=1, source_target_pairs={{0,8},{8,0},{16,24},{24,16},{1,9},{9,1},{17,25},{25,17},{2,10},{10... | collective-permute-start | bytes 1179656 | tf_op jit(solution)/shard_map/ppermute | solution.py:272
  71.1 21.4 %collective-permute-start.45 = (f32[2,32,3072]{2,1,0:T(8,128)}, f32[2,32,3072]{2,1,0:T(8,128)S(1)}, u32[]{:S(2)}, u32[]{:S(2)}) collective-permute-start(f32[2,32,3072]{2,1,0:T(8,128)} %collective-permute-done.26), channel_id=1, source_target_pairs={{2,0},{3,1},{4,2},{5,3},{10,8},{11,9},{12,10},{13,11},{18,16},{19,... | collective-permute-start | bytes 2359304 | tf_op jit(solution)/shard_map/ppermute | solution.py:311
  73.0 21.7 %collective-permute-start.46 = (f32[2,32,3072]{2,1,0:T(8,128)}, f32[2,32,3072]{2,1,0:T(8,128)S(1)}, u32[]{:S(2)}, u32[]{:S(2)}) collective-permute-start(f32[2,32,3072]{2,1,0:T(8,128)} %collective-permute-done.27), channel_id=1, source_target_pairs={{2,4},{3,5},{4,6},{5,7},{10,12},{11,13},{12,14},{13,15},{18,20},{1... | collective-permute-start | bytes 2359304 | tf_op jit(solution)/shard_map/ppermute | solution.py:311
  77.1 19.1 %collective-permute-start.44 = (f32[4,16,1536]{2,1,0:T(8,128)S(1)}, f32[4,16,1536]{2,1,0:T(8,128)S(1)}, u32[]{:S(2)}, u32[]{:S(2)}) collective-permute-start(f32[4,16,1536]{2,1,0:T(8,128)S(1)} %bitcast_dynamic-update-slice_fusion.19), channel_id=1, source_target_pairs={{0,24},{8,16},{16,8},{24,0},{1,25},{9,17},{17,9},{25,1},{2,26},{10... | collective-permute-start | bytes 1179656 | tf_op jit(solution)/shard_map/ppermute | solution.py:272
  79.6 18.1 %collective-permute-start.43 = (f32[4,16,1536]{2,1,0:T(8,128)S(1)}, f32[4,16,1536]{2,1,0:T(8,128)S(1)}, u32[]{:S(2)}, u32[]{:S(2)}) collective-permute-start(f32[4,16,1536]{2,1,0:T(8,128)S(1)} %bitcast_dynamic-update-slice_fusion.19), channel_id=1, source_target_pairs={{0,16},{8,24},{16,0},{24,8},{1,17},{9,25},{17,1},{25,9},{2,18},{10... | collective-permute-start | bytes 1179656 | tf_op jit(solution)/shard_map/ppermute | solution.py:272
  80.1 17.6 %collective-permute-start.42 = (f32[4,16,1536]{2,1,0:T(8,128)S(1)}, f32[4,16,1536]{2,1,0:T(8,128)S(1)}, u32[]{:S(2)}, u32[]{:S(2)}) collective-permute-start(f32[4,16,1536]{2,1,0:T(8,128)S(1)} %bitcast_dynamic-update-slice_fusion.19), channel_id=1, source_target_pairs={{0,8},{8,0},{16,24},{24,16},{1,9},{9,1},{17,25},{25,17},{2,10},{10... | collective-permute-start | bytes 1179656 | tf_op jit(solution)/shard_map/ppermute | solution.py:272
  80.8 10.7 %copy-start.15 = (f32[128,1536]{1,0:T(8,128)}, f32[128,1536]{1,0:T(8,128)S(1)}, u32[]{:S(2)}) copy-start(f32[128,1536]{1,0:T(8,128)S(1)} %get-tuple-element.268) | copy-start | bytes 2359300
  92.5 5.3 %copy-start.25 = (f32[2,32,3072]{2,1,0:T(8,128)}, f32[2,32,3072]{2,1,0:T(8,128)S(1)}, u32[]{:S(2)}) copy-start(f32[2,32,3072]{2,1,0:T(8,128)S(1)} %collective-permute-done.45) | copy-start | bytes 2359300
  92.5 15.9 %collective-permute-start.47 = (f32[2,32,3072]{2,1,0:T(8,128)}, f32[2,32,3072]{2,1,0:T(8,128)}, u32[]{:S(2)}, u32[]{:S(2)}) collective-permute-start(f32[2,32,3072]{2,1,0:T(8,128)} %broadcast_select_fusion.13), channel_id=1, source_target_pairs={{4,0},{5,1},{2,6},{3,7},{12,8},{13,9},{10,14},{11,15},{20,16},{21,... | collective-permute-start | bytes 2359304 | tf_op jit(solution)/shard_map/ppermute | solution.py:404
  94.7 13.7 %collective-permute-start.48 = (f32[64,1536]{1,0:T(8,128)}, f32[64,1536]{1,0:T(8,128)S(1)}, u32[]{:S(2)}, u32[]{:S(2)}) collective-permute-start(f32[64,1536]{1,0:T(8,128)} %constant_dynamic-slice_fusion.10), channel_id=1, source_target_pairs={{0,8},{8,0},{16,24},{24,16},{1,9},{9,1},{17,25},{25,17},{2,10},{10... | collective-permute-start | bytes 1179656 | tf_op jit(solution)/shard_map/ppermute | solution.py:272
  96.2 12.2 %collective-permute-start.49 = (f32[64,1536]{1,0:T(8,128)}, f32[64,1536]{1,0:T(8,128)}, u32[]{:S(2)}, u32[]{:S(2)}) collective-permute-start(f32[64,1536]{1,0:T(8,128)} %constant_dynamic-slice_fusion.11), channel_id=1, source_target_pairs={{0,16},{8,24},{16,0},{24,8},{1,17},{9,25},{17,1},{25,9},{2,18},{10... | collective-permute-start | bytes 1179656 | tf_op jit(solution)/shard_map/ppermute | solution.py:272
  112.7 3.6 %copy-start.14 = (f32[128,1536]{1,0:T(8,128)S(1)}, f32[128,1536]{1,0:T(8,128)}, u32[]{:S(2)}) copy-start(f32[128,1536]{1,0:T(8,128)} %get-tuple-element.110) | copy-start | bytes 2359300 | tf_op jit(solution)/shard_map/cond
  112.7 5.5 %collective-permute-start = (f32[2,32,3072]{2,1,0:T(8,128)S(1)}, f32[2,32,3072]{2,1,0:T(8,128)}, u32[]{:S(2)}, u32[]{:S(2)}) collective-permute-start(f32[2,32,3072]{2,1,0:T(8,128)S(1)} %get-tuple-element.231), channel_id=1, source_target_pairs={{0,1},{1,0},{2,3},{3,2},{4,5},{5,4},{6,7},{7,6},{8,9},{9,8},{10,11... | collective-permute-start | bytes 2359304 | tf_op jit(solution)/shard_map/cond/branch_1_fun/ppermute | solution.py:262
  114.7 38.9 %collective-permute-start.4 = (f32[32,1536]{1,0:T(8,128)}, f32[32,1536]{1,0:T(8,128)}, u32[]{:S(2)}, u32[]{:S(2)}) collective-permute-start(f32[32,1536]{1,0:T(8,128)} %constant_dynamic-slice_fusion.7), channel_id=1, source_target_pairs={{0,16},{8,24},{16,0},{24,8},{1,17},{9,25},{17,1},{25,9},{2,18},{10... | collective-permute-start | bytes 589832 | tf_op jit(solution)/shard_map/cond/branch_1_fun/ppermute | solution.py:272
  116.2 3.3 %collective-permute-start.1 = (f32[2,32,3072]{2,1,0:T(8,128)S(1)}, f32[2,32,3072]{2,1,0:T(8,128)S(1)}, u32[]{:S(2)}, u32[]{:S(2)}) collective-permute-start(f32[2,32,3072]{2,1,0:T(8,128)S(1)} %get-tuple-element.232), channel_id=1, source_target_pairs={{0,1},{1,0},{2,3},{3,2},{4,5},{5,4},{6,7},{7,6},{8,9},{9,8},{10,11... | collective-permute-start | bytes 2359304 | tf_op jit(solution)/shard_map/cond/branch_1_fun/ppermute | solution.py:262
  119.6 3.9 %copy-start.8 = (f32[256,3072]{1,0:T(8,128)S(1)}, f32[256,3072]{1,0:T(8,128)}, u32[]{:S(2)}) copy-start(f32[256,3072]{1,0:T(8,128)} %get-tuple-element.97.refs_1_.near_ref) | copy-start | bytes 9437188 | tf_op jit(solution)/shard_map/cond
  119.6 4.8 %copy-start.9 = (f32[3072,256]{1,0:T(8,128)S(1)}, f32[3072,256]{1,0:T(8,128)}, u32[]{:S(2)}) copy-start(f32[3072,256]{1,0:T(8,128)} %get-tuple-element.104.refs_0_) | copy-start | bytes 9437188 | tf_op jit(solution)/shard_map/cond
  132.0 3.7 %copy-start.21 = (f32[64,1536]{1,0:T(8,128)S(1)}, f32[64,1536]{1,0:T(8,128)}, u32[]{:S(2)}) copy-start(f32[64,1536]{1,0:T(8,128)} %dynamic-slice_add_fusion.2) | copy-start | bytes 1179652 | tf_op jit(solution)/shard_map/cond
  133.0 20.7 %collective-permute-start.2 = (f32[128,512]{1,0:T(8,128)}, f32[128,512]{1,0:T(8,128)}, u32[]{:S(2)}, u32[]{:S(2)}) collective-permute-start(f32[128,512]{1,0:T(8,128)} %constant_dynamic-slice_fusion.9), channel_id=1, source_target_pairs={{0,8},{8,0},{16,24},{24,16},{1,9},{9,1},{17,25},{25,17},{2,10},{10... | collective-permute-start | bytes 786440 | tf_op jit(solution)/shard_map/cond/branch_1_fun/ppermute | solution.py:272
  135.2 18.5 %collective-permute-start.3 = (f32[128,512]{1,0:T(8,128)}, f32[128,512]{1,0:T(8,128)}, u32[]{:S(2)}, u32[]{:S(2)}) collective-permute-start(f32[128,512]{1,0:T(8,128)} %constant_dynamic-slice_fusion.8), channel_id=1, source_target_pairs={{0,16},{8,24},{16,0},{24,8},{1,17},{9,25},{17,1},{25,9},{2,18},{10... | collective-permute-start | bytes 786440 | tf_op jit(solution)/shard_map/cond/branch_1_fun/ppermute | solution.py:272
  136.4 17.2 %collective-permute-start.5 = (f32[32,1536]{1,0:T(8,128)}, f32[32,1536]{1,0:T(8,128)}, u32[]{:S(2)}, u32[]{:S(2)}) collective-permute-start(f32[32,1536]{1,0:T(8,128)} %constant_dynamic-slice_fusion.6), channel_id=1, source_target_pairs={{0,8},{8,0},{16,24},{24,16},{1,9},{9,1},{17,25},{25,17},{2,10},{10... | collective-permute-start | bytes 589832 | tf_op jit(solution)/shard_map/cond/branch_1_fun/ppermute | solution.py:272
  136.9 16.7 %copy-start.20 = (f32[256,512]{1,0:T(8,128)S(1)}, f32[256,512]{1,0:T(8,128)}, u32[]{:S(2)}) copy-start(f32[256,512]{1,0:T(8,128)} %copy-done.19) | copy-start | bytes 1572868 | tf_op jit(solution)/shard_map/cond
  136.9 19.3 %copy-start.18 = (f32[256,512]{1,0:T(8,128)S(1)}, f32[256,512]{1,0:T(8,128)}, u32[]{:S(2)}) copy-start(f32[256,512]{1,0:T(8,128)} %copy-done.17) | copy-start | bytes 1572868 | tf_op jit(solution)/shard_map/cond
  154.7 8.9 %collective-permute-start.6 = (f32[64,512]{1,0:T(8,128)S(1)}, f32[64,512]{1,0:T(8,128)S(1)}, u32[]{:S(2)}, u32[]{:S(2)}) collective-permute-start(f32[64,512]{1,0:T(8,128)S(1)} %constant_dynamic-slice_fusion.5), channel_id=1, source_target_pairs={{0,16},{8,24},{16,0},{24,8},{1,17},{9,25},{17,1},{25,9},{2,18},{10... | collective-permute-start | bytes 393224 | tf_op jit(solution)/shard_map/cond/branch_1_fun/ppermute | solution.py:272
  157.3 6.3 %collective-permute-start.7 = (f32[64,512]{1,0:T(8,128)S(1)}, f32[64,512]{1,0:T(8,128)S(1)}, u32[]{:S(2)}, u32[]{:S(2)}) collective-permute-start(f32[64,512]{1,0:T(8,128)S(1)} %constant_dynamic-slice_fusion.4), channel_id=1, source_target_pairs={{0,8},{8,0},{16,24},{24,16},{1,9},{9,1},{17,25},{25,17},{2,10},{10... | collective-permute-start | bytes 393224 | tf_op jit(solution)/shard_map/cond/branch_1_fun/ppermute | solution.py:272
  159.7 19.7 %collective-permute-start.13 = (f32[256,256]{1,0:T(8,128)S(1)}, f32[256,256]{1,0:T(8,128)S(1)}, u32[]{:S(2)}, u32[]{:S(2)}) collective-permute-start(f32[256,256]{1,0:T(8,128)S(1)} %pad_maximum_fusion.10), channel_id=1, source_target_pairs={{0,8},{8,0},{16,24},{24,16},{1,9},{9,1},{17,25},{25,17},{2,10},{10... | collective-permute-start | bytes 786440 | tf_op jit(solution)/shard_map/cond/branch_1_fun/ppermute | solution.py:272
  160.5 15.8 %collective-permute-start.8 = (f32[64,1536]{1,0:T(8,128)S(1)}, f32[64,1536]{1,0:T(8,128)S(1)}, u32[]{:S(2)}, u32[]{:S(2)}) collective-permute-start(f32[64,1536]{1,0:T(8,128)S(1)} %constant_dynamic-slice_fusion.3), channel_id=1, source_target_pairs={{0,8},{8,0},{16,24},{24,16},{1,9},{9,1},{17,25},{25,17},{2,10},{10... | collective-permute-start | bytes 1179656 | tf_op jit(solution)/shard_map/cond/branch_1_fun/ppermute | solution.py:272
  162.1 14.2 %collective-permute-start.9 = (f32[64,1536]{1,0:T(8,128)S(1)}, f32[64,1536]{1,0:T(8,128)S(1)}, u32[]{:S(2)}, u32[]{:S(2)}) collective-permute-start(f32[64,1536]{1,0:T(8,128)S(1)} %constant_dynamic-slice_fusion.2), channel_id=1, source_target_pairs={{0,16},{8,24},{16,0},{24,8},{1,17},{9,25},{17,1},{25,9},{2,18},{10... | collective-permute-start | bytes 1179656 | tf_op jit(solution)/shard_map/cond/branch_1_fun/ppermute | solution.py:272
  176.6 2.9 collective-permute-start.10
  176.7 7.4 %collective-permute-start.12 = (f32[32,1536]{1,0:T(8,128)S(1)}, f32[32,1536]{1,0:T(8,128)S(1)}, u32[]{:S(2)}, u32[]{:S(2)}) collective-permute-start(f32[32,1536]{1,0:T(8,128)S(1)} %constant_dynamic-slice_fusion), channel_id=1, source_target_pairs={{0,8},{8,0},{16,24},{24,16},{1,9},{9,1},{17,25},{25,17},{2,10},{10... | collective-permute-start | bytes 589832 | tf_op jit(solution)/shard_map/cond/branch_1_fun/ppermute | solution.py:272
  177.9 7.0 %collective-permute-start.11 = (f32[32,1536]{1,0:T(8,128)S(1)}, f32[32,1536]{1,0:T(8,128)S(1)}, u32[]{:S(2)}, u32[]{:S(2)}) collective-permute-start(f32[32,1536]{1,0:T(8,128)S(1)} %constant_dynamic-slice_fusion.1), channel_id=1, source_target_pairs={{0,16},{8,24},{16,0},{24,8},{1,17},{9,25},{17,1},{25,9},{2,18},{10... | collective-permute-start | bytes 589832 | tf_op jit(solution)/shard_map/cond/branch_1_fun/ppermute | solution.py:272
  185.0 18.3 %collective-permute-start.17 = (f32[64,512]{1,0:T(8,128)S(1)}, f32[64,512]{1,0:T(8,128)S(1)}, u32[]{:S(2)}, u32[]{:S(2)}) collective-permute-start(f32[64,512]{1,0:T(8,128)S(1)} %fusion.1), channel_id=1, source_target_pairs={{0,2},{1,3},{6,4},{7,5},{8,10},{9,11},{14,12},{15,13},{16,18},{17,... | collective-permute-start | bytes 393224 | tf_op jit(solution)/shard_map/cond/branch_1_fun/ppermute | solution.py:437
  186.4 10.5 %collective-permute-start.15 = (f32[2,32,1536]{2,1,0:T(8,128)S(1)}, f32[2,32,1536]{2,1,0:T(8,128)S(1)}, u32[]{:S(2)}, u32[]{:S(2)}) collective-permute-start(f32[2,32,1536]{2,1,0:T(8,128)S(1)} %pad_maximum_fusion.9), channel_id=1, source_target_pairs={{0,8},{8,0},{16,24},{24,16},{1,9},{9,1},{17,25},{25,17},{2,10},{10... | collective-permute-start | bytes 1179656 | tf_op jit(solution)/shard_map/cond/branch_1_fun/ppermute | solution.py:272
  187.4 16.0 %collective-permute-start.16 = (f32[256,256]{1,0:T(8,128)S(1)}, f32[256,256]{1,0:T(8,128)S(1)}, u32[]{:S(2)}, u32[]{:S(2)}) collective-permute-start(f32[256,256]{1,0:T(8,128)S(1)} %fusion.5), channel_id=1, source_target_pairs={{0,16},{8,24},{16,0},{24,8},{1,17},{9,25},{17,1},{25,9},{2,18},{10... | collective-permute-start | bytes 786440 | tf_op jit(solution)/shard_map/cond/branch_1_fun/ppermute | solution.py:272
  188.0 15.2 %collective-permute-start.14 = (f32[2,32,1536]{2,1,0:T(8,128)S(1)}, f32[2,32,1536]{2,1,0:T(8,128)S(1)}, u32[]{:S(2)}, u32[]{:S(2)}) collective-permute-start(f32[2,32,1536]{2,1,0:T(8,128)S(1)} %pad_maximum_fusion.8), channel_id=1, source_target_pairs={{0,16},{8,24},{16,0},{24,8},{1,17},{9,25},{17,1},{25,9},{2,18},{10... | collective-permute-start | bytes 1179656 | tf_op jit(solution)/shard_map/cond/branch_1_fun/ppermute | solution.py:272
  203.4 17.8 %collective-permute-start.18 = (f32[2,64,1536]{2,1,0:T(8,128)S(1)}, f32[2,64,1536]{2,1,0:T(8,128)S(1)}, u32[]{:S(2)}, u32[]{:S(2)}) collective-permute-start(f32[2,64,1536]{2,1,0:T(8,128)S(1)} %pad_maximum_fusion.5), channel_id=1, source_target_pairs={{0,8},{8,0},{16,24},{24,16},{1,9},{9,1},{17,25},{25,17},{2,10},{10... | collective-permute-start | bytes 2359304 | tf_op jit(solution)/shard_map/cond/branch_1_fun/ppermute | solution.py:272
  204.6 19.7 %collective-permute-start.20 = (f32[64,512]{1,0:T(8,128)S(1)}, f32[64,512]{1,0:T(8,128)S(1)}, u32[]{:S(2)}, u32[]{:S(2)}) collective-permute-start(f32[64,512]{1,0:T(8,128)S(1)} %add.262), channel_id=1, source_target_pairs={{2,4},{3,5},{4,2},{5,3},{10,12},{11,13},{12,10},{13,11},{18,20},{1... | collective-permute-start | bytes 393224 | tf_op jit(solution)/shard_map/cond/branch_1_fun/ppermute | solution.py:437
  206.6 17.5 %collective-permute-start.19 = (f32[2,64,1536]{2,1,0:T(8,128)S(1)}, f32[2,64,1536]{2,1,0:T(8,128)S(1)}, u32[]{:S(2)}, u32[]{:S(2)}) collective-permute-start(f32[2,64,1536]{2,1,0:T(8,128)S(1)} %pad_maximum_fusion.6), channel_id=1, source_target_pairs={{0,16},{8,24},{16,0},{24,8},{1,17},{9,25},{17,1},{25,9},{2,18},{10... | collective-permute-start | bytes 2359304 | tf_op jit(solution)/shard_map/cond/branch_1_fun/ppermute | solution.py:272
  224.4 3.3 %copy-start.29 = (f32[2,256,256]{2,1,0:T(8,128)S(1)}, f32[2,256,256]{2,1,0:T(8,128)}, u32[]{:S(2)}) copy-start(f32[2,256,256]{2,1,0:T(8,128)} %get-tuple-element.228.factors_ref) | copy-start | bytes 1572868 | tf_op jit(solution)/shard_map/cond
  224.4 14.3 %collective-permute-start.21 = (f32[64,512]{1,0:T(8,128)S(1)}, f32[64,512]{1,0:T(8,128)S(1)}, u32[]{:S(2)}, u32[]{:S(2)}) collective-permute-start(f32[64,512]{1,0:T(8,128)S(1)} %add.263), channel_id=1, source_target_pairs={{2,0},{3,1},{4,6},{5,7},{10,8},{11,9},{12,14},{13,15},{18,16},{19,... | collective-permute-start | bytes 393224 | tf_op jit(solution)/shard_map/cond/branch_1_fun/ppermute | solution.py:437
  238.7 6.0 %collective-permute-start.24 = (f32[64,512]{1,0:T(8,128)S(1)}, f32[64,512]{1,0:T(8,128)S(1)}, u32[]{:S(2)}, u32[]{:S(2)}) collective-permute-start(f32[64,512]{1,0:T(8,128)S(1)} %broadcast_select_fusion.12), channel_id=1, source_target_pairs={{0,24},{8,16},{16,8},{24,0},{1,25},{9,17},{17,9},{25,1},{2,26},{10... | collective-permute-start | bytes 393224 | tf_op jit(solution)/shard_map/cond/branch_1_fun/ppermute | solution.py:272
  239.6 6.4 %collective-permute-start.23 = (f32[64,512]{1,0:T(8,128)S(1)}, f32[64,512]{1,0:T(8,128)S(1)}, u32[]{:S(2)}, u32[]{:S(2)}) collective-permute-start(f32[64,512]{1,0:T(8,128)S(1)} %broadcast_select_fusion.12), channel_id=1, source_target_pairs={{0,16},{8,24},{16,0},{24,8},{1,17},{9,25},{17,1},{25,9},{2,18},{10... | collective-permute-start | bytes 393224 | tf_op jit(solution)/shard_map/cond/branch_1_fun/ppermute | solution.py:272
  241.1 5.0 %collective-permute-start.22 = (f32[64,512]{1,0:T(8,128)S(1)}, f32[64,512]{1,0:T(8,128)S(1)}, u32[]{:S(2)}, u32[]{:S(2)}) collective-permute-start(f32[64,512]{1,0:T(8,128)S(1)} %broadcast_select_fusion.12), channel_id=1, source_target_pairs={{0,8},{8,0},{16,24},{24,16},{1,9},{9,1},{17,25},{25,17},{2,10},{10... | collective-permute-start | bytes 393224 | tf_op jit(solution)/shard_map/cond/branch_1_fun/ppermute | solution.py:272
  247.6 2.3 collective-permute-start.25
  247.6 4.2 %copy-start.24 = (f32[64,512]{1,0:T(8,128)S(1)}, f32[64,512]{1,0:T(8,128)}, u32[]{:S(2)}) copy-start(f32[64,512]{1,0:T(8,128)} %copy-done.23) | copy-start | bytes 393220 | tf_op jit(solution)/shard_map/cond
  (18 other events, 34.3 us)
Sparse Core Ops, SparseCore 0:
  108.6 141.1 all-reduce.2
